TPU v7x, 32 devices: a whole 2x2x4 slice. The times are simulated.
32 devices in a mesh: dp: 8 (over z, core), fsdp: 4 (over y, x).
Axes of the slice: x: 2, y: 2, z: 4, core: 2. Of those that a mesh axis runs over, the one named last changes fastest.
Arguments:
- hidden_in: bfloat16 [256, 2304], P(('dp', 'fsdp')), may hold values from -30 to 30
- cache_pool: bfloat16 [1152, 16, 2, 2048], P('dp', None, None, 'fsdp'), may hold values from -64 to 64
- project_in: bfloat16 [2304, 3, 2048], P('dp', None, 'fsdp'), may hold values from -0.125 to 0.125
- project_out: bfloat16 [2048, 2304], P('fsdp', 'dp'), may hold values from -0.125 to 0.125
- norm_first: bfloat16 [2304], replicated, may hold values from 0.099609375 to 1.8984375
- norm_second: bfloat16 [2304], replicated, may hold values from 0.099609375 to 1.8984375
- router: bfloat16 [2304, 8], replicated, may hold values from -0.125 to 0.125
- gate_up: bfloat16 [8, 2304, 2, 5760], P(None, 'dp', None, 'fsdp'), may hold values from -0.125 to 0.125
- expert_down: bfloat16 [8, 2304, 5760], P(None, 'dp', 'fsdp'), may hold values from -0.078125 to 0.078125
- lengths: int32 [256], replicated, may hold values from 65 to 128, as said below
- prompt_pages: int32 [32, 4], P('dp'), may hold values from 0 to 143, as said below
- own_pages: int32 [256, 4], P('dp'), may hold values from 0 to 143, as said below
- groups: int32 [256], P('dp'), may hold values from 0 to 3
- move_target: int32 [8, 4], replicated, may hold values from 0 to 7, as said below
- routes: int32 [256, 2], P(('dp', 'fsdp')), may hold values from 0 to 7, all different within a row; in each aligned block of 8 rows (0 to 7, 8 to 15, ...) at most 4 rows name the same one
Outputs:
- layer_out: bfloat16 [256, 2304], P(('dp', 'fsdp'))
Inputs may be any that keep to these rules, and one draw needn't show every extreme that they name: `lengths`: every request's cache holds its shared prompt's 4 * 16 positions and at least one more; some request holds 128. `prompt_pages`: within a row, the prompt pages of all its shared prompts and the own pages of all its requests are distinct pages. `own_pages`: within a row, the prompt pages of all its shared prompts and the own pages of all its requests are distinct pages. Row s sends its request slots 32 - 4 + j, j < 4, to rows move_target[s, j]; a row's 4 destinations are distinct and differ from s, and for each j every row is the destination of exactly one row. `routes`: in the 8 rows of one device no expert is named more than 4 times.
All inputs are finite; a program needn't handle non-finite values.
Results may differ from a plain program's by a relative error of at most 0.009.
Values may be sent and summed in bfloat16 or wider, within the bound.
No kernel may reach another device: no remote copies, remote signals or barrier semaphores. Data moves between devices by JAX's collectives and lax.ppermute only.
A program may use at most 128 MiB of HBM per device.

v0:
```python
import jax
import jax.numpy as jnp
from jax import lax
from jax.sharding import PartitionSpec as P

HD = 64
CAP = 4


def rms_scale(values, scaling):
    return (
        values
        * lax.rsqrt(jnp.mean(values * values, axis=-1, keepdims=True) + 1e-06)
        * scaling.astype(jnp.float32)
    )


def rotate(tensor, position):
    half_dim = tensor.shape[-1] // 2
    channel = jnp.arange(half_dim, dtype=jnp.float32)
    inverse = jnp.exp(-jnp.log(10000.0) * 2.0 * channel / tensor.shape[-1])
    angles = position.astype(jnp.float32)[:, None, None] * inverse
    cosine = jnp.cos(angles)
    sine_part = jnp.sin(angles)
    first_half = tensor[..., :half_dim]
    second_half = tensor[..., half_dim:]
    return jnp.concatenate(
        [
            first_half * cosine - second_half * sine_part,
            second_half * cosine + first_half * sine_part,
        ],
        axis=-1,
    )


def local(
    hidden_in,
    cache_pool,
    project_in,
    project_out,
    norm_first,
    norm_second,
    router,
    gate_up,
    expert_down,
    lengths,
    prompt_pages,
    own_pages,
    groups,
    move_target,
    routes,
):
    rows_count = lax.axis_size("dp")
    fsdp_count = lax.axis_size("fsdp")
    my_row = lax.axis_index("dp")
    my_column = lax.axis_index("fsdp")
    req_local = hidden_in.shape[0]
    model_width = hidden_in.shape[1]
    req_row = req_local * fsdp_count
    movers = move_target.shape[1]
    staying = req_row - movers
    page_len = cache_pool.shape[1]
    head_cols = cache_pool.shape[3]
    heads_here = head_cols // HD
    span_total = (prompt_pages.shape[1] + own_pages.shape[1]) * page_len
    expert_count = router.shape[1]
    rows_per_expert = rows_count // expert_count
    slots_row = (CAP + rows_per_expert - 1) // rows_per_expert
    gate_send = jnp.repeat(gate_up, rows_per_expert, axis=0)
    down_send = jnp.repeat(expert_down, rows_per_expert, axis=0)
    row_tokens = lax.all_gather(hidden_in, "fsdp", axis=0, tiled=True)
    group_hit = (
        groups[:, None] == jnp.arange(prompt_pages.shape[0], dtype=jnp.int32)[None, :]
    ).astype(jnp.int32)
    prompt_list = jnp.sum(group_hit[:, :, None] * prompt_pages[None, :, :], axis=1)
    page_list = jnp.concatenate([prompt_list, own_pages], axis=1)
    mover_cache = cache_pool[page_list[staying:]]
    my_targets = move_target[my_row]
    send_select = (my_targets[:, None] == jnp.arange(rows_count, dtype=jnp.int32)[None, :]).astype(
        jnp.bfloat16
    )
    cache_send = jnp.einsum(
        "jd,jpqkc->dpqkc", send_select, mover_cache, preferred_element_type=jnp.float32
    ).astype(jnp.bfloat16)
    tokens_send = jnp.einsum(
        "jd,jc->dc", send_select, row_tokens[staying:], preferred_element_type=jnp.float32
    ).astype(jnp.bfloat16)
    cache_recv, tokens_recv = (
        lax.all_to_all(cache_send, "dp", split_axis=0, concat_axis=0, tiled=True),
        lax.all_to_all(tokens_send, "dp", split_axis=0, concat_axis=0, tiled=True),
    )
    arrive_hit = move_target == my_row
    arrive_select = arrive_hit.astype(jnp.bfloat16)
    arrived_cache = jnp.einsum(
        "sj,spqkc->jpqkc", arrive_select, cache_recv, preferred_element_type=jnp.float32
    ).astype(jnp.bfloat16)
    arrived_tokens = jnp.einsum(
        "sj,sc->jc", arrive_select, tokens_recv, preferred_element_type=jnp.float32
    ).astype(jnp.bfloat16)
    source_row = jnp.sum(
        arrive_hit.astype(jnp.int32) * jnp.arange(rows_count, dtype=jnp.int32)[:, None], axis=0
    )
    row_lengths = lax.dynamic_slice_in_dim(lengths, my_row * req_row, req_row)
    arrived_lengths = lengths[source_row * req_row + staying + jnp.arange(movers, dtype=jnp.int32)]
    position = jnp.concatenate([row_lengths[:staying], arrived_lengths])
    tokens_row = jnp.concatenate([row_tokens[:staying], arrived_tokens], axis=0)
    normed_attn = rms_scale(tokens_row.astype(jnp.float32), norm_first).astype(jnp.bfloat16)
    piece = lax.all_gather(project_in, "dp", axis=0, tiled=True)
    projected = jnp.dot(
        normed_attn,
        piece.reshape(piece.shape[0], 3 * head_cols),
        preferred_element_type=jnp.float32,
    )
    projected = projected.reshape(req_row, 3, heads_here, HD)
    query = rotate(projected[:, 0], position).astype(jnp.bfloat16)
    key_new = rotate(projected[:, 1], position).astype(jnp.bfloat16)
    value_new = projected[:, 2].astype(jnp.bfloat16)
    resident_cache = cache_pool[page_list[:staying]]
    cache_rows = jnp.concatenate([resident_cache, arrived_cache], axis=0).reshape(
        req_row, span_total, 2, heads_here, HD
    )
    key_rows = cache_rows[:, :, 0]
    value_rows = cache_rows[:, :, 1]
    scale_factor = HD ** (-0.5)
    scores = (
        jnp.einsum("nhd,nlhd->nhl", query, key_rows, preferred_element_type=jnp.float32)
        * scale_factor
    )
    valid_mask = jnp.arange(span_total, dtype=jnp.int32)[None, :] < position[:, None]
    scores = jnp.where(valid_mask[:, None, :], scores, -jnp.inf)
    own_score = (
        jnp.sum(query.astype(jnp.float32) * key_new.astype(jnp.float32), axis=-1) * scale_factor
    )
    highest = jnp.maximum(jnp.max(scores, axis=-1), own_score)
    weights_cache = jnp.exp(scores - highest[..., None])
    weight_own = jnp.exp(own_score - highest)
    denominator = jnp.sum(weights_cache, axis=-1) + weight_own
    probs_cache = (weights_cache / denominator[..., None]).astype(jnp.bfloat16)
    prob_own = (weight_own / denominator).astype(jnp.bfloat16)
    mixture = jnp.einsum(
        "nhl,nlhd->nhd", probs_cache, value_rows, preferred_element_type=jnp.float32
    )
    mixture = mixture + prob_own.astype(jnp.float32)[..., None] * value_new.astype(jnp.float32)
    heads_out = mixture.astype(jnp.bfloat16).reshape(req_row, head_cols)
    out_columns = lax.all_gather(project_out, "dp", axis=1, tiled=True)
    attn_proj = lax.psum_scatter(
        jnp.dot(heads_out, out_columns, preferred_element_type=jnp.float32),
        "fsdp",
        scatter_dimension=0,
        tiled=True,
    )
    mine_tokens = lax.dynamic_slice_in_dim(tokens_row, my_column * req_local, req_local, 0)
    resid = mine_tokens.astype(jnp.float32) + attn_proj
    moe_in = rms_scale(resid, norm_second).astype(jnp.bfloat16)
    logits = jnp.dot(moe_in, router, preferred_element_type=jnp.float32)
    expert_ids = jnp.arange(expert_count, dtype=jnp.int32)
    picked = routes[:, :, None] == expert_ids[None, None, :]
    chosen = jnp.sum(jnp.where(picked, logits[:, None, :], 0.0), axis=-1)
    weight_pair = jnp.stack(
        [jax.nn.sigmoid(chosen[:, 0] - chosen[:, 1]), jax.nn.sigmoid(chosen[:, 1] - chosen[:, 0])],
        axis=1,
    )
    mix_expert = jnp.sum(picked.astype(jnp.float32) * weight_pair[:, :, None], axis=1)
    member = jnp.sum(picked.astype(jnp.int32), axis=1)
    rank_expert = jnp.cumsum(member, axis=0) - member
    row_numbers = jnp.arange(rows_count, dtype=jnp.int32)
    expert_of_row = (row_numbers[:, None] // rows_per_expert == expert_ids[None, :]).astype(
        jnp.int32
    )
    replica_of_row = row_numbers % rows_per_expert
    member_row = jnp.sum(member[:, None, :] * expert_of_row[None, :, :], axis=-1)
    rank_row = jnp.sum(rank_expert[:, None, :] * expert_of_row[None, :, :], axis=-1)
    mix_row = jnp.sum(
        mix_expert[:, None, :] * expert_of_row[None, :, :].astype(jnp.float32), axis=-1
    )
    slot_ids = jnp.arange(slots_row, dtype=jnp.int32)
    wanted_rank = slot_ids[None, :, None] * rows_per_expert + replica_of_row[:, None, None]
    select = (member_row.T[:, None, :] == 1) & (rank_row.T[:, None, :] == wanted_rank)
    dispatch = jnp.einsum(
        "dst,tm->dsm", select.astype(jnp.bfloat16), moe_in, preferred_element_type=jnp.float32
    ).astype(jnp.bfloat16)
    received = lax.all_to_all(dispatch, "dp", split_axis=0, concat_axis=0, tiled=True)
    expert_tokens = lax.all_gather(received[None], "fsdp", axis=0, tiled=True)
    gate_whole, down_whole = (
        lax.all_to_all(gate_send, "dp", split_axis=0, concat_axis=1, tiled=True),
        lax.all_to_all(down_send, "dp", split_axis=0, concat_axis=1, tiled=True),
    )
    flattened = expert_tokens.reshape(-1, model_width)
    units_here = gate_up.shape[3]
    gate_cols = gate_whole[0].reshape(model_width, 2 * units_here)
    down_cols = down_whole[0]
    both_parts = jnp.dot(flattened, gate_cols, preferred_element_type=jnp.float32)
    activation = (jax.nn.silu(both_parts[:, :units_here]) * both_parts[:, units_here:]).astype(
        jnp.bfloat16
    )
    returned = lax.psum_scatter(
        lax.dot_general(
            activation, down_cols, (((1,), (1,)), ((), ())), preferred_element_type=jnp.float32
        ).astype(jnp.bfloat16),
        "fsdp",
        scatter_dimension=0,
        tiled=True,
    ).astype(jnp.float32)
    back_rows = lax.all_to_all(
        returned.reshape(rows_count, slots_row, model_width),
        "dp",
        split_axis=0,
        concat_axis=0,
        tiled=True,
    )
    coefficient = select.astype(jnp.float32) * mix_row.T[:, None, :]
    moe_total = jnp.einsum("dst,dsm->tm", coefficient, back_rows, precision=lax.Precision.HIGHEST)
    return (resid + moe_total).astype(jnp.bfloat16)


def solution(mesh):
    placed = (
        P(("dp", "fsdp"), None),
        P("dp", None, None, "fsdp"),
        P("dp", None, "fsdp"),
        P("fsdp", "dp"),
        P(),
        P(),
        P(),
        P(None, "dp", None, "fsdp"),
        P(None, "dp", "fsdp"),
        P(),
        P("dp", None),
        P("dp", None),
        P("dp"),
        P(),
        P(("dp", "fsdp"), None),
    )
    return jax.shard_map(
        local, mesh=mesh, in_specs=placed, out_specs=P(("dp", "fsdp"), None), check_vma=False
    )
```

profile of v0, /device:TPU:0, one launch (start us, length us, event | category | flops | bytes accessed | tf_op | source)
XLA Modules:
  0.0 783.8 jit_solution(9107714346386358718)
XLA Ops:
  8.1 10.2 %all_gather.12 = bf16[32,2304]{1,0:T(8,128)(2,1)S(1)} all-gather(bf16[8,2304]{1,0:T(8,128)(2,1)} %param.15), channel_id=1, replica_groups=mesh['dp'=8,'fsdp'=4] {'fsdp'}, dimensions={0}, use_global_device_ids=true | all-gather | bytes 184320 | tf_op jit(solution)/shard_map/all_gather | solution.py:71
  20.5 4.9 all-to-all-start
  27.8 5.0 gather_fusion.2
  37.7 5.1 all-to-all-start.1
  44.9 21.8 %gather_fusion.1 = bf16[224,16,2,512]{3,2,1,0:T(2,128)(2,1)} fusion(bf16[144,16,2,512]{3,2,1,0:T(2,128)(2,1)} %param.16, s32[1024]{0:T(1024)S(1)} %pad_clamp_fusion.1), kind=kCustom, calls=%fused_computation.1 | custom fusion | bytes 14680960 | tf_op jit(solution)/shard_map/gather | solution.py:118
  66.7 7.9 %copy.122 = bf16[28,8,16,2,512]{4,2,1,3,0:T(8,128)(2,1)} copy(bf16[28,8,16,2,512]{4,3,2,1,0:T(2,128)(2,1)} %bitcast.83) | data formatting | bytes 14680064 | tf_op jit(solution)/shard_map/gather | solution.py:118
  76.5 50.2 %all-to-all-done.1 = bf16[8,8,16,2,512]{4,3,2,1,0:T(2,128)(2,1)S(1)} async-done(((bf16[8,8,16,2,512]{4,3,2,1,0:T(2,128)(2,1)}), bf16[8,8,16,2,512]{4,3,2,1,0:T(2,128)(2,1)S(1)}, u32[]{:S(2)}, u32[]{:S(2)}) %all-to-all-start.1) | async-done | bytes 2097184 | tf_op jit(solution)/shard_map/all_to_all | solution.py:89
  128.4 6.9 pad_maximum_fusion
  135.4 21.2 %reshape.306 = bf16[32,128,2,8,64]{4,3,1,2,0:T(8,128)(2,1)} reshape(bf16[32,8,16,2,512]{4,2,1,3,0:T(8,128)(2,1)} %pad_maximum_fusion) | data formatting | bytes 16777216 | tf_op jit(solution)/shard_map/reshape | solution.py:119
  156.6 11.5 %slice_bitcast_fusion.1 = (bf16[32,128,8,64]{3,2,1,0:T(8,128)(2,1)}, bf16[32,128,8,64]{3,2,1,0:T(8,128)(2,1)}) fusion(bf16[32,128,2,8,64]{4,3,1,2,0:T(8,128)(2,1)} %reshape.306), kind=kLoop, calls=%fused_computation.4 | loop fusion | bytes 16777216 | tf_op jit(solution)/shard_map/squeeze | solution.py:122
  168.1 9.7 %copy.116 = bf16[2304,3,512]{0,2,1:T(8,128)(2,1)} copy(bf16[2304,3,512]{2,0,1:T(8,128)(2,1)} %all-gather.4.cloned.1.call-done) | data formatting | bytes 14155776 | tf_op jit(solution)/shard_map/all_gather | solution.py:108
  177.8 6.5 fusion.21
  190.0 5.7 fusion
  199.5 41.6 %all-reduce.3.cloned.1.call-done = f32[32,2304]{1,0:T(8,128)} async-done(((f32[32,2304]{1,0:T(8,128)}), f32[32,2304]{1,0:T(8,128)}) %all-reduce.3.cloned.1.call-update) | async-done | bytes 294928
  242.5 11.4 %all_to_all.45 = bf16[8,4,2304]{2,1,0:T(4,128)(2,1)S(1)} all-to-all(bf16[8,4,2304]{2,1,0:T(4,128)(2,1)S(1)} %copy.130), channel_id=1, replica_groups=mesh['dp'=8,'fsdp'=4] {'dp'}, dimensions={0} | all-to-all | bytes 294912 | tf_op jit(solution)/shard_map/all_to_all | solution.py:182
  253.9 315.2 %all_to_all.46 = bf16[8,288,2,1440]{3,2,1,0:T(2,128)(2,1)} all-to-all(bf16[8,288,2,1440]{3,2,1,0:T(2,128)(2,1)} %param.22), channel_id=1, replica_groups=mesh['dp'=8,'fsdp'=4] {'dp'}, dimensions={0} | all-to-all | bytes 26542080 | tf_op jit(solution)/shard_map/all_to_all | solution.py:185
  569.1 4.8 all-to-all-start.4
  574.0 10.9 %all-gather = bf16[32,4,2304]{2,1,0:T(4,128)(2,1)S(1)} all-gather(bf16[8,4,2304]{2,1,0:T(4,128)(2,1)S(1)} %all_to_all.45), channel_id=2, replica_groups=mesh['dp'=8,'fsdp'=4] {'fsdp'}, dimensions={0}, use_global_device_ids=true | all-gather | bytes 737280 | tf_op jit(solution)/shard_map/all_gather | solution.py:183
  585.0 31.9 %reshape_squeeze.3 = bf16[2304,2880]{1,0:T(8,128)(2,1)} reshape(bf16[8,288,2,1440]{3,2,1,0:T(2,128)(2,1)} %all_to_all.46) | data formatting | bytes 26542080 | tf_op jit(solution)/shard_map/reshape;squeeze | solution.py:190
  616.9 8.9 %fusion.66 = f32[128,2880]{0,1:T(8,128)S(1)} fusion(bf16[128,2304]{1,0:T(8,128)(2,1)S(1)} %reshape.308, bf16[2304,2880]{1,0:T(8,128)(2,1)} %reshape_squeeze.3), kind=kOutput, calls=%fused_computation.130 | convolution fusion | flops 1698693120 | bytes 15335424 | tf_op jit(solution)/shard_map/dot_general | solution.py:192
  625.8 103.9 %all-to-all-done.4 = bf16[8,288,1440]{2,1,0:T(8,128)(2,1)} async-done(((bf16[8,288,1440]{2,1,0:T(8,128)(2,1)}), bf16[8,288,1440]{2,1,0:T(8,128)(2,1)}, u32[]{:S(2)}, u32[]{:S(2)}) %all-to-all-start.4) | async-done | bytes 6635552 | tf_op jit(solution)/shard_map/all_to_all | solution.py:186
  729.7 6.3 convolution_convert_fusion
  736.4 22.8 %reduce-scatter.2.cloned.1.call-done = bf16[32,2304]{1,0:T(8,128)(2,1)} async-done(((bf16[128,2304]{1,0:T(8,128)(2,1)}), bf16[32,2304]{1,0:T(8,128)(2,1)}) %reduce-scatter.2.cloned.1.call-update) | async-done | bytes 147472 | tf_op jit(solution)/shard_map/reduce_scatter | solution.py:196
  765.7 10.3 %all-to-all-done.5 = f32[8,4,2304]{2,1,0:T(4,128)S(1)} async-done(((f32[8,4,2304]{2,1,0:T(4,128)}), f32[8,4,2304]{2,1,0:T(4,128)S(1)}, u32[]{:S(2)}, u32[]{:S(2)}) %all-to-all-start.5) | async-done | bytes 294944 | tf_op jit(solution)/shard_map/all_to_all | solution.py:204
  (102 shorter events, 35.2 us)
Async XLA Ops:
  6.5 729.5 %copy-start = (bf16[2304,8]{0,1:T(8,128)(2,1)S(1)}, bf16[2304,8]{0,1:T(8,128)(2,1)}, u32[]{:S(2)}) copy-start(bf16[2304,8]{0,1:T(8,128)(2,1)} %param.21) | copy-start | bytes 110596
  6.5 161.6 %all-gather.4.cloned.1.call-start = ((), (), s32[]{:S(2)}) async-start(), calls=%async_computation.7 | async-start | bytes 7962624 | tf_op jit(solution)/shard_map/all_gather | solution.py:108
  19.8 24.0 %copy-start.5 = (bf16[2304]{0:T(1024)(128)(2,1)S(1)}, bf16[2304]{0:T(1024)(128)(2,1)}, u32[]{:S(2)}) copy-start(bf16[2304]{0:T(1024)(128)(2,1)} %param.19) | copy-start | bytes 13828
  19.8 24.0 %copy-start.1 = (s32[256]{0:T(256)S(1)}, s32[256]{0:T(256)}, u32[]{:S(2)}) copy-start(s32[256]{0:T(256)} %param.24) | copy-start | bytes 3076
  19.9 24.1 %copy-start.4 = (s32[8,4]{0,1:T(4,128)S(1)}, s32[8,4]{0,1:T(4,128)}, u32[]{:S(2)}) copy-start(s32[8,4]{0,1:T(4,128)} %param.28) | copy-start | bytes 388
  20.5 17.2 %all-to-all-start = ((bf16[8,2,1152]{2,1,0:T(2,128)(2,1)}), bf16[8,2,1152]{2,1,0:T(2,128)(2,1)S(1)}, u32[]{:S(2)}, u32[]{:S(2)}) async-start(bf16[8,2,1152]{2,1,0:T(2,128)(2,1)} %reshape.355), calls=%async_computation | async-start | bytes 73728 | tf_op jit(solution)/shard_map/all_to_all | solution.py:90
  37.7 89.0 %all-to-all-start.1 = ((bf16[8,8,16,2,512]{4,3,2,1,0:T(2,128)(2,1)}), bf16[8,8,16,2,512]{4,3,2,1,0:T(2,128)(2,1)S(1)}, u32[]{:S(2)}, u32[]{:S(2)}) async-start(bf16[8,8,16,2,512]{4,3,2,1,0:T(2,128)(2,1)} %copy.120), calls=%async_computation.1 | async-start | bytes 4194304 | tf_op jit(solution)/shard_map/all_to_all | solution.py:89
  42.8 153.1 %all-gather.6.cloned.1.call-start = ((), (), s32[]{:S(2)}) async-start(), calls=%async_computation.8 | async-start | bytes 2654208 | tf_op jit(solution)/shard_map/all_gather | solution.py:145
  43.6 197.6 %all-reduce.3.cloned.1.call-start = ((), (), s32[]{:S(2)}) async-start(), calls=%async_computation.10 | async-start | bytes 589824
  66.7 7.9 %copy-start.6 = (bf16[2304]{0:T(1024)(128)(2,1)S(1)}, bf16[2304]{0:T(1024)(128)(2,1)}, u32[]{:S(2)}) copy-start(bf16[2304]{0:T(1024)(128)(2,1)} %param.20) | copy-start | bytes 13828
  66.7 7.9 %copy-start.3 = (s32[8,2]{0,1:T(2,128)S(1)}, s32[8,2]{0,1:T(2,128)}, u32[]{:S(2)}) copy-start(s32[8,2]{0,1:T(2,128)} %param.29) | copy-start | bytes 196
  66.7 8.0 %copy-start.7 = (u32[32]{0:T(128)S(1)}, u32[32]{0:T(128)}, u32[]{:S(2)}) copy-start(u32[32]{0:T(128)} %constant.87) | copy-start | bytes 388
  177.8 6.8 copy-start.2
  569.1 160.6 %all-to-all-start.4 = ((bf16[8,288,1440]{2,1,0:T(8,128)(2,1)}), bf16[8,288,1440]{2,1,0:T(8,128)(2,1)}, u32[]{:S(2)}, u32[]{:S(2)}) async-start(bf16[8,288,1440]{2,1,0:T(8,128)(2,1)} %param.23), calls=%async_computation.4 | async-start | bytes 14155776 | tf_op jit(solution)/shard_map/all_to_all | solution.py:186
  573.9 185.3 %reduce-scatter.2.cloned.1.call-start = ((), (), s32[]{:S(2)}) async-start(), calls=%async_computation.9 | async-start | bytes 737280 | tf_op jit(solution)/shard_map/reduce_scatter | solution.py:196
  760.9 15.0 %all-to-all-start.5 = ((f32[8,4,2304]{2,1,0:T(4,128)}), f32[8,4,2304]{2,1,0:T(4,128)S(1)}, u32[]{:S(2)}, u32[]{:S(2)}) async-start(f32[8,4,2304]{2,1,0:T(4,128)} %reshape.313), calls=%async_computation.6 | async-start | bytes 589824 | tf_op jit(solution)/shard_map/all_to_all | solution.py:204
Sparse Core Ops, SparseCore 0:
  9.0 115.1 all-gather.3
  125.8 30.4 all-gather.5
  199.3 41.8 all-reduce.2
  736.2 23.0 reduce-scatter.1
where the time goes:
time: 786 us; the launch traced here: 784 us
  blocking collectives  348 us (44%)
  waiting for transfers between devices  230 us (29%)
  local copies, waits for them, and re-layouts  119 us (15%)
  matrix products  39.8 us (5%)
  starting transfers between devices  19.7 us (3%)
  between operations  14.1 us (2%)
  other arithmetic  13.3 us (2%)
    all_to_all x1, blocking collectives, local(): lax.all_to_all(gate_send, 'dp', split_axis=0, concat_axis=1, tiled=True)  315 us
    all_to_all x1, waiting for transfers between devices, local(): lax.all_to_all(down_send, 'dp', split_axis=0, concat_axis=1, tiled=True)  104 us
    all_to_all x1, waiting for transfers between devices, local(): lax.all_to_all(cache_send, 'dp', split_axis=0, concat_axis=0, tiled=True)  50.2 us
    unnamed x5, waiting for transfers between devices  43.1 us
    another operation x1, local copies, waits for them, and re-layouts, local(): gate_cols = gate_whole[0].reshape(model_width, 2 * units_here)  31.9 us
    gather x2, local copies, waits for them, and re-layouts, local(): resident_cache = cache_pool[page_list[:staying]]  29.6 us
    reduce_scatter x1, waiting for transfers between devices, local(): lax.psum_scatter(lax.dot_general(activation, down_cols, (((1,), (1,)), ((...  22.8 us
    reshape x1, local copies, waits for them, and re-layouts, local(): jnp.concatenate([resident_cache, arrived_cache], axis=0)  21.2 us
  transfers between devices with their start and end apart: 8, of which 5 were waited for; matrix products, arithmetic and copies ran while one was open for 20% of the time, Pallas kernels for 0%

commit v1 on v0

v1 whole, which is shorter than its diff:
```python
import functools

import jax
import jax.numpy as jnp
from jax import lax
from jax.experimental import pallas as pl
from jax.experimental.pallas import tpu as pltpu
from jax.sharding import PartitionSpec as P

HD = 64
CAP = 4
PIECES = 3
LANES = 128
BF16 = jnp.bfloat16
F32 = jnp.float32
FAR = -3.0e38


def params(mib=40):
    return pltpu.CompilerParams(vmem_limit_bytes=mib * 2**20)


def dot_nn(a, b):
    return lax.dot_general(a, b, (((1,), (0,)), ((), ())), preferred_element_type=F32)


def dot_nt(a, b):
    return lax.dot_general(a, b, (((1,), (1,)), ((), ())), preferred_element_type=F32)


def split_bf16(value, count=PIECES):
    pieces = []
    for _ in range(count):
        piece = value.astype(BF16).astype(F32)
        pieces.append(piece)
        value = value - piece
    return pieces


def full_spec(shape):
    zeros = (0,) * len(shape)
    return pl.BlockSpec(tuple(shape), lambda *_: zeros)


def pool_kernel(pool_ref, key_ref, value_ref):
    pages, page_len, _, cols = pool_ref.shape
    rows = pages * page_len
    both = pool_ref[...].reshape(2 * rows, cols)
    wide = lax.broadcasted_iota(jnp.int32, (rows, 2 * rows), 1)
    high = lax.broadcasted_iota(jnp.int32, (rows, 2 * rows), 0)
    key_ref[...] = dot_nn((wide == 2 * high).astype(BF16), both).astype(BF16)
    value_ref[...] = dot_nn((wide == 2 * high + 1).astype(BF16), both).astype(BF16)


def split_pool(cache_pool):
    pages, page_len, _, cols = cache_pool.shape
    block = next(b for b in (16, 8, 4, 2, 1) if pages % b == 0)
    out = jax.ShapeDtypeStruct((pages * page_len, cols), BF16)
    spec = pl.BlockSpec((block * page_len, cols), lambda b: (b, 0))
    return pl.pallas_call(
        pool_kernel,
        grid=(pages // block,),
        in_specs=[pl.BlockSpec((block, page_len, 2, cols), lambda b: (b, 0, 0, 0))],
        out_specs=[spec, spec],
        out_shape=[out, out],
        compiler_params=params(),
        cost_estimate=pl.CostEstimate(
            flops=8 * block * page_len * cache_pool.size,
            bytes_accessed=4 * cache_pool.size,
            transcendentals=0,
        ),
        name="pool_split",
    )(cache_pool)


def qkv_kernel(order_ref, recv_ref, norm_ref, w_ref, keep_ref, send_ref, raw_ref, normed, slots):
    width = norm_ref.shape[1]
    half, row, _ = keep_ref.shape
    cols = w_ref.shape[2]
    values = recv_ref[:, :width]
    scale = recv_ref[:, width : width + 1].astype(F32)
    for piece in range(1, PIECES):
        scale = scale + recv_ref[:, width + piece : width + piece + 1].astype(F32)
    normed[...] = (values.astype(F32) * scale * norm_ref[...]).astype(BF16)
    for slot in range(2 * half):
        rows = pl.ds(pl.multiple_of(order_ref[slot] * row, row), row)
        slots[slot * row : (slot + 1) * row] = normed[rows]
        raw_ref[slot * row : (slot + 1) * row] = recv_ref[rows, :width]
    for part in range(3):
        here = slice(part * cols, (part + 1) * cols)
        result = dot_nn(slots[...], w_ref[part]).astype(BF16).reshape(2 * half, row, cols)
        keep_ref[:, :, here] = result[:half]
        send_ref[:, :, here] = result[half:]


def project_qkv(order, recv, norm_slice, weights, half, row):
    total, _ = recv.shape
    width, cols = weights.shape[1:]
    out = jax.ShapeDtypeStruct((half, row, 3 * cols), BF16)
    raw = jax.ShapeDtypeStruct((total, width), BF16)
    return pl.pallas_call(
        qkv_kernel,
        grid_spec=pltpu.PrefetchScalarGridSpec(
            num_scalar_prefetch=1,
            grid=(1,),
            in_specs=[full_spec(recv.shape), full_spec(norm_slice.shape), full_spec(weights.shape)],
            out_specs=[full_spec(out.shape), full_spec(out.shape), full_spec(raw.shape)],
            scratch_shapes=[pltpu.VMEM((total, width), BF16), pltpu.VMEM((total, width), BF16)],
        ),
        out_shape=[out, out, raw],
        compiler_params=params(),
        cost_estimate=pl.CostEstimate(
            flops=6 * total * width * cols, bytes_accessed=6 * total * cols + 6 * width * cols, transcendentals=0
        ),
        name="qkv",
    )(order, recv, norm_slice, weights)


def attention_kernel(*refs):
    parts, (cos_ref, sin_ref, bias_ref, key_ref, value_ref, out_ref, scores, probs) = refs[:-8], refs[-8:]
    row, cols = out_ref.shape
    heads = cols // HD
    total = parts[0][...].astype(F32)
    for part in parts[1:]:
        total = total + part[...].astype(F32)
    lane = lax.broadcasted_iota(jnp.int32, (row, cols), 1)
    first_half = lane % HD < HD // 2

    def rotate(values):
        partner = jnp.where(
            first_half, pltpu.roll(values, cols - HD // 2, 1), pltpu.roll(values, HD // 2, 1)
        )
        return (values * cos_ref[...] + partner * sin_ref[...]).astype(BF16)

    query = rotate(total[:, :cols]).astype(F32)
    key_new = rotate(total[:, cols : 2 * cols]).astype(F32)
    value_new = total[:, 2 * cols :].astype(BF16).astype(F32)
    spread = jnp.concatenate(
        [jnp.where(lane // HD == h, query, 0.0).astype(BF16) for h in range(heads)], axis=0
    )
    scores[...] = dot_nt(spread, key_ref[...])
    own_parts = []
    for h in range(heads):
        here = slice(h * row, (h + 1) * row)
        mine = lane // HD == h
        own = jnp.sum(jnp.where(mine, query * key_new, 0.0), axis=1, keepdims=True) * HD**-0.5
        score = scores[here] * HD**-0.5 + bias_ref[...]
        highest = jnp.maximum(jnp.max(score, axis=1, keepdims=True), own)
        weight = jnp.exp(score - highest)
        weight_own = jnp.exp(own - highest)
        inverse = 1.0 / (jnp.sum(weight, axis=1, keepdims=True) + weight_own)
        probs[here] = (weight * inverse).astype(BF16)
        own_parts.append((weight_own * inverse).astype(BF16).astype(F32))
    mixture = dot_nn(probs[...], value_ref[...])
    result = jnp.zeros((row, cols), F32)
    for h in range(heads):
        mixed = mixture[h * row : (h + 1) * row] + own_parts[h] * value_new
        result = jnp.where(lane // HD == h, mixed, result)
    out_ref[...] = result.astype(BF16)


def attend(parts, cosine, sine, bias, keys, values):
    row, cols = cosine.shape
    stretch = keys.shape[0]
    heads = cols // HD
    operands = [*parts, cosine, sine, bias, keys, values]
    return pl.pallas_call(
        attention_kernel,
        grid=(1,),
        in_specs=[full_spec(x.shape) for x in operands],
        out_specs=full_spec((row, cols)),
        out_shape=jax.ShapeDtypeStruct((row, cols), BF16),
        scratch_shapes=[
            pltpu.VMEM((heads * row, stretch), F32),
            pltpu.VMEM((heads * row, stretch), BF16),
        ],
        compiler_params=params(),
        cost_estimate=pl.CostEstimate(
            flops=4 * heads * row * stretch * cols,
            bytes_accessed=4 * stretch * cols,
            transcendentals=heads * row * stretch,
        ),
        name="attention",
    )(*operands)


def out_kernel(*refs):
    parts, (other_ref, w_ref, out_ref) = refs[:-3], refs[-3:]
    half = len(parts) * parts[0].shape[0]
    mine = jnp.concatenate([part[...] for part in parts], axis=0)
    out_ref[:, :half] = dot_nt(w_ref[...], mine).astype(BF16)
    out_ref[:, half:] = dot_nt(w_ref[...], other_ref[...]).astype(BF16)


def project_heads(parts, other, weights):
    half = other.shape[0]
    operands = [*parts, other, weights]
    out = (weights.shape[0], 2 * half)
    return pl.pallas_call(
        out_kernel,
        grid=(1,),
        in_specs=[full_spec(x.shape) for x in operands],
        out_specs=full_spec(out),
        out_shape=jax.ShapeDtypeStruct(out, BF16),
        compiler_params=params(),
        cost_estimate=pl.CostEstimate(
            flops=2 * weights.size * out[1], bytes_accessed=4 * weights.size, transcendentals=0
        ),
        name="out_projection",
    )(*operands)


def pair_block(pairs):
    return next(b for b in (256, 128, 64, 32, 16) if pairs % b == 0)


def dispatch(parts, hid_ref, norm_ref, router_ref, pos_ref, route_ref, resid_ref, spread_ref, aux_ref, aux_at):
    width, total = hid_ref.shape
    pairs = spread_ref.shape[1]
    resid = hid_ref[...].astype(F32)
    for part in parts:
        resid = resid + part[...].astype(F32)
    resid_ref[...] = resid
    moe = (resid * norm_ref[...]).astype(BF16)
    squares = jnp.sum(resid * resid, axis=0, keepdims=True)
    logits = dot_nn(router_ref[...], moe)
    expert = lax.broadcasted_iota(jnp.int32, logits.shape, 0)
    sign = (expert == route_ref[0:1]).astype(F32) - (expert == route_ref[1:2]).astype(F32)
    gap = jnp.sum(logits * sign, axis=0, keepdims=True)
    high = lax.broadcasted_iota(jnp.int32, (LANES, total), 0)
    aux_plain = jnp.zeros((LANES, total), F32)
    aux_signed = jnp.zeros((LANES, total), F32)
    for k, piece in enumerate(split_bf16(squares)):
        aux_plain = jnp.where(high == aux_at + k, piece, aux_plain)
    for k, piece in enumerate(split_bf16(gap)):
        aux_signed = jnp.where(high == aux_at + PIECES + k, piece, aux_signed)
    aux_plain = aux_plain.astype(BF16)
    aux_signed = aux_signed.astype(BF16)
    feature = lax.broadcasted_iota(jnp.int32, (width, 2 * width), 0)
    lane = lax.broadcasted_iota(jnp.int32, (width, 2 * width), 1)
    even = (lane == 2 * feature).astype(BF16)
    odd = (lane == 2 * feature + 1).astype(BF16)
    block = pair_block(pairs)
    for start in range(0, pairs, block):
        here = slice(start, start + block)
        pair = lax.broadcasted_iota(jnp.int32, (block, total), 0) + start
        first = (pair == pos_ref[0:1]).astype(F32)
        second = (pair == pos_ref[1:2]).astype(F32)
        both = (first + second).astype(BF16)
        rows = dot_nt(both, moe).astype(BF16)
        spread_ref[0, here] = dot_nn(rows, even).astype(BF16)
        spread_ref[1, here] = dot_nn(rows, odd).astype(BF16)
        aux_ref[here] = dot_nt(both, aux_plain) + dot_nt((first - second).astype(BF16), aux_signed)


def windows(pairs, per_expert):
    return min(per_expert + 16, pairs)


def window_of(offset_ref, expert, pairs, window):
    first = offset_ref[expert]
    start = pl.multiple_of(jnp.minimum(first // 16 * 16, pairs - window), 16)
    rows = lax.broadcasted_iota(jnp.int32, (window, 1), 0) + start
    return pl.ds(start, window), (rows >= first) & (rows < offset_ref[expert + 1])


def gate_kernel(count_parts, columns, tail, window, offset_ref, order_ref, *refs):
    first = count_parts > 0
    if first:
        parts, refs = refs[:count_parts], refs[count_parts:]
        hid_ref, norm_ref, router_ref, pos_ref, route_ref, w_ref, tail_ref = refs[:7]
        keep_ref, send_ref, resid_ref, spread_ref, held, aux = refs[7:]
    else:
        spread_ref, w_ref, keep_ref, send_ref, held = refs
    expert = pl.program_id(0)
    pairs = spread_ref.shape[1]
    width = spread_ref.shape[2] // 2

    if first:
        tail_width, _, aux_at, size = tail

        @pl.when(expert == 0)
        def _():
            dispatch(
                parts, hid_ref, norm_ref, router_ref, pos_ref, route_ref, resid_ref, spread_ref, aux, aux_at % LANES
            )

    rows, valid = window_of(offset_ref, expert, pairs, window)
    left = jnp.concatenate([spread_ref[0, rows], spread_ref[1, rows]], axis=0)
    weights = w_ref[0].reshape(2 * width, w_ref.shape[3])[:, :columns]
    result = dot_nn(left, weights).astype(BF16)
    held[rows, :columns] = jnp.where(valid, result[:window], held[rows, :columns])
    held[rows, columns : 2 * columns] = jnp.where(
        valid, result[window:], held[rows, columns : 2 * columns]
    )
    if first:
        weights = tail_ref[0].reshape(2 * width, LANES)
        result = dot_nn(left, weights)
        lane = lax.broadcasted_iota(jnp.int32, (window, LANES), 1)
        gate, up = result[:window], result[window:]
        if tail_width == LANES:
            block = jnp.where(lane < size, gate, pltpu.roll(up, size, 1))
            block = jnp.where(lane < 2 * size, block, aux[rows])
        else:
            block = jnp.concatenate(
                [jnp.where(lane < size, gate, 0.0), jnp.where(lane < size, up, 0.0), aux[rows]], axis=1
            )
        here = slice(2 * columns, 2 * columns + tail_width)
        held[rows, here] = jnp.where(valid, block.astype(BF16), held[rows, here])

    @pl.when(expert == pl.num_programs(0) - 1)
    def _():
        half, block, _ = keep_ref.shape
        for slot in range(half):
            mine = pl.ds(pl.multiple_of(order_ref[slot] * block, block), block)
            other = pl.ds(pl.multiple_of(order_ref[half + slot] * block, block), block)
            keep_ref[slot] = held[mine]
            send_ref[slot] = held[other]


def tail_layout(units):
    size = units % LANES
    if 2 * size + 2 * PIECES <= LANES:
        return LANES, size, 2 * size, size
    return 3 * LANES, LANES, 2 * LANES, size


def core_kernel(aux_at, keep_ref, recv_ref, *outs):
    half, block, width = keep_ref.shape
    for slot in range(half):
        total = keep_ref[slot].astype(F32) + recv_ref[slot].astype(F32)
        if aux_at is None:
            outs[slot][...] = total.astype(BF16)
            continue
        base = aux_at // LANES * LANES
        if base:
            outs[slot][:, :base] = total[:, :base].astype(BF16)
        tile = total[:, base : base + LANES]
        lane = lax.broadcasted_iota(jnp.int32, tile.shape, 1)
        at = aux_at - base
        for start in (at, at + PIECES):
            value = tile[:, start : start + 1]
            for k in range(1, PIECES):
                value = value + tile[:, start + k : start + k + 1]
            for k, piece in enumerate(split_bf16(value)):
                tile = jnp.where(lane == start + k, piece, tile)
        outs[slot][:, base : base + LANES] = tile.astype(BF16)
        if base + LANES < width:
            outs[slot][:, base + LANES :] = total[:, base + LANES :].astype(BF16)


def core_sum(keep, recv, aux_at, name):
    half, block, width = keep.shape
    out = jax.ShapeDtypeStruct((block, width), BF16)
    return pl.pallas_call(
        functools.partial(core_kernel, aux_at),
        grid=(1,),
        in_specs=[full_spec(keep.shape)] * 2,
        out_specs=[full_spec(out.shape)] * half,
        out_shape=[out] * half,
        compiler_params=params(),
        cost_estimate=pl.CostEstimate(flops=keep.size, bytes_accessed=6 * keep.size, transcendentals=0),
        name=name,
    )(keep, recv)


def act_kernel(count_parts, columns, tail, features, *refs):
    parts, refs = refs[:count_parts], refs[count_parts:]
    total = parts[0][...].astype(F32)
    for part in parts[1:]:
        total = total + part[...].astype(F32)
    if tail is None:
        stat_ref, act_ref = refs
        inverse, weight = stat_ref[:, 0:1], stat_ref[:, 1:2]
    else:
        act_ref, stat_ref = refs
        tail_width, up_at, aux_at, size = tail
        base = 2 * columns + aux_at
        squares = total[:, base : base + 1]
        gap = total[:, base + PIECES : base + PIECES + 1]
        for k in range(1, PIECES):
            squares = squares + total[:, base + k : base + k + 1]
            gap = gap + total[:, base + PIECES + k : base + PIECES + k + 1]
        inverse = lax.rsqrt(squares / features + 1e-06)
        weight = 1.0 / (1.0 + jnp.exp(-gap * inverse))
        lane = lax.broadcasted_iota(jnp.int32, (total.shape[0], LANES), 1)
        stat_ref[...] = jnp.where(lane == 0, inverse, weight)

    def activate(gate, up):
        gate = gate * inverse
        return gate / (1.0 + jnp.exp(-gate)) * (up * inverse) * weight

    act_ref[:, :columns] = activate(total[:, :columns], total[:, columns : 2 * columns]).astype(BF16)
    if tail is not None:
        block = total[:, 2 * columns : 2 * columns + LANES]
        if tail_width == LANES:
            up = pltpu.roll(block, LANES - size, 1)
        else:
            up = total[:, 2 * columns + LANES : 2 * columns + 2 * LANES]
        last = jnp.where(lane < size, activate(block, up), 0.0)
        act_ref[:, columns:] = last.astype(BF16)


def activation(parts, stats, columns, tail, features, name):
    rows = parts[0].shape[0]
    out = jax.ShapeDtypeStruct((rows, columns + (LANES if tail else 0)), BF16)
    stat = jax.ShapeDtypeStruct((rows, LANES), F32)
    operands = [*parts] + ([] if tail else [stats])
    outs = [out, stat] if tail else [out]
    result = pl.pallas_call(
        functools.partial(act_kernel, len(parts), columns, tail, features),
        grid=(1,),
        in_specs=[full_spec(x.shape) for x in operands],
        out_specs=[full_spec(x.shape) for x in outs],
        out_shape=outs,
        compiler_params=params(),
        cost_estimate=pl.CostEstimate(
            flops=16 * rows * columns, bytes_accessed=20 * rows * columns, transcendentals=rows * columns
        ),
        name=name,
    )(*operands)
    return (result[0], result[1]) if tail else (result[0], stats)


def down_kernel(count_parts, columns, tail, window, begins, ends, requests, offset_ref, order_ref, *refs):
    parts, refs = refs[:count_parts], refs[count_parts:]
    other_ref, w_ref, refs = refs[0], refs[1], refs[2:]
    if tail:
        tail_ref, refs = refs[0], refs[1:]
    if not begins:
        before_ref, refs = refs[0], refs[1:]
    if ends:
        place_ref, resid_ref, out_ref, total_ref, held = refs
    else:
        total_ref, held = refs
    expert = pl.program_id(0)
    block = parts[0].shape[0]
    half = len(parts)
    pairs = held.shape[0]

    @pl.when(expert == 0)
    def _():
        for slot in range(half):
            mine = pl.ds(pl.multiple_of(order_ref[slot] * block, block), block)
            other = pl.ds(pl.multiple_of(order_ref[half + slot] * block, block), block)
            held[mine] = parts[slot][...]
            held[other] = other_ref[slot]
        total_ref[...] = jnp.zeros_like(total_ref) if begins else before_ref[...]

    rows, valid = window_of(offset_ref, expert, pairs, window)
    result = dot_nt(held[rows, :columns], w_ref[0][:, :columns])
    if tail:
        size = tail[3]
        result = result + dot_nt(held[rows, columns : columns + size], tail_ref[0][:, :size])
    total_ref[rows] = total_ref[rows] + jnp.where(valid, result, 0.0)

    if ends:

        @pl.when(expert == pl.num_programs(0) - 1)
        def _():
            total = out_ref.shape[0]
            pieces = [x.astype(BF16) for x in split_bf16(total_ref[...], 2)]
            resid = [x.astype(BF16) for x in split_bf16(resid_ref[...], 2)]
            step = pair_block(total) if total > 256 else total
            step = min(step, 256)
            for start in range(0, total, step):
                here = slice(start, start + step)
                pair = lax.broadcasted_iota(jnp.int32, (step, pairs), 1)
                pick = (pair == place_ref[here, 0:1]) | (pair == place_ref[here, 1:2])
                pick = pick.astype(F32).astype(BF16)
                token = lax.broadcasted_iota(jnp.int32, (step, total), 1)
                move = (token == place_ref[here, 2:3]).astype(F32).astype(BF16)
                result = dot_nn(pick, pieces[0]) + dot_nn(pick, pieces[1])
                result = result + dot_nt(move, resid[0]) + dot_nt(move, resid[1])
                out_ref[here] = result.astype(BF16)


def largest_tile(full):
    return LANES * min(4, full)


def local(
    hidden_in,
    cache_pool,
    project_in,
    project_out,
    norm_first,
    norm_second,
    router,
    gate_up,
    expert_down,
    lengths,
    prompt_pages,
    own_pages,
    groups,
    move_target,
    routes,
):
    dp = lax.axis_size("dp")
    fs = lax.axis_size("fsdp")
    half = dp // 2
    my_row = lax.axis_index("dp")
    my_column = lax.axis_index("fsdp")
    my_chip, my_core = my_row // 2, my_row % 2
    req, features = hidden_in.shape
    row = req * fs
    total = row * dp
    pairs = 2 * total
    width = project_in.shape[0]
    cols = cache_pool.shape[3]
    heads = cols // HD
    page_len = cache_pool.shape[1]
    movers = move_target.shape[1]
    staying = row - movers
    experts = router.shape[1]
    units = gate_up.shape[3]
    window = windows(pairs, CAP * dp * fs)

    chip = jnp.arange(half, dtype=jnp.int32)
    order = jnp.concatenate([(chip ^ my_chip) * 2 + my_core, (chip ^ my_chip) * 2 + 1 - my_core])

    def swap(x):
        return lax.ppermute(x, "dp", [(i, i ^ 1) for i in range(dp)])

    def over_chips(x, s):
        return lax.ppermute(x, "dp", [(i, i ^ (2 * s)) for i in range(dp)])

    def over_columns(x, s):
        return lax.ppermute(x, "fsdp", [(i, i ^ s) for i in range(fs)])

    wide = hidden_in.astype(F32)
    factor = lax.rsqrt(jnp.mean(wide * wide, axis=1, keepdims=True) + 1e-06)
    extra = []
    for _ in range(PIECES):
        piece = lax.reduce_precision(factor, 8, 7)
        extra.append(piece.astype(BF16))
        factor = factor - piece
    extra = jnp.concatenate([*extra, routes.astype(BF16)], axis=1)
    sliced = hidden_in.reshape(req, dp, width).transpose(1, 0, 2)
    room = -(width + extra.shape[1]) % LANES
    sliced = jnp.concatenate(
        [
            sliced,
            jnp.broadcast_to(extra[None], (dp, *extra.shape)),
            jnp.zeros((dp, req, room), BF16),
        ],
        axis=2,
    )
    payload = jnp.broadcast_to(sliced[:, None], (dp, fs, *sliced.shape[1:]))
    payload = payload.reshape(dp * fs, req, sliced.shape[2])
    recv = lax.all_to_all(payload, ("dp", "fsdp"), 0, 0, tiled=True).reshape(total, sliced.shape[2])

    keys, values = split_pool(cache_pool)
    group_hit = groups[:, None] == jnp.arange(prompt_pages.shape[0], dtype=jnp.int32)[None, :]
    prompt_list = jnp.sum(jnp.where(group_hit[:, :, None], prompt_pages[None], 0), axis=1)
    page_list = jnp.concatenate([prompt_list, own_pages], axis=1)
    row_lengths = lax.dynamic_slice_in_dim(lengths, my_row * row, row)
    spot = jnp.arange(cache_pool.shape[0] * page_len, dtype=jnp.int32)
    listed = page_list[:, :, None] == (spot // page_len)[None, None, :]
    left = row_lengths[:, None] - page_len * jnp.arange(page_list.shape[1], dtype=jnp.int32)[None, :]
    reach = jnp.sum(jnp.where(listed, left[:, :, None], 0), axis=1)
    bias = jnp.where((spot % page_len)[None, :] < reach, 0.0, FAR).astype(F32)
    lane = jnp.arange(cols, dtype=jnp.int32)
    channel = (lane % (HD // 2)).astype(F32)
    inverse = jnp.exp(-jnp.log(10000.0) * 2.0 * channel / HD)
    angles = row_lengths.astype(F32)[:, None] * inverse[None, :]
    cosine = jnp.cos(angles)
    sine = jnp.where((lane % HD < HD // 2)[None, :], -1.0, 1.0) * jnp.sin(angles)

    def slice_of(vector):
        return lax.dynamic_slice_in_dim(vector, my_row * width, width)

    keep, send, raw = project_qkv(
        order,
        recv,
        slice_of(norm_first).astype(F32)[None, :],
        project_in.transpose(1, 0, 2),
        half,
        row,
    )
    other = swap(send)
    sums = [(keep[s].astype(F32) + other[s].astype(F32)).astype(BF16) for s in range(half)]
    parts = [sums[0]] + [over_chips(sums[s], s) for s in range(1, half)]
    heads_out = attend(parts, cosine, sine, bias, keys, values)

    parts = [heads_out] + [over_chips(heads_out, s) for s in range(1, half)]
    other = swap(jnp.concatenate(parts, axis=0))
    projected = project_heads(parts, other, project_out.T)
    parts = [projected] + [over_columns(projected, s) for s in range(1, fs)]

    routes_all = recv[:, width + PIECES : width + PIECES + 2].astype(jnp.int32)
    expert_ids = jnp.arange(experts, dtype=jnp.int32)
    picked = (routes_all[:, :, None] == expert_ids[None, None, :]).astype(jnp.int32)
    member = picked[:, 0] + picked[:, 1]
    upto = jnp.cumsum(member, axis=0)
    counts = upto[-1]
    ends = jnp.cumsum(counts)
    offsets = jnp.concatenate([jnp.zeros((1,), jnp.int32), ends]).astype(jnp.int32)
    places = (upto - member) + offsets[None, :experts]
    place = jnp.sum(picked * places[:, None, :], axis=2)

    row_ids = jnp.arange(dp, dtype=jnp.int32)
    table = jnp.concatenate([place, routes_all], axis=1).reshape(dp, row, 4)
    to_row = (move_target[:, :, None] == row_ids[None, None, :]).astype(jnp.int32)
    moved = jnp.sum(to_row[:, :, :, None] * table[:, staying:].transpose(1, 0, 2)[None], axis=2)
    by_source = jnp.concatenate([table[:, :staying], moved], axis=1)
    here = (order[:, None] == row_ids[None, :]).astype(jnp.int32)
    by_slot = jnp.sum(here[:, :, None, None] * by_source[None], axis=1).reshape(total, 4).T
    slot_of_row = jnp.sum(here * row_ids[:, None], axis=0)
    source_slot = jnp.sum(to_row * slot_of_row[:, None, None], axis=0).T
    slot_of = jnp.concatenate([jnp.broadcast_to(slot_of_row[:, None], (dp, staying)), source_slot], axis=1)
    token = jnp.arange(total, dtype=jnp.int32)
    lies_at = slot_of.reshape(total) * row + token % row
    lies_at = jnp.where(token // req % fs == my_column, lies_at, -1)
    place_table = jnp.concatenate([place, lies_at[:, None]], axis=1)

    full = units // LANES
    step = largest_tile(full)
    chunks = [(k, min(step, full * LANES - k * step)) for k in range(-(-full * LANES // step))]
    tail = tail_layout(units)
    tail_block = units // LANES
    block = pairs // dp
    spread = jax.ShapeDtypeStruct((2, pairs, 2 * width), BF16)
    resid_shape = jax.ShapeDtypeStruct((width, total), F32)
    norm_column = slice_of(norm_second).astype(F32)[:, None]
    router_slice = lax.dynamic_slice_in_dim(router, my_row * width, width).T
    acts, stats = [], None
    pos_slot, route_slot = by_slot[:2], by_slot[2:]
    reduced = []
    for index, (number, columns) in enumerate(chunks):
        first = index == 0
        out_width = 2 * columns + (tail[0] if first else 0)
        half_out = jax.ShapeDtypeStruct((half, block, out_width), BF16)
        weight_spec = pl.BlockSpec((1, width, 2, step), lambda e, *_, k=number: (e, 0, 0, k))
        if first:
            operands = [*parts, raw.T, norm_column, router_slice, pos_slot, route_slot]
            in_specs = [full_spec(x.shape) for x in operands] + [
                weight_spec,
                pl.BlockSpec((1, width, 2, LANES), lambda e, *_: (e, 0, 0, tail_block)),
            ]
            operands += [gate_up, gate_up]
            outs = [half_out, half_out, resid_shape, spread]
            scratch = [pltpu.VMEM((pairs, out_width), BF16), pltpu.VMEM((pairs, LANES), F32)]
        else:
            operands = [spread_value, gate_up]
            in_specs = [full_spec(spread.shape), weight_spec]
            outs = [half_out, half_out]
            scratch = [pltpu.VMEM((pairs, out_width), BF16)]
        result = pl.pallas_call(
            functools.partial(gate_kernel, len(parts) if first else 0, columns, tail, window),
            grid_spec=pltpu.PrefetchScalarGridSpec(
                num_scalar_prefetch=2,
                grid=(experts,),
                in_specs=in_specs,
                out_specs=[full_spec(x.shape) for x in outs],
                scratch_shapes=scratch,
            ),
            out_shape=outs,
            compiler_params=params(40 if pairs <= 1024 else 60),
            cost_estimate=pl.CostEstimate(
                flops=8 * experts * window * width * columns,
                bytes_accessed=4 * experts * width * columns,
                transcendentals=0,
            ),
            name=f"gate_up_{index}",
        )(offsets, order, *operands)
        if first:
            keep, send, resid, spread_value = result
        else:
            keep, send = result
        aux_at = 2 * columns + tail[2] if first else None
        sums = core_sum(keep, swap(send), aux_at, f"core_sum_{index}")
        reduced.append([sums[0]] + [over_chips(sums[s], s) for s in range(1, half)])

    result = None
    for index, (number, columns) in enumerate(chunks):
        first, last = index == 0, index == len(chunks) - 1
        act, stats = activation(
            reduced[index], stats, columns, tail if first else None, float(features), f"activation_{index}"
        )
        parts = [act] + [over_chips(act, s) for s in range(1, half)]
        other = swap(jnp.stack(parts))
        operands = [*parts, other]
        in_specs = [full_spec(x.shape) for x in operands]
        operands.append(expert_down)
        in_specs.append(pl.BlockSpec((1, width, step), lambda e, *_, k=number: (e, 0, k)))
        if first:
            operands.append(expert_down)
            in_specs.append(pl.BlockSpec((1, width, LANES), lambda e, *_: (e, 0, tail_block)))
        else:
            operands.append(result)
            in_specs.append(full_spec(result.shape))
        sum_shape = jax.ShapeDtypeStruct((pairs, width), F32)
        scratch = [pltpu.VMEM((pairs, act.shape[1]), BF16)]
        outs = [sum_shape]
        if last:
            operands += [place_table, resid]
            in_specs += [full_spec(place_table.shape), full_spec(resid.shape)]
            outs = [jax.ShapeDtypeStruct((total, width), BF16)]
            scratch = [pltpu.VMEM(sum_shape.shape, F32)] + scratch
        result = pl.pallas_call(
            functools.partial(
                down_kernel, len(parts), columns, tail if first else None, window, first, last, total
            ),
            grid_spec=pltpu.PrefetchScalarGridSpec(
                num_scalar_prefetch=2,
                grid=(experts,),
                in_specs=in_specs,
                out_specs=[full_spec(x.shape) for x in outs],
                scratch_shapes=scratch,
            ),
            out_shape=outs,
            compiler_params=params(40 if pairs <= 1024 else 60),
            cost_estimate=pl.CostEstimate(
                flops=2 * experts * window * width * columns,
                bytes_accessed=2 * experts * width * columns,
                transcendentals=0,
            ),
            name=f"down_{index}",
        )(offsets, order, *operands)[0]

    back = lax.all_to_all(result.reshape(dp * fs, req, width), ("dp", "fsdp"), 0, 0, tiled=True)
    back = back.reshape(dp, fs, req, width).astype(F32)
    return jnp.sum(back, axis=1).transpose(1, 0, 2).reshape(req, features).astype(BF16)


def solution(mesh):
    placed = (
        P(("dp", "fsdp"), None),
        P("dp", None, None, "fsdp"),
        P("dp", None, "fsdp"),
        P("fsdp", "dp"),
        P(),
        P(),
        P(),
        P(None, "dp", None, "fsdp"),
        P(None, "dp", "fsdp"),
        P(),
        P("dp", None),
        P("dp", None),
        P("dp"),
        P(),
        P(("dp", "fsdp"), None),
    )
    return jax.shard_map(
        local, mesh=mesh, in_specs=placed, out_specs=P(("dp", "fsdp"), None), check_vma=False
    )
```

time: 786 us -> 194 us (0.25)
  blocking collectives: 348 us -> 12.4 us
  waiting for transfers between devices: 230 us -> 45.7 us
  local copies, waits for them, and re-layouts: 119 us -> 23.8 us
  Pallas kernels: 0 us -> 44.2 us
  matrix products: 39.8 us -> 0 us
  starting transfers between devices: 19.7 us -> 50.8 us
  between operations: 14.1 us -> 0.46 us
    all_to_all x2 -> x1, blocking collectives: 327 us -> 12.4 us  [local(): lax.all_to_all(result.reshape(dp * fs, req, width), ('dp', 'fsdp'), 0, 0,...]
    all_to_all x4 -> x1, waiting for transfers between devices: 164 us -> 0.01 us  [local(): lax.all_to_all(payload, ('dp', 'fsdp'), 0, 0, tiled=True)]
    ppermute x0 -> x35, waiting for transfers between devices: none -> 45.7 us  [the longest x24 35.6 us: over_chips(): return lax.ppermute(x, 'dp', [(i, i ^ 2 * s) for i in range(dp)])]
    pallas_call x0 -> x16, Pallas kernels: none -> 44.2 us  [the longest x3 23.9 us: local(): pl.pallas_call(functools.partial(gate_kernel, len(parts) if first else 0,...]
    ppermute x0 -> x35, starting transfers between devices: none -> 43.5 us  [the longest x24 38.3 us: over_chips(): return lax.ppermute(x, 'dp', [(i, i ^ 2 * s) for i in range(dp)])]
    unnamed x5 -> x0, waiting for transfers between devices: 43.1 us -> none
    dot_general x13 -> x0, matrix products: 39.8 us -> none  [the longest x1 8.91 us: local(): jnp.dot(flattened, gate_cols, preferred_element_type=jnp.float32)]
    gather x4 -> x0, local copies, waits for them, and re-layouts: 35.3 us -> none  [the longest x2 29.6 us: local(): resident_cache = cache_pool[page_list[:staying]]]
  transfers between devices with their start and end apart: 8 -> 36, of which waited for: 5 -> 12; matrix products, arithmetic and copies ran while one was open for 20% -> 7% of each run, Pallas kernels for 0% -> 14%
where the time goes in v1:
time: 194 us; the launch traced here: 193 us
  starting transfers between devices  50.8 us (26%)
  waiting for transfers between devices  45.7 us (24%)
  Pallas kernels  44.2 us (23%)
  local copies, waits for them, and re-layouts  23.8 us (12%)
  other arithmetic  15.4 us (8%)
  blocking collectives  12.4 us (6%)
    ppermute x24, starting transfers between devices, over_chips(): return lax.ppermute(x, 'dp', [(i, i ^ 2 * s) for i in range(dp)])  38.3 us
    ppermute x24, waiting for transfers between devices, over_chips(): return lax.ppermute(x, 'dp', [(i, i ^ 2 * s) for i in range(dp)])  35.6 us
    pallas_call x3, Pallas kernels, local(): pl.pallas_call(functools.partial(gate_kernel, len(parts) if first else 0,...  23.9 us
    unnamed x32, local copies, waits for them, and re-layouts  18.7 us
    all_to_all x1, blocking collectives, local(): lax.all_to_all(result.reshape(dp * fs, req, width), ('dp', 'fsdp'), 0, 0,...  12.4 us
    pallas_call x3, Pallas kernels, local(): pl.pallas_call(functools.partial(down_kernel, len(parts), columns, tail i...  10.4 us
    all_to_all x1, starting transfers between devices, local(): lax.all_to_all(payload, ('dp', 'fsdp'), 0, 0, tiled=True)  7.3 us
    ppermute x3, waiting for transfers between devices, over_columns(): return lax.ppermute(x, 'fsdp', [(i, i ^ s) for i in range(fs)])  7.1 us
  transfers between devices with their start and end apart: 36, of which 12 were waited for; matrix products, arithmetic and copies ran while one was open for 7% of the time, Pallas kernels for 14%

profile of v1, /device:TPU:0, one launch (start us, length us, event | category | flops | bytes accessed | tf_op | source)
XLA Modules:
  0.0 192.8 jit_solution(14364928976575707986)
XLA Ops:
  3.5 7.3 %all-to-all-start = ((bf16[32,8,384]{2,1,0:T(8,128)(2,1)}), bf16[32,8,384]{2,1,0:T(8,128)(2,1)S(1)}, u32[]{:S(2)}, u32[]{:S(2)}) async-start(bf16[32,8,384]{2,1,0:T(8,128)(2,1)} %bitcast.2), calls=%async_computation | async-start | bytes 393216 | tf_op jit(solution)/shard_map/all_to_all | solution.py:551
  21.8 4.1 %pool_split.1 = (bf16[2304,512]{1,0:T(8,128)(2,1)S(1)}, bf16[2304,512]{1,0:T(8,128)(2,1)S(1)}) custom-call(bf16[144,16,2,512]{3,2,1,0:T(2,128)(2,1)S(1)} %copy-done.12), custom_call_target="tpu_custom_call" | custom-call | flops 4831838208 | bytes 9437184 | tf_op jit(solution)/shard_map/pool_split/pallas_call | solution.py:60
  38.4 2.4 %collective-permute-start.2 = (bf16[32,1536]{1,0:T(8,128)(2,1)}, bf16[32,1536]{1,0:T(8,128)(2,1)S(1)}, u32[]{:S(2)}, u32[]{:S(2)}) collective-permute-start(bf16[32,1536]{1,0:T(8,128)(2,1)} %get-tuple-element.62), channel_id=1, source_target_pairs={{0,16},{4,20},{8,24},{12,28},{16,0},{20,4},{24,8},{28,12},{1,17},{... | collective-permute-start | bytes 294920 | tf_op jit(solution)/shard_map/ppermute | solution.py:526
  41.8 7.5 %collective-permute-done.2.refs_2_ = bf16[32,1536]{1,0:T(8,128)(2,1)S(1)} collective-permute-done((bf16[32,1536]{1,0:T(8,128)(2,1)}, bf16[32,1536]{1,0:T(8,128)(2,1)S(1)}, u32[]{:S(2)}, u32[]{:S(2)}) %collective-permute-start.2) | collective-permute-done | bytes 98336 | tf_op jit(solution)/shard_map/ppermute | solution.py:526
  71.0 3.1 %collective-permute-done.8.refs_1_ = bf16[288,256]{1,0:T(8,128)(2,1)S(1)} collective-permute-done((bf16[288,256]{1,0:T(8,128)(2,1)S(1)}, bf16[288,256]{1,0:T(8,128)(2,1)S(1)}, u32[]{:S(2)}, u32[]{:S(2)}) %collective-permute-start.8) | collective-permute-done | bytes 147488 | tf_op jit(solution)/shard_map/ppermute | solution.py:529
  74.2 3.9 %collective-permute-done.9.refs_2_ = bf16[288,256]{1,0:T(8,128)(2,1)S(1)} collective-permute-done((bf16[288,256]{1,0:T(8,128)(2,1)S(1)}, bf16[288,256]{1,0:T(8,128)(2,1)S(1)}, u32[]{:S(2)}, u32[]{:S(2)}) %collective-permute-start.9) | collective-permute-done | bytes 147488 | tf_op jit(solution)/shard_map/ppermute | solution.py:529
  78.1 9.5 %gate_up_0.1 = (bf16[4,64,1152]{2,1,0:T(8,128)(2,1)S(1)}, bf16[4,64,1152]{2,1,0:T(8,128)(2,1)S(1)}, f32[288,256]{1,0:T(8,128)S(1)}, bf16[2,512,576]{2,1,0:T(8,128)(2,1)S(1)}) custom-call(s32[9]{0:T(128)S(1)} %pad_add_fusion.4.offset_ref, s32[8]{0:T(128)S(1)} %pad_add_fusion.5.order_ref, bf16[288,256]{1,0:T(8,128)(2,1)S(1)} %out_projection.1.refs_0_, ...), custom_call_target="tpu_custom_call" | custom-call | flops 1358954496 | bytes 4718592 | tf_op jit(solution)/shard_map/gate_up_0/pallas_call | solution.py:649
  87.8 7.1 %gate_up_1.1 = (bf16[4,64,1024]{2,1,0:T(8,128)(2,1)S(1)}, bf16[4,64,1024]{2,1,0:T(8,128)(2,1)S(1)}) custom-call(s32[9]{0:T(128)S(1)} %pad_add_fusion.4.offset_ref, s32[8]{0:T(128)S(1)} %pad_add_fusion.5.order_ref, bf16[2,512,576]{2,1,0:T(8,128)(2,1)S(1)} %get-tuple-element.37.refs_0_, bf16[8,288,2,1440]{3,2,1,0:T(2,128)(2,1)} %refs_1_.3), custom_call_target="tpu_custom_call" | custom-call | flops 1358954496 | bytes 4718592 | tf_op jit(solution)/shard_map/gate_up_1/pallas_call | solution.py:649
  95.4 7.2 %gate_up_2.1 = (bf16[4,64,768]{2,1,0:T(8,128)(2,1)S(1)}, bf16[4,64,768]{2,1,0:T(8,128)(2,1)S(1)}) custom-call(s32[9]{0:T(128)S(1)} %pad_add_fusion.4.offset_ref, s32[8]{0:T(128)S(1)} %pad_add_fusion.5.order_ref, bf16[2,512,576]{2,1,0:T(8,128)(2,1)S(1)} %get-tuple-element.37.refs_0_, bf16[8,288,2,1440]{3,2,1,0:T(2,128)(2,1)} %refs_1_.3), custom_call_target="tpu_custom_call" | custom-call | flops 1019215872 | bytes 3538944 | tf_op jit(solution)/shard_map/gate_up_2/pallas_call | solution.py:649
  105.5 2.4 %collective-permute-start.18 = (bf16[64,1152]{1,0:T(8,128)(2,1)S(1)}, bf16[64,1152]{1,0:T(8,128)(2,1)S(1)}, u32[]{:S(2)}, u32[]{:S(2)}) collective-permute-start(bf16[64,1152]{1,0:T(8,128)(2,1)S(1)} %get-tuple-element.49), channel_id=1, source_target_pairs={{0,24},{4,28},{8,16},{12,20},{16,8},{20,12},{24,0},{28,4},{1,25},{... | collective-permute-start | bytes 442376 | tf_op jit(solution)/shard_map/ppermute | solution.py:526
  110.4 8.2 %collective-permute-done.12.refs_1_ = bf16[64,768]{1,0:T(8,128)(2,1)S(1)} collective-permute-done((bf16[64,768]{1,0:T(8,128)(2,1)S(1)}, bf16[64,768]{1,0:T(8,128)(2,1)S(1)}, u32[]{:S(2)}, u32[]{:S(2)}) %collective-permute-start.12) | collective-permute-done | bytes 98336 | tf_op jit(solution)/shard_map/ppermute | solution.py:526
  118.7 2.4 %collective-permute-start.14 = (bf16[64,768]{1,0:T(8,128)(2,1)S(1)}, bf16[64,768]{1,0:T(8,128)(2,1)S(1)}, u32[]{:S(2)}, u32[]{:S(2)}) collective-permute-start(bf16[64,768]{1,0:T(8,128)(2,1)S(1)} %get-tuple-element.43), channel_id=1, source_target_pairs={{0,24},{4,28},{8,16},{12,20},{16,8},{20,12},{24,0},{28,4},{1,25},{... | collective-permute-start | bytes 294920 | tf_op jit(solution)/shard_map/ppermute | solution.py:526
  122.0 2.4 %collective-permute-start.26 = (bf16[64,1024]{1,0:T(8,128)(2,1)S(1)}, bf16[64,1024]{1,0:T(8,128)(2,1)S(1)}, u32[]{:S(2)}, u32[]{:S(2)}) collective-permute-start(bf16[64,1024]{1,0:T(8,128)(2,1)S(1)} %get-tuple-element.56), channel_id=1, source_target_pairs={{0,24},{4,28},{8,16},{12,20},{16,8},{20,12},{24,0},{28,4},{1,25},{... | collective-permute-start | bytes 393224 | tf_op jit(solution)/shard_map/ppermute | solution.py:526
  124.9 8.5 %collective-permute-done.13.refs_2_ = bf16[64,768]{1,0:T(8,128)(2,1)S(1)} collective-permute-done((bf16[64,768]{1,0:T(8,128)(2,1)S(1)}, bf16[64,768]{1,0:T(8,128)(2,1)S(1)}, u32[]{:S(2)}, u32[]{:S(2)}) %collective-permute-start.13) | collective-permute-done | bytes 98336 | tf_op jit(solution)/shard_map/ppermute | solution.py:526
  133.5 2.7 %collective-permute-start.19 = (bf16[64,384]{1,0:T(8,128)(2,1)S(1)}, bf16[64,384]{1,0:T(8,128)(2,1)S(1)}, u32[]{:S(2)}, u32[]{:S(2)}) collective-permute-start(bf16[64,384]{1,0:T(8,128)(2,1)S(1)} %activation_2.1.refs_0_), channel_id=1, source_target_pairs={{0,8},{4,12},{8,0},{12,4},{16,24},{20,28},{24,16},{28,20},{1,9},{5... | collective-permute-start | bytes 147464 | tf_op jit(solution)/shard_map/ppermute | solution.py:526
  139.1 4.9 %collective-permute-start.27 = (bf16[64,512]{1,0:T(8,128)(2,1)S(1)}, bf16[64,512]{1,0:T(8,128)(2,1)S(1)}, u32[]{:S(2)}, u32[]{:S(2)}) collective-permute-start(bf16[64,512]{1,0:T(8,128)(2,1)S(1)} %activation_1.1.refs_0_), channel_id=1, source_target_pairs={{0,8},{4,12},{8,0},{12,4},{16,24},{20,28},{24,16},{28,20},{1,9},{5... | collective-permute-start | bytes 196616 | tf_op jit(solution)/shard_map/ppermute | solution.py:526
  153.0 5.4 %collective-permute-done.32.refs_2_ = bf16[64,640]{1,0:T(8,128)(2,1)S(1)} collective-permute-done((bf16[64,640]{1,0:T(8,128)(2,1)S(1)}, bf16[64,640]{1,0:T(8,128)(2,1)S(1)}, u32[]{:S(2)}, u32[]{:S(2)}) %collective-permute-start.32) | collective-permute-done | bytes 81952 | tf_op jit(solution)/shard_map/ppermute | solution.py:526
  160.2 3.0 %copy-done.1 = bf16[8,288,1440]{2,1,0:T(8,128)(2,1)S(1)} copy-done((bf16[8,288,1440]{2,1,0:T(8,128)(2,1)S(1)}, bf16[8,288,1440]{2,1,0:T(8,128)(2,1)}, u32[]{:S(2)}) %copy-start.1) | copy-done | bytes 6635544
  163.2 3.5 %down_0.1.refs_6_ = f32[512,288]{1,0:T(8,128)S(1)} custom-call(s32[9]{0:T(128)S(1)} %pad_add_fusion.4.offset_ref, s32[8]{0:T(128)S(1)} %pad_add_fusion.5.order_ref, bf16[64,640]{1,0:T(8,128)(2,1)S(1)} %get-tuple-element.57.refs_0_, bf16[64,640]{1,0:T(8,128)(2,1)S(1)} %collective-permute-done.31.refs_1_, bf16[64,640]{1,0:T(8,128)(2,1)S(1)} %collective-permute-done.32.refs_2_, ...), custom_call_target="tpu_custom_call" | custom-call | flops 339738624 | bytes 2359296 | tf_op jit(solution)/shard_map/down_0/pallas_call | solution.py:701
  166.7 3.0 %copy-done.2 = bf16[8,288,1440]{2,1,0:T(8,128)(2,1)S(1)} copy-done((bf16[8,288,1440]{2,1,0:T(8,128)(2,1)S(1)}, bf16[8,288,1440]{2,1,0:T(8,128)(2,1)}, u32[]{:S(2)}) %copy-start.2) | copy-done | bytes 6635544
  169.7 3.3 %down_1.1.refs_6_ = f32[512,288]{1,0:T(8,128)S(1)} custom-call(s32[9]{0:T(128)S(1)} %pad_add_fusion.4.offset_ref, s32[8]{0:T(128)S(1)} %pad_add_fusion.5.order_ref, bf16[64,512]{1,0:T(8,128)(2,1)S(1)} %activation_1.1.refs_0_, bf16[64,512]{1,0:T(8,128)(2,1)S(1)} %collective-permute-done.27.refs_1_, bf16[64,512]{1,0:T(8,128)(2,1)S(1)} %collective-permute-done.28.refs_2_, ...), custom_call_target="tpu_custom_call" | custom-call | flops 339738624 | bytes 2359296 | tf_op jit(solution)/shard_map/down_1/pallas_call | solution.py:701
  173.0 3.0 %copy-done.3 = bf16[8,288,1440]{2,1,0:T(8,128)(2,1)S(1)} copy-done((bf16[8,288,1440]{2,1,0:T(8,128)(2,1)S(1)}, bf16[8,288,1440]{2,1,0:T(8,128)(2,1)}, u32[]{:S(2)}) %copy-start.3) | copy-done | bytes 6635544
  176.0 3.6 %down_2.1 = bf16[256,288]{1,0:T(8,128)(2,1)S(1)} custom-call(s32[9]{0:T(128)S(1)} %pad_add_fusion.4.offset_ref, s32[8]{0:T(128)S(1)} %pad_add_fusion.5.order_ref, bf16[64,384]{1,0:T(8,128)(2,1)S(1)} %activation_2.1.refs_0_, bf16[64,384]{1,0:T(8,128)(2,1)S(1)} %collective-permute-done.19.refs_1_, bf16[64,384]{1,0:T(8,128)(2,1)S(1)} %collective-permute-done.20.refs_2_, ...), custom_call_target="tpu_custom_call" | custom-call | flops 254803968 | bytes 1769472 | tf_op jit(solution)/shard_map/down_2/pallas_call | solution.py:701
  179.6 12.4 %all_to_all.10 = bf16[32,8,288]{2,1,0:T(8,128)(2,1)S(1)} all-to-all(bf16[32,8,288]{2,1,0:T(8,128)(2,1)S(1)} %bitcast.67), channel_id=1, replica_groups=mesh['dp'=8,'fsdp'=4] {'dp','fsdp'}, dimensions={0} | all-to-all | bytes 294912 | tf_op jit(solution)/shard_map/all_to_all | solution.py:722
  (174 shorter events, 71.3 us)
Async XLA Ops:
  3.5 23.9 %all-to-all-start = ((bf16[32,8,384]{2,1,0:T(8,128)(2,1)}), bf16[32,8,384]{2,1,0:T(8,128)(2,1)S(1)}, u32[]{:S(2)}, u32[]{:S(2)}) async-start(bf16[32,8,384]{2,1,0:T(8,128)(2,1)} %bitcast.2), calls=%async_computation | async-start | bytes 393216 | tf_op jit(solution)/shard_map/all_to_all | solution.py:551
  38.4 10.9 %collective-permute-start.2 = (bf16[32,1536]{1,0:T(8,128)(2,1)}, bf16[32,1536]{1,0:T(8,128)(2,1)S(1)}, u32[]{:S(2)}, u32[]{:S(2)}) collective-permute-start(bf16[32,1536]{1,0:T(8,128)(2,1)} %get-tuple-element.62), channel_id=1, source_target_pairs={{0,16},{4,20},{8,24},{12,28},{16,0},{20,4},{24,8},{28,12},{1,17},{... | collective-permute-start | bytes 294920 | tf_op jit(solution)/shard_map/ppermute | solution.py:526
  40.8 8.5 %collective-permute-start.3 = (bf16[32,1536]{1,0:T(8,128)(2,1)}, bf16[32,1536]{1,0:T(8,128)(2,1)S(1)}, u32[]{:S(2)}, u32[]{:S(2)}) collective-permute-start(bf16[32,1536]{1,0:T(8,128)(2,1)} %get-tuple-element.61), channel_id=1, source_target_pairs={{0,24},{4,28},{8,16},{12,20},{16,8},{20,12},{24,0},{28,4},{1,25},{... | collective-permute-start | bytes 294920 | tf_op jit(solution)/shard_map/ppermute | solution.py:526
  69.0 9.1 %collective-permute-start.9 = (bf16[288,256]{1,0:T(8,128)(2,1)S(1)}, bf16[288,256]{1,0:T(8,128)(2,1)S(1)}, u32[]{:S(2)}, u32[]{:S(2)}) collective-permute-start(bf16[288,256]{1,0:T(8,128)(2,1)S(1)} %out_projection.1.refs_0_), channel_id=1, source_target_pairs={{0,2},{1,3},{2,0},{3,1},{4,6},{5,7},{6,4},{7,5},{8,10},{9,11},{10,... | collective-permute-start | bytes 442376 | tf_op jit(solution)/shard_map/ppermute | solution.py:529
  87.7 15.1 %collective-permute-start.15 = (bf16[4,64,1152]{2,1,0:T(8,128)(2,1)S(1)}, bf16[4,64,1152]{2,1,0:T(8,128)(2,1)S(1)}, u32[]{:S(2)}, u32[]{:S(2)}) collective-permute-start(bf16[4,64,1152]{2,1,0:T(8,128)(2,1)S(1)} %get-tuple-element.45), channel_id=1, source_target_pairs={{0,4},{4,0},{8,12},{12,8},{16,20},{20,16},{24,28},{28,24},{1,5},{5... | collective-permute-start | bytes 1769480 | tf_op jit(solution)/shard_map/ppermute | solution.py:523
  94.9 13.2 %collective-permute-start.23 = (bf16[4,64,1024]{2,1,0:T(8,128)(2,1)S(1)}, bf16[4,64,1024]{2,1,0:T(8,128)(2,1)S(1)}, u32[]{:S(2)}, u32[]{:S(2)}) collective-permute-start(bf16[4,64,1024]{2,1,0:T(8,128)(2,1)S(1)} %get-tuple-element.52), channel_id=1, source_target_pairs={{0,4},{4,0},{8,12},{12,8},{16,20},{20,16},{24,28},{28,24},{1,5},{5... | collective-permute-start | bytes 1572872 | tf_op jit(solution)/shard_map/ppermute | solution.py:523
  103.4 15.3 %collective-permute-start.16 = (bf16[64,1152]{1,0:T(8,128)(2,1)S(1)}, bf16[64,1152]{1,0:T(8,128)(2,1)S(1)}, u32[]{:S(2)}, u32[]{:S(2)}) collective-permute-start(bf16[64,1152]{1,0:T(8,128)(2,1)S(1)} %get-tuple-element.47), channel_id=1, source_target_pairs={{0,8},{4,12},{8,0},{12,4},{16,24},{20,28},{24,16},{28,20},{1,9},{5... | collective-permute-start | bytes 442376 | tf_op jit(solution)/shard_map/ppermute | solution.py:526
  103.5 17.6 %collective-permute-start.17 = (bf16[64,1152]{1,0:T(8,128)(2,1)S(1)}, bf16[64,1152]{1,0:T(8,128)(2,1)S(1)}, u32[]{:S(2)}, u32[]{:S(2)}) collective-permute-start(bf16[64,1152]{1,0:T(8,128)(2,1)S(1)} %get-tuple-element.48), channel_id=1, source_target_pairs={{0,16},{4,20},{8,24},{12,28},{16,0},{20,4},{24,8},{28,12},{1,17},{... | collective-permute-start | bytes 442376 | tf_op jit(solution)/shard_map/ppermute | solution.py:526
  105.5 16.5 %collective-permute-start.18 = (bf16[64,1152]{1,0:T(8,128)(2,1)S(1)}, bf16[64,1152]{1,0:T(8,128)(2,1)S(1)}, u32[]{:S(2)}, u32[]{:S(2)}) collective-permute-start(bf16[64,1152]{1,0:T(8,128)(2,1)S(1)} %get-tuple-element.49), channel_id=1, source_target_pairs={{0,24},{4,28},{8,16},{12,20},{16,8},{20,12},{24,0},{28,4},{1,25},{... | collective-permute-start | bytes 442376 | tf_op jit(solution)/shard_map/ppermute | solution.py:526
  108.0 10.6 %collective-permute-start.12 = (bf16[64,768]{1,0:T(8,128)(2,1)S(1)}, bf16[64,768]{1,0:T(8,128)(2,1)S(1)}, u32[]{:S(2)}, u32[]{:S(2)}) collective-permute-start(bf16[64,768]{1,0:T(8,128)(2,1)S(1)} %get-tuple-element.41), channel_id=1, source_target_pairs={{0,8},{4,12},{8,0},{12,4},{16,24},{20,28},{24,16},{28,20},{1,9},{5... | collective-permute-start | bytes 294920 | tf_op jit(solution)/shard_map/ppermute | solution.py:526
  108.2 28.5 %collective-permute-start.24 = (bf16[64,1024]{1,0:T(8,128)(2,1)S(1)}, bf16[64,1024]{1,0:T(8,128)(2,1)S(1)}, u32[]{:S(2)}, u32[]{:S(2)}) collective-permute-start(bf16[64,1024]{1,0:T(8,128)(2,1)S(1)} %get-tuple-element.54), channel_id=1, source_target_pairs={{0,8},{4,12},{8,0},{12,4},{16,24},{20,28},{24,16},{28,20},{1,9},{5... | collective-permute-start | bytes 393224 | tf_op jit(solution)/shard_map/ppermute | solution.py:526
  118.6 14.8 %collective-permute-start.13 = (bf16[64,768]{1,0:T(8,128)(2,1)S(1)}, bf16[64,768]{1,0:T(8,128)(2,1)S(1)}, u32[]{:S(2)}, u32[]{:S(2)}) collective-permute-start(bf16[64,768]{1,0:T(8,128)(2,1)S(1)} %get-tuple-element.42), channel_id=1, source_target_pairs={{0,16},{4,20},{8,24},{12,28},{16,0},{20,4},{24,8},{28,12},{1,17},{... | collective-permute-start | bytes 294920 | tf_op jit(solution)/shard_map/ppermute | solution.py:526
  118.7 14.7 %collective-permute-start.14 = (bf16[64,768]{1,0:T(8,128)(2,1)S(1)}, bf16[64,768]{1,0:T(8,128)(2,1)S(1)}, u32[]{:S(2)}, u32[]{:S(2)}) collective-permute-start(bf16[64,768]{1,0:T(8,128)(2,1)S(1)} %get-tuple-element.43), channel_id=1, source_target_pairs={{0,24},{4,28},{8,16},{12,20},{16,8},{20,12},{24,0},{28,4},{1,25},{... | collective-permute-start | bytes 294920 | tf_op jit(solution)/shard_map/ppermute | solution.py:526
  121.1 17.8 %collective-permute-start.25 = (bf16[64,1024]{1,0:T(8,128)(2,1)S(1)}, bf16[64,1024]{1,0:T(8,128)(2,1)S(1)}, u32[]{:S(2)}, u32[]{:S(2)}) collective-permute-start(bf16[64,1024]{1,0:T(8,128)(2,1)S(1)} %get-tuple-element.55), channel_id=1, source_target_pairs={{0,16},{4,20},{8,24},{12,28},{16,0},{20,4},{24,8},{28,12},{1,17},{... | collective-permute-start | bytes 393224 | tf_op jit(solution)/shard_map/ppermute | solution.py:526
  122.0 16.9 %collective-permute-start.26 = (bf16[64,1024]{1,0:T(8,128)(2,1)S(1)}, bf16[64,1024]{1,0:T(8,128)(2,1)S(1)}, u32[]{:S(2)}, u32[]{:S(2)}) collective-permute-start(bf16[64,1024]{1,0:T(8,128)(2,1)S(1)} %get-tuple-element.56), channel_id=1, source_target_pairs={{0,24},{4,28},{8,16},{12,20},{16,8},{20,12},{24,0},{28,4},{1,25},{... | collective-permute-start | bytes 393224 | tf_op jit(solution)/shard_map/ppermute | solution.py:526
  133.5 10.9 %collective-permute-start.19 = (bf16[64,384]{1,0:T(8,128)(2,1)S(1)}, bf16[64,384]{1,0:T(8,128)(2,1)S(1)}, u32[]{:S(2)}, u32[]{:S(2)}) collective-permute-start(bf16[64,384]{1,0:T(8,128)(2,1)S(1)} %activation_2.1.refs_0_), channel_id=1, source_target_pairs={{0,8},{4,12},{8,0},{12,4},{16,24},{20,28},{24,16},{28,20},{1,9},{5... | collective-permute-start | bytes 147464 | tf_op jit(solution)/shard_map/ppermute | solution.py:526
  136.3 10.2 %collective-permute-start.20 = (bf16[64,384]{1,0:T(8,128)(2,1)S(1)}, bf16[64,384]{1,0:T(8,128)(2,1)S(1)}, u32[]{:S(2)}, u32[]{:S(2)}) collective-permute-start(bf16[64,384]{1,0:T(8,128)(2,1)S(1)} %activation_2.1.refs_0_), channel_id=1, source_target_pairs={{0,16},{4,20},{8,24},{12,28},{16,0},{20,4},{24,8},{28,12},{1,17},{... | collective-permute-start | bytes 147464 | tf_op jit(solution)/shard_map/ppermute | solution.py:526
  136.7 10.8 %collective-permute-start.21 = (bf16[64,384]{1,0:T(8,128)(2,1)S(1)}, bf16[64,384]{1,0:T(8,128)(2,1)S(1)}, u32[]{:S(2)}, u32[]{:S(2)}) collective-permute-start(bf16[64,384]{1,0:T(8,128)(2,1)S(1)} %activation_2.1.refs_0_), channel_id=1, source_target_pairs={{0,24},{4,28},{8,16},{12,20},{16,8},{20,12},{24,0},{28,4},{1,25},{... | collective-permute-start | bytes 147464 | tf_op jit(solution)/shard_map/ppermute | solution.py:526
  139.1 9.8 %collective-permute-start.27 = (bf16[64,512]{1,0:T(8,128)(2,1)S(1)}, bf16[64,512]{1,0:T(8,128)(2,1)S(1)}, u32[]{:S(2)}, u32[]{:S(2)}) collective-permute-start(bf16[64,512]{1,0:T(8,128)(2,1)S(1)} %activation_1.1.refs_0_), channel_id=1, source_target_pairs={{0,8},{4,12},{8,0},{12,4},{16,24},{20,28},{24,16},{28,20},{1,9},{5... | collective-permute-start | bytes 196616 | tf_op jit(solution)/shard_map/ppermute | solution.py:526
  144.0 8.4 %collective-permute-start.28 = (bf16[64,512]{1,0:T(8,128)(2,1)S(1)}, bf16[64,512]{1,0:T(8,128)(2,1)S(1)}, u32[]{:S(2)}, u32[]{:S(2)}) collective-permute-start(bf16[64,512]{1,0:T(8,128)(2,1)S(1)} %activation_1.1.refs_0_), channel_id=1, source_target_pairs={{0,16},{4,20},{8,24},{12,28},{16,0},{20,4},{24,8},{28,12},{1,17},{... | collective-permute-start | bytes 196616 | tf_op jit(solution)/shard_map/ppermute | solution.py:526
  147.5 10.9 %collective-permute-start.32 = (bf16[64,640]{1,0:T(8,128)(2,1)S(1)}, bf16[64,640]{1,0:T(8,128)(2,1)S(1)}, u32[]{:S(2)}, u32[]{:S(2)}) collective-permute-start(bf16[64,640]{1,0:T(8,128)(2,1)S(1)} %get-tuple-element.57.refs_0_), channel_id=1, source_target_pairs={{0,16},{4,20},{8,24},{12,28},{16,0},{20,4},{24,8},{28,12},{1,17},{... | collective-permute-start | bytes 245768 | tf_op jit(solution)/shard_map/ppermute | solution.py:526
  148.9 9.5 %collective-permute-start.33 = (bf16[64,640]{1,0:T(8,128)(2,1)S(1)}, bf16[64,640]{1,0:T(8,128)(2,1)S(1)}, u32[]{:S(2)}, u32[]{:S(2)}) collective-permute-start(bf16[64,640]{1,0:T(8,128)(2,1)S(1)} %get-tuple-element.57.refs_0_), channel_id=1, source_target_pairs={{0,24},{4,28},{8,16},{12,20},{16,8},{20,12},{24,0},{28,4},{1,25},{... | collective-permute-start | bytes 245768 | tf_op jit(solution)/shard_map/ppermute | solution.py:526
  152.4 20.6 %collective-permute-start.22 = (bf16[4,64,384]{2,1,0:T(8,128)(2,1)S(1)}, bf16[4,64,384]{2,1,0:T(8,128)(2,1)S(1)}, u32[]{:S(2)}, u32[]{:S(2)}) collective-permute-start(bf16[4,64,384]{2,1,0:T(8,128)(2,1)S(1)} %pad_maximum_fusion.2), channel_id=1, source_target_pairs={{0,4},{4,0},{8,12},{12,8},{16,20},{20,16},{24,28},{28,24},{1,5},{5... | collective-permute-start | bytes 589832 | tf_op jit(solution)/shard_map/ppermute | solution.py:523
  152.5 14.3 %collective-permute-start.30 = (bf16[4,64,512]{2,1,0:T(8,128)(2,1)S(1)}, bf16[4,64,512]{2,1,0:T(8,128)(2,1)S(1)}, u32[]{:S(2)}, u32[]{:S(2)}) collective-permute-start(bf16[4,64,512]{2,1,0:T(8,128)(2,1)S(1)} %pad_maximum_fusion.1), channel_id=1, source_target_pairs={{0,4},{4,0},{8,12},{12,8},{16,20},{20,16},{24,28},{28,24},{1,5},{5... | collective-permute-start | bytes 786440 | tf_op jit(solution)/shard_map/ppermute | solution.py:523
  (28 other events, 154.0 us)

commit v2 on v1

v2 whole, which is shorter than its diff:
```python
import functools

import jax
import jax.numpy as jnp
from jax import lax
from jax.experimental import pallas as pl
from jax.experimental.pallas import tpu as pltpu
from jax.sharding import PartitionSpec as P

HD = 64
CAP = 4
PIECES = 3
LANES = 128
BF16 = jnp.bfloat16
F32 = jnp.float32
FAR = -3.0e38
SMALL, ATTENTION, LARGE = 12, 24, 60
SLOTS = 4


def params(mib=SMALL):
    return pltpu.CompilerParams(vmem_limit_bytes=mib * 2**20)


def room(tokens):
    return SMALL if tokens <= 512 else LARGE


def dot_nn(a, b):
    return lax.dot_general(a, b, (((1,), (0,)), ((), ())), preferred_element_type=F32)


def dot_nt(a, b):
    return lax.dot_general(a, b, (((1,), (1,)), ((), ())), preferred_element_type=F32)


def split_bf16(value, count=PIECES):
    pieces = []
    for _ in range(count):
        piece = value.astype(BF16).astype(F32)
        pieces.append(piece)
        value = value - piece
    return pieces


def full_spec(shape):
    zeros = (0,) * len(shape)
    return pl.BlockSpec(tuple(shape), lambda *_: zeros, pipeline_mode=pl.Buffered(1))


def pack_kernel(hidden_ref, routes_ref, out_ref):
    slices, copies, req, room = out_ref.shape
    features = hidden_ref.shape[1]
    width = features // slices
    values = hidden_ref[...].astype(F32)
    factor = lax.rsqrt(jnp.mean(values * values, axis=1, keepdims=True) + 1e-06)
    lane = lax.broadcasted_iota(jnp.int32, (req, room), 1)
    extra = jnp.zeros((req, room), F32)
    for k, piece in enumerate(split_bf16(factor)):
        extra = jnp.where(lane == width + k, piece, extra)
    spot = lax.broadcasted_iota(jnp.int32, (req, req), 1) == lax.broadcasted_iota(jnp.int32, (req, req), 0)
    for k in range(2):
        route = jnp.sum(jnp.where(spot, routes_ref[k : k + 1].astype(F32), 0.0), axis=1, keepdims=True)
        extra = jnp.where(lane == width + PIECES + k, route, extra)
    for index in range(slices):
        moved = pltpu.roll(values, (features - index * width) % features, 1) if index else values
        block = jnp.where(lane < width, moved[:, :room], extra).astype(BF16)
        for copy in range(copies):
            out_ref[index, copy] = block


def pack(hidden_in, routes, slices, copies):
    req, features = hidden_in.shape
    width = features // slices
    room = -(-(width + PIECES + 2) // LANES) * LANES
    out = (slices, copies, req, room)
    return pl.pallas_call(
        pack_kernel,
        grid=(1,),
        in_specs=[full_spec(hidden_in.shape), full_spec(routes.shape)],
        out_specs=full_spec(out),
        out_shape=jax.ShapeDtypeStruct(out, BF16),
        compiler_params=params(),
        cost_estimate=pl.CostEstimate(flops=hidden_in.size, bytes_accessed=4 * hidden_in.size, transcendentals=0),
        name="pack",
    )(hidden_in, routes)


def places_kernel(
    experts, width, staying, move_ref, order_ref, slot_ref, column_ref, recv_ref, _, off_ref, place_ref, line_ref, table, slots
):
    total = recv_ref.shape[0]
    rows_count, movers = move_ref.shape
    row = total // rows_count
    block = min(total, 256)
    lane = lax.broadcasted_iota(jnp.int32, (block, LANES), 1)
    above = lax.broadcasted_iota(jnp.int32, (block, block), 0)
    beside = lax.broadcasted_iota(jnp.int32, (block, block), 1)
    before = (beside < above).astype(F32).astype(BF16)
    counts = jnp.zeros((1, LANES), F32)
    for start in range(0, total, block):
        here = slice(start, start + block)
        first = recv_ref[here, width + PIECES : width + PIECES + 1].astype(F32).astype(jnp.int32)
        second = recv_ref[here, width + PIECES + 1 : width + PIECES + 2].astype(F32).astype(jnp.int32)
        member = (lane == first).astype(F32) + (lane == second).astype(F32)
        rank = dot_nn(before, member.astype(BF16)) + counts
        counts = counts + jnp.sum(member, axis=0, keepdims=True)
        mine = jnp.sum(jnp.where(lane == first, rank, 0.0), axis=1, keepdims=True)
        other = jnp.sum(jnp.where(lane == second, rank, 0.0), axis=1, keepdims=True)
        block_table = jnp.where(lane == 0, mine, jnp.where(lane == 1, other, 0.0))
        block_table = jnp.where(lane == 2, first.astype(F32), block_table)
        table[here] = jnp.where(lane == 3, second.astype(F32), block_table)
    single = lax.broadcasted_iota(jnp.int32, (1, LANES), 1)
    sums = [jnp.sum(jnp.where(single == e, counts, 0.0)) for e in range(experts)]
    off_ref[0] = 0
    running = jnp.float32(0.0)
    begins = jnp.zeros((1, LANES), F32)
    for e in range(experts):
        begins = jnp.where(single == e, running, begins)
        running = running + sums[e]
        off_ref[e + 1] = running.astype(jnp.int32)
    for start in range(0, total, block):
        here = slice(start, start + block)
        values = table[here]
        first = values[:, 2:3].astype(jnp.int32)
        second = values[:, 3:4].astype(jnp.int32)
        begin_first = jnp.sum(jnp.where(lane == first, begins, 0.0), axis=1, keepdims=True)
        begin_second = jnp.sum(jnp.where(lane == second, begins, 0.0), axis=1, keepdims=True)
        values = values + jnp.where(lane == 0, begin_first, jnp.where(lane == 1, begin_second, 0.0))
        table[here] = values
        place_ref[here] = values
    within = lax.broadcasted_iota(jnp.int32, (row, LANES), 0)
    wide = lax.broadcasted_iota(jnp.int32, (row, LANES), 1)
    req = row // column_ref[1]
    mine = (within >= column_ref[0] * req) & (within < (column_ref[0] + 1) * req)
    for r in range(rows_count):
        here = slice(r * row, (r + 1) * row)
        lies = jnp.where(mine, (within + slot_ref[r] * row).astype(F32), -1.0)
        place_ref[here] = jnp.where(wide == 2, lies, place_ref[here])
    for r in range(rows_count):
        for j in range(movers):
            at = staying + j
            target = pl.ds(move_ref[r, j] * row + at, 1)
            held = (at >= column_ref[0] * req) & (at < (column_ref[0] + 1) * req)
            lies = jnp.where(held, slot_ref[r] * row + at, -1).astype(F32)
            place_ref[target] = jnp.where(single == 2, lies, place_ref[target])
    for b in range(rows_count):
        slots[b * row : (b + 1) * row] = table[pl.ds(pl.multiple_of(order_ref[b] * row, row), row)]
        for j in range(movers):
            at = staying + j
            source = pl.ds(move_ref[order_ref[b], j] * row + at, 1)
            slots[b * row + at : b * row + at + 1] = table[source]
    line_ref[...] = slots[...].T[:8]


def pair_places(move_target, order, slot_of, column, recv, after, experts, width):
    total = recv.shape[0]
    rows_count, movers = move_target.shape
    staying = total // rows_count - movers
    outs = [
        jax.ShapeDtypeStruct((experts + 1,), jnp.int32),
        jax.ShapeDtypeStruct((total, LANES), F32),
        jax.ShapeDtypeStruct((8, total), F32),
    ]
    return pl.pallas_call(
        functools.partial(places_kernel, experts, width, staying),
        grid_spec=pltpu.PrefetchScalarGridSpec(
            num_scalar_prefetch=4,
            grid=(1,),
            in_specs=[full_spec(recv.shape), pl.BlockSpec(memory_space=pl.ANY)],
            out_specs=[
                pl.BlockSpec(memory_space=pltpu.SMEM),
                full_spec(outs[1].shape),
                full_spec(outs[2].shape),
            ],
            scratch_shapes=[pltpu.VMEM((total, LANES), F32), pltpu.VMEM((total, LANES), F32)],
        ),
        out_shape=outs,
        compiler_params=params(room(total)),
        cost_estimate=pl.CostEstimate(
            flops=total * total * LANES, bytes_accessed=16 * total * LANES, transcendentals=0
        ),
        name="pair_places",
    )(move_target, order, slot_of, column, recv, after)


def pool_kernel(prompt_ref, lists_ref, pool_ref, _, key_ref, value_ref, bias_ref):
    pages, page_len, _, cols = pool_ref.shape
    rows = pages * page_len
    both = pool_ref[...].reshape(2 * rows, cols)
    wide = lax.broadcasted_iota(jnp.int32, (rows, 2 * rows), 1)
    high = lax.broadcasted_iota(jnp.int32, (rows, 2 * rows), 0)
    key_ref[...] = dot_nn((wide == 2 * high).astype(BF16), both).astype(BF16)
    value_ref[...] = dot_nn((wide == 2 * high + 1).astype(BF16), both).astype(BF16)
    requests = bias_ref.shape[0]
    prompts, prompt_len = prompt_ref.shape
    own_len = lists_ref.shape[1] - 2
    group, length = lists_ref[:, own_len : own_len + 1], lists_ref[:, own_len + 1 :]
    spot = lax.broadcasted_iota(jnp.int32, (requests, rows), 1)
    page = spot // page_len + pl.program_id(0) * pages
    reach = jnp.zeros((requests, rows), jnp.int32)
    for k in range(prompt_len):
        listed = jnp.zeros((requests, 1), jnp.int32)
        for g in range(prompts):
            listed = jnp.where(group == g, prompt_ref[g, k], listed)
        reach = jnp.where(page == listed, length - page_len * k, reach)
    for k in range(own_len):
        reach = jnp.where(page == lists_ref[:, k : k + 1], length - page_len * (prompt_len + k), reach)
    bias_ref[...] = jnp.where(spot % page_len < reach, 0.0, FAR)


def split_pool(prompt_pages, lists, cache_pool, after):
    pages, page_len, _, cols = cache_pool.shape
    requests = lists.shape[0]
    block = next(b for b in (16, 8, 4, 2, 1) if pages % b == 0)
    out = jax.ShapeDtypeStruct((pages * page_len, cols), BF16)
    spec = pl.BlockSpec((block * page_len, cols), lambda b, *_: (b, 0))
    return pl.pallas_call(
        pool_kernel,
        grid_spec=pltpu.PrefetchScalarGridSpec(
            num_scalar_prefetch=1,
            grid=(pages // block,),
            in_specs=[
                full_spec(lists.shape),
                pl.BlockSpec((block, page_len, 2, cols), lambda b, *_: (b, 0, 0, 0)),
                pl.BlockSpec(memory_space=pl.ANY),
            ],
            out_specs=[spec, spec, pl.BlockSpec((requests, block * page_len), lambda b, *_: (0, b))],
        ),
        out_shape=[out, out, jax.ShapeDtypeStruct((requests, pages * page_len), F32)],
        compiler_params=params(),
        cost_estimate=pl.CostEstimate(
            flops=8 * block * page_len * cache_pool.size,
            bytes_accessed=4 * cache_pool.size,
            transcendentals=0,
        ),
        name="pool_split",
    )(prompt_pages, lists, cache_pool, after)


def qkv_kernel(order_ref, recv_ref, norm_ref, w_ref, _, keep_ref, send_ref, raw_ref, normed, slots):
    width = norm_ref.shape[1]
    half, row, _ = keep_ref.shape
    cols = w_ref.shape[2]
    values = recv_ref[:, :width]
    scale = recv_ref[:, width : width + 1].astype(F32)
    for piece in range(1, PIECES):
        scale = scale + recv_ref[:, width + piece : width + piece + 1].astype(F32)
    normed[...] = (values.astype(F32) * scale * norm_ref[...]).astype(BF16)
    for slot in range(2 * half):
        rows = pl.ds(pl.multiple_of(order_ref[slot] * row, row), row)
        slots[slot * row : (slot + 1) * row] = normed[rows]
        raw_ref[slot * row : (slot + 1) * row] = recv_ref[rows, :width]
    for part in range(3):
        here = slice(part * cols, (part + 1) * cols)
        result = dot_nn(slots[...], w_ref[part]).astype(BF16).reshape(2 * half, row, cols)
        keep_ref[:, :, here] = result[:half]
        send_ref[:, :, here] = result[half:]


def project_qkv(order, recv, norm_slice, weights, half, row, after):
    total, _ = recv.shape
    width, cols = weights.shape[1:]
    out = jax.ShapeDtypeStruct((half, row, 3 * cols), BF16)
    raw = jax.ShapeDtypeStruct((total, width), BF16)
    return pl.pallas_call(
        qkv_kernel,
        grid_spec=pltpu.PrefetchScalarGridSpec(
            num_scalar_prefetch=1,
            grid=(1,),
            in_specs=[full_spec(x.shape) for x in (recv, norm_slice, weights)] + [pl.BlockSpec(memory_space=pl.ANY)],
            out_specs=[full_spec(out.shape), full_spec(out.shape), full_spec(raw.shape)],
            scratch_shapes=[pltpu.VMEM((total, width), BF16), pltpu.VMEM((total, width), BF16)],
        ),
        out_shape=[out, out, raw],
        compiler_params=params(room(total)),
        cost_estimate=pl.CostEstimate(
            flops=6 * total * width * cols, bytes_accessed=6 * total * cols + 6 * width * cols, transcendentals=0
        ),
        name="qkv",
    )(order, recv, norm_slice, weights, after)


def attention_kernel(*refs):
    parts, refs = refs[:-9], refs[-9:]
    cos_ref, sin_ref, bias_ref, key_ref, value_ref, _, out_ref, scores, probs = refs
    row, cols = out_ref.shape
    heads = cols // HD
    total = parts[0][0].astype(F32)
    for part in parts[1:]:
        total = total + part[0].astype(F32)
    lane = lax.broadcasted_iota(jnp.int32, (row, cols), 1)
    first_half = lane % HD < HD // 2

    def rotate(values):
        partner = jnp.where(
            first_half, pltpu.roll(values, cols - HD // 2, 1), pltpu.roll(values, HD // 2, 1)
        )
        return (values * cos_ref[...] + partner * sin_ref[...]).astype(BF16)

    query = rotate(total[:, :cols]).astype(F32)
    key_new = rotate(total[:, cols : 2 * cols]).astype(F32)
    value_new = total[:, 2 * cols :].astype(BF16).astype(F32)
    spread = jnp.concatenate(
        [jnp.where(lane // HD == h, query, 0.0).astype(BF16) for h in range(heads)], axis=0
    )
    scores[...] = dot_nt(spread, key_ref[...])
    own_parts = []
    for h in range(heads):
        here = slice(h * row, (h + 1) * row)
        mine = lane // HD == h
        own = jnp.sum(jnp.where(mine, query * key_new, 0.0), axis=1, keepdims=True) * HD**-0.5
        score = scores[here] * HD**-0.5 + bias_ref[...]
        highest = jnp.maximum(jnp.max(score, axis=1, keepdims=True), own)
        weight = jnp.exp(score - highest)
        weight_own = jnp.exp(own - highest)
        inverse = 1.0 / (jnp.sum(weight, axis=1, keepdims=True) + weight_own)
        probs[here] = (weight * inverse).astype(BF16)
        own_parts.append((weight_own * inverse).astype(BF16).astype(F32))
    mixture = dot_nn(probs[...], value_ref[...])
    result = jnp.zeros((row, cols), F32)
    for h in range(heads):
        mixed = mixture[h * row : (h + 1) * row] + own_parts[h] * value_new
        result = jnp.where(lane // HD == h, mixed, result)
    out_ref[...] = result.astype(BF16)


def attend(parts, cosine, sine, bias, keys, values, after):
    row, cols = cosine.shape
    stretch = keys.shape[0]
    heads = cols // HD
    operands = [*parts, cosine, sine, bias, keys, values]
    return pl.pallas_call(
        attention_kernel,
        grid=(1,),
        in_specs=[full_spec(x.shape) for x in operands] + [pl.BlockSpec(memory_space=pl.ANY)],
        out_specs=full_spec((row, cols)),
        out_shape=jax.ShapeDtypeStruct((row, cols), BF16),
        scratch_shapes=[
            pltpu.VMEM((heads * row, stretch), F32),
            pltpu.VMEM((heads * row, stretch), BF16),
        ],
        compiler_params=params(ATTENTION),
        cost_estimate=pl.CostEstimate(
            flops=4 * heads * row * stretch * cols,
            bytes_accessed=4 * stretch * cols,
            transcendentals=heads * row * stretch,
        ),
        name="attention",
    )(*operands, after)


def out_kernel(*refs):
    parts, (other_ref, w_ref, out_ref) = refs[:-3], refs[-3:]
    half = len(parts) * parts[0].shape[0]
    mine = jnp.concatenate([part[...] for part in parts], axis=0)
    out_ref[:, :half] = dot_nt(w_ref[...], mine).astype(BF16)
    out_ref[:, half:] = dot_nt(w_ref[...], other_ref[...]).astype(BF16)


def project_heads(parts, other, weights):
    half = other.shape[0]
    operands = [*parts, other, weights]
    out = (weights.shape[0], 2 * half)
    return pl.pallas_call(
        out_kernel,
        grid=(1,),
        in_specs=[full_spec(x.shape) for x in operands],
        out_specs=full_spec(out),
        out_shape=jax.ShapeDtypeStruct(out, BF16),
        compiler_params=params(room(2 * half)),
        cost_estimate=pl.CostEstimate(
            flops=2 * weights.size * out[1], bytes_accessed=4 * weights.size, transcendentals=0
        ),
        name="out_projection",
    )(*operands)


def pair_block(pairs):
    return next(b for b in (256, 128, 64, 32, 16) if pairs % b == 0)


def dispatch(parts, hid_ref, norm_ref, router_ref, line_ref, resid_ref, spread_ref, aux_ref, aux_at):
    width, total = hid_ref.shape
    pairs = spread_ref.shape[1]
    resid = hid_ref[...].astype(F32)
    for part in parts:
        resid = resid + part[...].astype(F32)
    resid_ref[...] = resid
    moe = (resid * norm_ref[...]).astype(BF16)
    squares = jnp.sum(resid * resid, axis=0, keepdims=True)
    logits = dot_nn(router_ref[...], moe)
    expert = lax.broadcasted_iota(jnp.int32, logits.shape, 0)
    line = line_ref[...].astype(jnp.int32)
    sign = (expert == line[2:3]).astype(F32) - (expert == line[3:4]).astype(F32)
    gap = jnp.sum(logits * sign, axis=0, keepdims=True)
    high = lax.broadcasted_iota(jnp.int32, (LANES, total), 0)
    aux_plain = jnp.zeros((LANES, total), F32)
    aux_signed = jnp.zeros((LANES, total), F32)
    for k, piece in enumerate(split_bf16(squares)):
        aux_plain = jnp.where(high == aux_at + k, piece, aux_plain)
    for k, piece in enumerate(split_bf16(gap)):
        aux_signed = jnp.where(high == aux_at + PIECES + k, piece, aux_signed)
    aux_plain = aux_plain.astype(BF16)
    aux_signed = aux_signed.astype(BF16)
    feature = lax.broadcasted_iota(jnp.int32, (width, 2 * width), 0)
    lane = lax.broadcasted_iota(jnp.int32, (width, 2 * width), 1)
    even = (lane == 2 * feature).astype(BF16)
    odd = (lane == 2 * feature + 1).astype(BF16)
    block = pair_block(pairs)
    for start in range(0, pairs, block):
        here = slice(start, start + block)
        pair = lax.broadcasted_iota(jnp.int32, (block, total), 0) + start
        first = (pair == line[0:1]).astype(F32)
        second = (pair == line[1:2]).astype(F32)
        both = (first + second).astype(BF16)
        rows = dot_nt(both, moe).astype(BF16)
        spread_ref[0, here] = dot_nn(rows, even).astype(BF16)
        spread_ref[1, here] = dot_nn(rows, odd).astype(BF16)
        aux_ref[here] = dot_nt(both, aux_plain) + dot_nt((first - second).astype(BF16), aux_signed)


def windows(pairs, per_expert):
    return min(per_expert + 16, pairs)


def window_of(offset_ref, expert, pairs, window):
    first = offset_ref[expert]
    start = pl.multiple_of(jnp.minimum(first // 16 * 16, pairs - window), 16)
    rows = lax.broadcasted_iota(jnp.int32, (window, 1), 0) + start
    return pl.ds(start, window), (rows >= first) & (rows < offset_ref[expert + 1])


def gate_kernel(count_parts, begin, columns, tail, window, offset_ref, order_ref, *refs):
    first = count_parts > 0
    if first:
        parts, refs = refs[:count_parts], refs[count_parts:]
        hid_ref, norm_ref, router_ref, line_ref, tail_ref, w_ref, _ = refs[:7]
        keep_ref, send_ref, resid_ref, spread_ref, held, aux, w_held, w_sems, tail_held, tail_sem = refs[7:]
    else:
        spread_ref, w_ref, _, keep_ref, send_ref, held, w_held, w_sems = refs
    experts = w_ref.shape[0]
    pairs = spread_ref.shape[1]
    width = spread_ref.shape[2] // 2
    copies = [
        pltpu.make_async_copy(w_ref.at[e, :, :, pl.ds(begin, columns)], w_held.at[e % SLOTS], w_sems.at[e % SLOTS])
        for e in range(experts)
    ]
    for copy in copies[:SLOTS]:
        copy.start()
    if first:
        tail_width, _, aux_at, size = tail
        tail_copy = pltpu.make_async_copy(tail_ref, tail_held, tail_sem)
        tail_copy.start()
        dispatch(parts, hid_ref, norm_ref, router_ref, line_ref, resid_ref, spread_ref, aux, aux_at % LANES)
        tail_copy.wait()

    for expert in range(experts):
        rows, valid = window_of(offset_ref, expert, pairs, window)
        left = jnp.concatenate([spread_ref[0, rows], spread_ref[1, rows]], axis=0)
        copies[expert].wait()
        result = dot_nn(left, w_held[expert % SLOTS].reshape(2 * width, columns)).astype(BF16)
        if expert + SLOTS < experts:
            copies[expert + SLOTS].start()
        held[rows, :columns] = jnp.where(valid, result[:window], held[rows, :columns])
        held[rows, columns : 2 * columns] = jnp.where(
            valid, result[window:], held[rows, columns : 2 * columns]
        )
        if first:
            result = dot_nn(left, tail_held[expert])
            lane = lax.broadcasted_iota(jnp.int32, (window, LANES), 1)
            gate, up = result[:window], result[window:]
            if tail_width == LANES:
                block = jnp.where(lane < size, gate, pltpu.roll(up, size, 1))
                block = jnp.where(lane < 2 * size, block, aux[rows])
            else:
                block = jnp.concatenate([gate, up, aux[rows]], axis=1)
            here = slice(2 * columns, 2 * columns + tail_width)
            held[rows, here] = jnp.where(valid, block.astype(BF16), held[rows, here])

    half, block, _ = keep_ref.shape
    for slot in range(half):
        mine = pl.ds(pl.multiple_of(order_ref[slot] * block, block), block)
        other = pl.ds(pl.multiple_of(order_ref[half + slot] * block, block), block)
        keep_ref[slot] = held[mine]
        send_ref[slot] = held[other]


def gate_tail_kernel(size, gate_ref, _, out_ref):
    experts, width, _, lanes = gate_ref.shape
    lane = lax.broadcasted_iota(jnp.int32, (2 * width, lanes), 1)
    for e in range(experts):
        out_ref[e] = jnp.where(lane < size, gate_ref[e].reshape(2 * width, lanes).astype(F32), 0.0).astype(BF16)


def down_tail_kernel(size, down_ref, _, out_ref):
    lane = lax.broadcasted_iota(jnp.int32, down_ref.shape[1:], 1)
    for e in range(down_ref.shape[0]):
        out_ref[e] = jnp.where(lane < size, down_ref[e].astype(F32), 0.0).astype(BF16)


def last_units(weights, after, kernel, rows, name):
    number, size = weights.shape[-1] // LANES, weights.shape[-1] % LANES
    lead = weights.shape[:-1]
    out = (weights.shape[0], rows, LANES)
    return pl.pallas_call(
        functools.partial(kernel, size),
        grid=(1,),
        in_specs=[
            pl.BlockSpec((*lead, LANES), lambda *_: (0,) * len(lead) + (number,)),
            pl.BlockSpec(memory_space=pl.ANY),
        ],
        out_specs=full_spec(out),
        out_shape=jax.ShapeDtypeStruct(out, BF16),
        compiler_params=params(),
        cost_estimate=pl.CostEstimate(flops=0, bytes_accessed=4 * out[0] * rows * LANES, transcendentals=0),
        name=name,
    )(weights, after)


def tail_layout(units):
    size = units % LANES
    if 2 * size + 2 * PIECES <= LANES:
        return LANES, size, 2 * size, size
    return 3 * LANES, LANES, 2 * LANES, size


def sum_kernel(aux_at, groups, keep_ref, recv_ref, _, *outs):
    outs = outs[-len(groups) :]
    width = keep_ref.shape[2]

    def added(slot):
        total = keep_ref[slot].astype(F32) + recv_ref[slot].astype(F32)
        if aux_at is None:
            return [(slice(0, width), total)]
        base = aux_at // LANES * LANES
        tile = total[:, base : base + LANES]
        lane = lax.broadcasted_iota(jnp.int32, tile.shape, 1)
        for start in (aux_at - base, aux_at - base + PIECES):
            value = tile[:, start : start + 1]
            for k in range(1, PIECES):
                value = value + tile[:, start + k : start + k + 1]
            for k, piece in enumerate(split_bf16(value)):
                tile = jnp.where(lane == start + k, piece, tile)
        spans = [(slice(base, base + LANES), tile)]
        if base:
            spans.append((slice(0, base), total[:, :base]))
        if base + LANES < width:
            spans.append((slice(base + LANES, width), total[:, base + LANES :]))
        return spans

    for group, out in zip(groups, outs):
        for k, slot in enumerate(group):
            for span, value in added(slot):
                out[k, :, span] = value.astype(BF16)


def sum_parts(keep, recv, groups, aux_at, name, after=None, hold=None):
    _, block, width = keep.shape
    outs = [jax.ShapeDtypeStruct((len(group), block, width), BF16) for group in groups]
    in_specs = [full_spec(keep.shape)] * 2 + [pl.BlockSpec(memory_space=pl.ANY)]
    out_specs = [full_spec(out.shape) for out in outs]
    operands = [keep, recv, keep if after is None else after]
    aliases = {}
    if hold is not None:
        operands.append(hold)
        in_specs.append(pl.BlockSpec(memory_space=pl.ANY))
        outs.insert(0, jax.ShapeDtypeStruct(hold.shape, hold.dtype))
        out_specs.insert(0, pl.BlockSpec(memory_space=pl.ANY))
        aliases = {3: 0}
    return pl.pallas_call(
        functools.partial(sum_kernel, aux_at, groups),
        grid=(1,),
        in_specs=in_specs,
        out_specs=out_specs,
        out_shape=outs,
        input_output_aliases=aliases,
        compiler_params=params(),
        cost_estimate=pl.CostEstimate(flops=keep.size, bytes_accessed=6 * keep.size, transcendentals=0),
        name=name,
    )(*operands)


def halves(count):
    return [list(range(0, count, 2)), list(range(1, count, 2))] if count > 1 else [[0]]


def act_kernel(count_parts, columns, tail, features, *refs):
    parts, refs = refs[:count_parts], refs[count_parts:]
    total = parts[0][0].astype(F32)
    for part in parts[1:]:
        total = total + part[0].astype(F32)
    if tail is None:
        stat_ref, _, act_ref = refs
        inverse, weight = stat_ref[:, 0:1], stat_ref[:, 1:2]
    else:
        _, act_ref, stat_ref = refs
        tail_width, up_at, aux_at, size = tail
        base = 2 * columns + aux_at
        squares = total[:, base : base + 1]
        gap = total[:, base + PIECES : base + PIECES + 1]
        for k in range(1, PIECES):
            squares = squares + total[:, base + k : base + k + 1]
            gap = gap + total[:, base + PIECES + k : base + PIECES + k + 1]
        inverse = lax.rsqrt(squares / features + 1e-06)
        weight = 1.0 / (1.0 + jnp.exp(-gap * inverse))
        lane = lax.broadcasted_iota(jnp.int32, (total.shape[0], LANES), 1)
        stat_ref[...] = jnp.where(lane == 0, inverse, weight)

    def activate(gate, up):
        gate = gate * inverse
        return gate / (1.0 + jnp.exp(-gate)) * (up * inverse) * weight

    act_ref[:, :columns] = activate(total[:, :columns], total[:, columns : 2 * columns]).astype(BF16)
    if tail is not None:
        block = total[:, 2 * columns : 2 * columns + LANES]
        if tail_width == LANES:
            up = pltpu.roll(block, LANES - size, 1)
        else:
            up = total[:, 2 * columns + LANES : 2 * columns + 2 * LANES]
        last = jnp.where(lane < size, activate(block, up), 0.0)
        act_ref[:, columns:] = last.astype(BF16)


def activation(parts, stats, columns, tail, features, name, after):
    rows = parts[0].shape[1]
    out = jax.ShapeDtypeStruct((rows, columns + (LANES if tail else 0)), BF16)
    stat = jax.ShapeDtypeStruct((rows, LANES), F32)
    operands = [*parts] + ([] if tail else [stats])
    outs = [out, stat] if tail else [out]
    in_specs = [full_spec(x.shape) for x in operands] + [pl.BlockSpec(memory_space=pl.ANY)]
    result = pl.pallas_call(
        functools.partial(act_kernel, len(parts), columns, tail, features),
        grid=(1,),
        in_specs=in_specs,
        out_specs=[full_spec(x.shape) for x in outs],
        out_shape=outs,
        compiler_params=params(),
        cost_estimate=pl.CostEstimate(
            flops=16 * rows * columns, bytes_accessed=20 * rows * columns, transcendentals=rows * columns
        ),
        name=name,
    )(*operands, after)
    return (result[0], result[1]) if tail else (result[0], stats)


def down_kernel(count_parts, begin, columns, tail, window, begins, ends, offset_ref, order_ref, *refs):
    parts, refs = refs[:count_parts], refs[count_parts:]
    other_ref, w_ref, _, refs = refs[0], refs[1], refs[2], refs[3:]
    if tail:
        tail_ref, refs = refs[0], refs[1:]
    if not begins:
        before_ref, refs = refs[0], refs[1:]
    if ends:
        place_ref, resid_ref, out_ref, total_ref, held, w_held, w_sems = refs
    else:
        total_ref, held, w_held, w_sems = refs
    block = parts[0].shape[0]
    half = len(parts)
    pairs = held.shape[0]
    experts = w_ref.shape[0]
    copies = [
        pltpu.make_async_copy(w_ref.at[e, :, pl.ds(begin, columns)], w_held.at[e % SLOTS], w_sems.at[e % SLOTS])
        for e in range(experts)
    ]
    for copy in copies[:SLOTS]:
        copy.start()
    for slot in range(half):
        mine = pl.ds(pl.multiple_of(order_ref[slot] * block, block), block)
        other = pl.ds(pl.multiple_of(order_ref[half + slot] * block, block), block)
        held[mine] = parts[slot][...]
        held[other] = other_ref[slot]
    total_ref[...] = jnp.zeros_like(total_ref) if begins else before_ref[...]
    for expert in range(experts):
        rows, valid = window_of(offset_ref, expert, pairs, window)
        copies[expert].wait()
        result = dot_nt(held[rows, :columns], w_held[expert % SLOTS])
        if expert + SLOTS < experts:
            copies[expert + SLOTS].start()
        if tail:
            result = result + dot_nt(held[rows, columns:], tail_ref[expert])
        total_ref[rows] = total_ref[rows] + jnp.where(valid, result, 0.0)

    if ends:
        total = out_ref.shape[0]
        pieces = [x.astype(BF16) for x in split_bf16(total_ref[...], 2)]
        resid = [x.astype(BF16) for x in split_bf16(resid_ref[...], 2)]
        step = pair_block(total) if total > 256 else total
        step = min(step, 256)
        for start in range(0, total, step):
            here = slice(start, start + step)
            pair = lax.broadcasted_iota(jnp.int32, (step, pairs), 1)
            place = place_ref[here].astype(jnp.int32)
            pick = (pair == place[:, 0:1]) | (pair == place[:, 1:2])
            pick = pick.astype(F32).astype(BF16)
            token = lax.broadcasted_iota(jnp.int32, (step, total), 1)
            move = (token == place[:, 2:3]).astype(F32).astype(BF16)
            result = dot_nn(pick, pieces[0]) + dot_nn(pick, pieces[1])
            result = result + dot_nt(move, resid[0]) + dot_nt(move, resid[1])
            out_ref[here] = result.astype(BF16)


def chunk_columns(units):
    full = units // LANES
    count = 3 if full >= 6 else 1
    ends = [full * (k + 1) // count for k in range(count)]
    return [(LANES * (e - n), LANES * n) for e, n in zip(ends, [b - a for a, b in zip([0, *ends], ends)])]


def local(
    hidden_in,
    cache_pool,
    project_in,
    project_out,
    norm_first,
    norm_second,
    router,
    gate_up,
    expert_down,
    lengths,
    prompt_pages,
    own_pages,
    groups,
    move_target,
    routes,
):
    dp = lax.axis_size("dp")
    fs = lax.axis_size("fsdp")
    half = dp // 2
    my_row = lax.axis_index("dp")
    my_column = lax.axis_index("fsdp")
    my_chip, my_core = my_row // 2, my_row % 2
    req, features = hidden_in.shape
    row = req * fs
    total = row * dp
    pairs = 2 * total
    width = project_in.shape[0]
    cols = cache_pool.shape[3]
    heads = cols // HD
    page_len = cache_pool.shape[1]
    movers = move_target.shape[1]
    staying = row - movers
    experts = router.shape[1]
    units = gate_up.shape[3]
    window = windows(pairs, CAP * dp * fs)

    gate_up = pltpu.with_memory_space_constraint(gate_up, pltpu.HBM)
    expert_down = pltpu.with_memory_space_constraint(expert_down, pltpu.HBM)

    chip = jnp.arange(half, dtype=jnp.int32)
    row_ids = jnp.arange(dp, dtype=jnp.int32)
    order = jnp.concatenate([(chip ^ my_chip) * 2 + my_core, (chip ^ my_chip) * 2 + 1 - my_core])

    def swap(x):
        return lax.ppermute(x, "dp", [(i, i ^ 1) for i in range(dp)])

    def over_chips(x, s):
        return lax.ppermute(x, "dp", [(i, i ^ (2 * s)) for i in range(dp)])

    def over_columns(x, s):
        return lax.ppermute(x, "fsdp", [(i, i ^ s) for i in range(fs)])

    payload = pack(hidden_in, routes.T, dp, fs)
    recv = lax.all_to_all(
        payload.reshape(dp * fs, req, payload.shape[3]), ("dp", "fsdp"), 0, 0, tiled=True
    ).reshape(total, payload.shape[3])

    row_lengths = lax.dynamic_slice_in_dim(lengths, my_row * row, row)
    lists = jnp.concatenate([own_pages, groups[:, None], row_lengths[:, None]], axis=1)
    lane = jnp.arange(cols, dtype=jnp.int32)
    channel = (lane % (HD // 2)).astype(F32)
    inverse = jnp.exp(-jnp.log(10000.0) * 2.0 * channel / HD)
    angles = row_lengths.astype(F32)[:, None] * inverse[None, :]
    cosine = jnp.cos(angles)
    sine = jnp.where((lane % HD < HD // 2)[None, :], -1.0, 1.0) * jnp.sin(angles)

    def slice_of(vector):
        return lax.dynamic_slice_in_dim(vector, my_row * width, width)

    keys, values, bias = split_pool(prompt_pages, lists, cache_pool, payload)
    keep, send, raw = project_qkv(
        order,
        recv,
        slice_of(norm_first).astype(F32)[None, :],
        project_in.transpose(1, 0, 2),
        half,
        row,
        bias,
    )
    sums = sum_parts(keep, swap(send), [[s] for s in range(half)], None, "core_sum_qkv")
    slot_of = (row_ids % 2 ^ my_core) * half + (row_ids // 2 ^ my_chip)
    column = jnp.stack([my_column, jnp.int32(fs)]).astype(jnp.int32)
    offsets, place_table, line_table = pair_places(
        move_target, order, slot_of, column, recv, sums[0], experts, width
    )
    gate_tail = last_units(gate_up, place_table, gate_tail_kernel, 2 * width, "gate_tail")
    parts = [sums[0]] + [over_chips(sums[s], s) for s in range(1, half)]
    heads_out = attend(parts, cosine, sine, bias, keys, values, gate_tail)

    parts = [heads_out] + [over_chips(heads_out, s) for s in range(1, half)]
    other = swap(jnp.concatenate(parts, axis=0))
    projected = project_heads(parts, other, project_out.T)
    parts = [projected] + [over_columns(projected, s) for s in range(1, fs)]

    chunks = chunk_columns(units)
    tail = tail_layout(units)
    block = pairs // dp
    hbm = pl.BlockSpec(memory_space=pltpu.HBM)
    anywhere = pl.BlockSpec(memory_space=pl.ANY)
    spread = jax.ShapeDtypeStruct((2, pairs, 2 * width), BF16)
    resid_shape = jax.ShapeDtypeStruct((width, total), F32)
    norm_column = slice_of(norm_second).astype(F32)[:, None]
    router_slice = lax.dynamic_slice_in_dim(router, my_row * width, width).T
    state = {"after": line_table}

    def gate(index):
        begin, columns = chunks[index]
        first = index == 0
        out_width = 2 * columns + (tail[0] if first else 0)
        half_out = jax.ShapeDtypeStruct((half, block, out_width), BF16)
        scratch = [pltpu.VMEM((pairs, out_width), BF16)]
        weights = [pltpu.VMEM((SLOTS, width, 2, columns), BF16), pltpu.SemaphoreType.DMA((SLOTS,))]
        if first:
            operands = [*parts, raw.T, norm_column, router_slice, line_table]
            in_specs = [full_spec(x.shape) for x in operands] + [hbm]
            operands.append(gate_tail)
            outs = [half_out, half_out, resid_shape, spread]
            scratch += [pltpu.VMEM((pairs, LANES), F32), *weights]
            scratch += [pltpu.VMEM(gate_tail.shape, BF16), pltpu.SemaphoreType.DMA]
        else:
            operands = [state["spread"]]
            in_specs = [full_spec(spread.shape)]
            outs = [half_out, half_out]
            scratch += weights
        result = pl.pallas_call(
            functools.partial(gate_kernel, len(parts) if first else 0, begin, columns, tail, window),
            grid_spec=pltpu.PrefetchScalarGridSpec(
                num_scalar_prefetch=2,
                grid=(1,),
                in_specs=[*in_specs, anywhere, anywhere],
                out_specs=[full_spec(x.shape) for x in outs],
                scratch_shapes=scratch,
            ),
            out_shape=outs,
            compiler_params=params(room(total)),
            cost_estimate=pl.CostEstimate(
                flops=8 * experts * window * width * columns,
                bytes_accessed=4 * experts * width * columns,
                transcendentals=0,
            ),
            name=f"gate_up_{index}",
        )(offsets, order, *operands, gate_up, state["after"])
        if first:
            state["resid"], state["spread"] = result[2:]
        state["after"] = result[0]
        return result[:2]

    def combine(index, bit, held, hold=None):
        aux_at = 2 * chunks[index][1] + tail[2] if index == 0 else None
        sums = sum_parts(
            *held, halves(held[0].shape[0]), aux_at, f"sum_{index}_{bit}", state["after"], hold
        )
        kept, sent = sums[-2:]
        state["after"] = kept
        return [kept, over_chips(sent, 1 << bit)], sums[0]

    def activate(index, held):
        act, state["stats"] = activation(
            held,
            state.get("stats"),
            chunks[index][1],
            tail if index == 0 else None,
            float(features),
            f"activation_{index}",
            state["after"],
        )
        state["after"] = act
        parts = {0: act}
        for bit in reversed(range(stages)):
            parts.update({s | 1 << bit: over_chips(x, 1 << bit) for s, x in list(parts.items())})
        return [parts[s] for s in range(half)]

    def down(index, parts):
        begin, columns = chunks[index]
        first, last = index == 0, index == len(chunks) - 1
        operands = [*parts, swap(jnp.stack(parts))]
        in_specs = [full_spec(x.shape) for x in operands] + [anywhere, anywhere]
        operands += [expert_down, state["after"]]
        if first:
            operands.append(state["tail"])
            in_specs.append(full_spec(state["tail"].shape))
        else:
            operands.append(state["sum"])
            in_specs.append(full_spec(state["sum"].shape))
        sum_shape = jax.ShapeDtypeStruct((pairs, width), F32)
        scratch = [
            pltpu.VMEM((pairs, parts[0].shape[1]), BF16),
            pltpu.VMEM((SLOTS, width, columns), BF16),
            pltpu.SemaphoreType.DMA((SLOTS,)),
        ]
        outs = [sum_shape]
        if last:
            operands += [place_table, state["resid"]]
            in_specs += [full_spec(place_table.shape), full_spec(state["resid"].shape)]
            outs = [jax.ShapeDtypeStruct((total, width), BF16)]
            scratch = [pltpu.VMEM(sum_shape.shape, F32)] + scratch
        result = pl.pallas_call(
            functools.partial(
                down_kernel, len(parts), begin, columns, tail if first else None, window, first, last
            ),
            grid_spec=pltpu.PrefetchScalarGridSpec(
                num_scalar_prefetch=2,
                grid=(1,),
                in_specs=in_specs,
                out_specs=[full_spec(x.shape) for x in outs],
                scratch_shapes=scratch,
            ),
            out_shape=outs,
            compiler_params=params(room(total)),
            cost_estimate=pl.CostEstimate(
                flops=2 * experts * window * width * columns,
                bytes_accessed=2 * experts * width * columns,
                transcendentals=0,
            ),
            name=f"down_{index}",
        )(offsets, order, *operands)[0]
        state["sum"] = state["after"] = result
        return result

    stages = half.bit_length() - 1
    count = len(chunks)
    held, gathered = {}, {}
    for step in range(count + stages + 3):
        sent = None
        if step < count:
            kept, sent = gate(step)
        if step == count - 1:
            state["tail"] = last_units(expert_down, state["after"], down_tail_kernel, width, "down_tail")
        for k in range(count):
            if step - k == stages + 2:
                result = down(k, gathered[k])
        for k in range(count):
            if step >= count and step - k == stages:
                gathered[k] = activate(k, held[k])
        for k in range(count):
            if 1 <= step - k < stages:
                held[k], through = combine(k, step - k, held[k], sent)
                sent = None if sent is None else through
        if step < count:
            held[step], _ = combine(step, 0, [kept, swap(sent)])
        for k in range(count):
            if step < count and step - k == stages:
                gathered[k] = activate(k, held[k])

    back = lax.all_to_all(result.reshape(dp * fs, req, width), ("dp", "fsdp"), 0, 0, tiled=True)
    back = back.reshape(dp, fs, req, width).astype(F32)
    return jnp.sum(back, axis=1).transpose(1, 0, 2).reshape(req, features).astype(BF16)


def solution(mesh):
    placed = (
        P(("dp", "fsdp"), None),
        P("dp", None, None, "fsdp"),
        P("dp", None, "fsdp"),
        P("fsdp", "dp"),
        P(),
        P(),
        P(),
        P(None, "dp", None, "fsdp"),
        P(None, "dp", "fsdp"),
        P(),
        P("dp", None),
        P("dp", None),
        P("dp"),
        P(),
        P(("dp", "fsdp"), None),
    )
    return jax.shard_map(
        local, mesh=mesh, in_specs=placed, out_specs=P(("dp", "fsdp"), None), check_vma=False
    )
```

time: 194 us -> 162 us (0.84)
  starting transfers between devices: 50.8 us -> 33.4 us
  local copies, waits for them, and re-layouts: 23.8 us -> 8.57 us
  other arithmetic: 15.4 us -> 3.62 us
  waiting for transfers between devices: 45.7 us -> 54.9 us
  Pallas kernels: 44.2 us -> 47.5 us
    ppermute x24 -> x21, starting transfers between devices: 38.3 us -> 21.7 us  [over_chips(): return lax.ppermute(x, 'dp', [(i, i ^ 2 * s) for i in range(dp)])]
    unnamed x32 -> x25, local copies, waits for them, and re-layouts: 18.7 us -> 7.44 us
    ppermute x24 -> x21, waiting for transfers between devices: 35.6 us -> 41.8 us  [over_chips(): return lax.ppermute(x, 'dp', [(i, i ^ 2 * s) for i in range(dp)])]
    ppermute x8, waiting for transfers between devices: 3.01 us -> 7.7 us  [swap(): return lax.ppermute(x, 'dp', [(i, i ^ 1) for i in range(dp)])]
    convert_element_type x7 -> x0, other arithmetic: 4.63 us -> none  [the longest x1 1.82 us: local(): (keep[s].astype(F32) + other[s].astype(F32)).astype(BF16)]
    pallas_call x10 -> x18, Pallas kernels: 39.2 us -> 43.2 us  [the longest x3 17.6 us: gate(): pl.pallas_call(functools.partial(gate_kernel, len(parts) if first else 0,...]
    reduce_sum x8 -> x0, other arithmetic: 3.8 us -> none  [the longest x1 0.91 us: local(): factor = lax.rsqrt(jnp.mean(wide * wide, axis=1, keepdims=True) + 1e-06)]
  transfers between devices with their start and end apart: 36 -> 33, of which waited for: 12 -> 22; matrix products, arithmetic and copies ran while one was open for 7% -> 3% of each run, Pallas kernels for 14% -> 18%
where the time goes in v2:
time: 162 us
  waiting for transfers between devices  54.9 us (34%)
  Pallas kernels  47.5 us (29%)
  starting transfers between devices  33.4 us (21%)
  blocking collectives  13.4 us (8%)
  local copies, waits for them, and re-layouts  8.57 us (5%)
  other arithmetic  3.62 us (2%)
    ppermute x21, waiting for transfers between devices, over_chips(): return lax.ppermute(x, 'dp', [(i, i ^ 2 * s) for i in range(dp)])  41.8 us
    ppermute x21, starting transfers between devices, over_chips(): return lax.ppermute(x, 'dp', [(i, i ^ 2 * s) for i in range(dp)])  21.7 us
    pallas_call x3, Pallas kernels, gate(): pl.pallas_call(functools.partial(gate_kernel, len(parts) if first else 0,...  17.6 us
    all_to_all x1, blocking collectives, local(): lax.all_to_all(result.reshape(dp * fs, req, width), ('dp', 'fsdp'), 0, 0,...  13.4 us
    pallas_call x3, Pallas kernels, down(): pl.pallas_call(functools.partial(down_kernel, len(parts), begin, columns,...  13.3 us
    ppermute x8, waiting for transfers between devices, swap(): return lax.ppermute(x, 'dp', [(i, i ^ 1) for i in range(dp)])  7.7 us
    unnamed x25, local copies, waits for them, and re-layouts  7.44 us
    all_to_all x1, starting transfers between devices, local(): lax.all_to_all(payload.reshape(dp * fs, req, payload.shape[3]), ('dp', 'f...  7.3 us
  transfers between devices with their start and end apart: 33, of which 22 were waited for; matrix products, arithmetic and copies ran while one was open for 3% of the time, Pallas kernels for 18%

profile of v2, /device:TPU:0, one launch (start us, length us, event | category | flops | bytes accessed | tf_op | source)
XLA Modules:
  0.0 161.8 jit_solution(4377308342904674983)
XLA Ops:
  2.3 7.3 %all-to-all-start = ((bf16[32,8,384]{2,1,0:T(8,128)(2,1)}), bf16[32,8,384]{2,1,0:T(8,128)(2,1)S(1)}, u32[]{:S(2)}, u32[]{:S(2)}) async-start(bf16[32,8,384]{2,1,0:T(8,128)(2,1)} %bitcast.2), calls=%async_computation | async-start | bytes 393216 | tf_op jit(solution)/shard_map/all_to_all | solution.py:764
  12.0 2.3 %copy-done.9 = bf16[144,16,2,512]{3,2,1,0:T(2,128)(2,1)S(1)} copy-done((bf16[144,16,2,512]{3,2,1,0:T(2,128)(2,1)S(1)}, bf16[144,16,2,512]{3,2,1,0:T(2,128)(2,1)}, u32[]{:S(2)}) %copy-start.9) | copy-done | bytes 4718616
  15.0 4.7 %pool_split.1 = (bf16[2304,512]{1,0:T(8,128)(2,1)S(1)}, bf16[2304,512]{1,0:T(8,128)(2,1)S(1)}, f32[32,2304]{1,0:T(8,128)S(1)}) custom-call(s32[4,4]{1,0:T(4,128)S(1)} %copy-done.10, s32[32,6]{1,0:T(8,128)S(1)} %copy.33.lists_ref, bf16[144,16,2,512]{3,2,1,0:T(2,128)(2,1)S(1)} %copy-done.9, bf16[8,4,8,384]{3,2,1,0:T(8,128)(2,1)} %pack.1._), custom_call_target="tpu_custom_call" | custom-call | flops 4831838208 | bytes 9437184 | tf_op jit(solution)/shard_map/pool_split/pallas_call | solution.py:218
  27.6 2.4 %collective-permute-start.2 = (bf16[1,32,1536]{2,1,0:T(8,128)(2,1)S(1)}, bf16[1,32,1536]{2,1,0:T(8,128)(2,1)S(1)}, u32[]{:S(2)}, u32[]{:S(2)}) collective-permute-start(bf16[1,32,1536]{2,1,0:T(8,128)(2,1)S(1)} %get-tuple-element.48), channel_id=1, source_target_pairs={{0,16},{4,20},{8,24},{12,28},{16,0},{20,4},{24,8},{28,12},{1,17},{... | collective-permute-start | bytes 294920 | tf_op jit(solution)/shard_map/ppermute | solution.py:758
  34.5 3.8 %collective-permute-done.2.refs_2_ = bf16[1,32,1536]{2,1,0:T(8,128)(2,1)S(1)} collective-permute-done((bf16[1,32,1536]{2,1,0:T(8,128)(2,1)S(1)}, bf16[1,32,1536]{2,1,0:T(8,128)(2,1)S(1)}, u32[]{:S(2)}, u32[]{:S(2)}) %collective-permute-start.2) | collective-permute-done | bytes 98336 | tf_op jit(solution)/shard_map/ppermute | solution.py:758
  44.9 2.4 %collective-permute-done.5.refs_2_ = bf16[32,512]{1,0:T(8,128)(2,1)S(1)} collective-permute-done((bf16[32,512]{1,0:T(8,128)(2,1)S(1)}, bf16[32,512]{1,0:T(8,128)(2,1)S(1)}, u32[]{:S(2)}, u32[]{:S(2)}) %collective-permute-start.5) | collective-permute-done | bytes 32800 | tf_op jit(solution)/shard_map/ppermute | solution.py:758
  51.0 2.5 %collective-permute-start.10 = (bf16[288,256]{1,0:T(8,128)(2,1)S(1)}, bf16[288,256]{1,0:T(8,128)(2,1)S(1)}, u32[]{:S(2)}, u32[]{:S(2)}) collective-permute-start(bf16[288,256]{1,0:T(8,128)(2,1)S(1)} %out_projection.1.refs_0_), channel_id=1, source_target_pairs={{0,3},{1,2},{2,1},{3,0},{4,7},{5,6},{6,5},{7,4},{8,11},{9,10},{10,... | collective-permute-start | bytes 442376 | tf_op jit(solution)/shard_map/ppermute | solution.py:761
  55.6 3.0 %collective-permute-done.10.refs_3_ = bf16[288,256]{1,0:T(8,128)(2,1)S(1)} collective-permute-done((bf16[288,256]{1,0:T(8,128)(2,1)S(1)}, bf16[288,256]{1,0:T(8,128)(2,1)S(1)}, u32[]{:S(2)}, u32[]{:S(2)}) %collective-permute-start.10) | collective-permute-done | bytes 147488 | tf_op jit(solution)/shard_map/ppermute | solution.py:761
  58.6 2.4 %collective-permute-done.8.refs_1_ = bf16[288,256]{1,0:T(8,128)(2,1)S(1)} collective-permute-done((bf16[288,256]{1,0:T(8,128)(2,1)S(1)}, bf16[288,256]{1,0:T(8,128)(2,1)S(1)}, u32[]{:S(2)}, u32[]{:S(2)}) %collective-permute-start.8) | collective-permute-done | bytes 147488 | tf_op jit(solution)/shard_map/ppermute | solution.py:761
  61.0 7.3 %gate_up_0.1 = (bf16[4,64,896]{2,1,0:T(8,128)(2,1)S(1)}, bf16[4,64,896]{2,1,0:T(8,128)(2,1)S(1)}, f32[288,256]{1,0:T(8,128)S(1)}, bf16[2,512,576]{2,1,0:T(8,128)(2,1)S(1)}) custom-call(s32[9]{0:T(128)S(1)} %get-tuple-element.46.offset_ref, s32[8]{0:T(128)S(1)} %pad_add_fusion.1.order_ref, bf16[288,256]{1,0:T(8,128)(2,1)S(1)} %out_projection.1.refs_0_, ...), custom_call_target="tpu_custom_call" | custom-call | flops 1019215872 | bytes 3538944 | tf_op jit(solution)/shard_map/gate_up_0/pallas_call | solution.py:835
  71.0 5.2 %gate_up_1.1 = (bf16[4,64,1024]{2,1,0:T(8,128)(2,1)S(1)}, bf16[4,64,1024]{2,1,0:T(8,128)(2,1)S(1)}) custom-call(s32[9]{0:T(128)S(1)} %get-tuple-element.46.offset_ref, s32[8]{0:T(128)S(1)} %pad_add_fusion.1.order_ref, bf16[2,512,576]{2,1,0:T(8,128)(2,1)S(1)} %get-tuple-element.55.refs_0_, bf16[8,288,2,1440]{3,2,1,0:T(2,128)(2,1)} %refs_1_.3, ...), custom_call_target="tpu_custom_call" | custom-call | flops 1358954496 | bytes 4718592 | tf_op jit(solution)/shard_map/gate_up_1/pallas_call | solution.py:835
  76.1 2.5 %collective-permute-done.12.recv_ref = bf16[2,64,896]{2,1,0:T(8,128)(2,1)S(1)} collective-permute-done((bf16[2,64,896]{2,1,0:T(8,128)(2,1)S(1)}, bf16[2,64,896]{2,1,0:T(8,128)(2,1)S(1)}, u32[]{:S(2)}, u32[]{:S(2)}) %collective-permute-start.12) | collective-permute-done | bytes 229408 | tf_op jit(solution)/shard_map/ppermute | solution.py:758
  81.4 5.2 %gate_up_2.1 = (bf16[4,64,1024]{2,1,0:T(8,128)(2,1)S(1)}, bf16[4,64,1024]{2,1,0:T(8,128)(2,1)S(1)}) custom-call(s32[9]{0:T(128)S(1)} %get-tuple-element.46.offset_ref, s32[8]{0:T(128)S(1)} %pad_add_fusion.1.order_ref, bf16[2,512,576]{2,1,0:T(8,128)(2,1)S(1)} %get-tuple-element.55.refs_0_, bf16[8,288,2,1440]{3,2,1,0:T(2,128)(2,1)} %refs_1_.3, ...), custom_call_target="tpu_custom_call" | custom-call | flops 1358954496 | bytes 4718592 | tf_op jit(solution)/shard_map/gate_up_2/pallas_call | solution.py:835
  86.6 2.9 %collective-permute-done.14.recv_ref = bf16[2,64,1024]{2,1,0:T(8,128)(2,1)S(1)} collective-permute-done((bf16[2,64,1024]{2,1,0:T(8,128)(2,1)S(1)}, bf16[2,64,1024]{2,1,0:T(8,128)(2,1)S(1)}, u32[]{:S(2)}, u32[]{:S(2)}) %collective-permute-start.14) | collective-permute-done | bytes 262176 | tf_op jit(solution)/shard_map/ppermute | solution.py:758
  91.7 6.6 %collective-permute-done.18.refs_1_ = bf16[1,64,896]{2,1,0:T(8,128)(2,1)S(1)} collective-permute-done((bf16[1,64,896]{2,1,0:T(8,128)(2,1)S(1)}, bf16[1,64,896]{2,1,0:T(8,128)(2,1)S(1)}, u32[]{:S(2)}, u32[]{:S(2)}) %collective-permute-start.18) | collective-permute-done | bytes 114720 | tf_op jit(solution)/shard_map/ppermute | solution.py:758
  100.6 3.3 %collective-permute-done.21.refs_2_ = bf16[64,512]{1,0:T(8,128)(2,1)S(1)} collective-permute-done((bf16[64,512]{1,0:T(8,128)(2,1)S(1)}, bf16[64,512]{1,0:T(8,128)(2,1)S(1)}, u32[]{:S(2)}, u32[]{:S(2)}) %collective-permute-start.21) | collective-permute-done | bytes 65568 | tf_op jit(solution)/shard_map/ppermute | solution.py:758
  105.9 3.0 %collective-permute-done.22.refs_3_ = bf16[64,512]{1,0:T(8,128)(2,1)S(1)} collective-permute-done((bf16[64,512]{1,0:T(8,128)(2,1)S(1)}, bf16[64,512]{1,0:T(8,128)(2,1)S(1)}, u32[]{:S(2)}, u32[]{:S(2)}) %collective-permute-start.22) | collective-permute-done | bytes 65568 | tf_op jit(solution)/shard_map/ppermute | solution.py:758
  109.5 9.1 %collective-permute-done.17.refs_1_ = bf16[1,64,1024]{2,1,0:T(8,128)(2,1)S(1)} collective-permute-done((bf16[1,64,1024]{2,1,0:T(8,128)(2,1)S(1)}, bf16[1,64,1024]{2,1,0:T(8,128)(2,1)S(1)}, u32[]{:S(2)}, u32[]{:S(2)}) %collective-permute-start.17) | collective-permute-done | bytes 131104 | tf_op jit(solution)/shard_map/ppermute | solution.py:758
  118.8 2.9 %collective-permute-start.29 = (bf16[64,512]{1,0:T(8,128)(2,1)S(1)}, bf16[64,512]{1,0:T(8,128)(2,1)S(1)}, u32[]{:S(2)}, u32[]{:S(2)}) collective-permute-start(bf16[64,512]{1,0:T(8,128)(2,1)S(1)} %activation_1.1._.refs_0_), channel_id=1, source_target_pairs={{0,16},{4,20},{8,24},{12,28},{16,0},{20,4},{24,8},{28,12},{1,17},{... | collective-permute-start | bytes 196616 | tf_op jit(solution)/shard_map/ppermute | solution.py:758
  122.9 4.8 %down_0.1.refs_3_.refs_7_ = f32[512,288]{1,0:T(8,128)S(1)} custom-call(s32[9]{0:T(128)S(1)} %get-tuple-element.46.offset_ref, s32[8]{0:T(128)S(1)} %pad_add_fusion.1.order_ref, bf16[64,512]{1,0:T(8,128)(2,1)S(1)} %get-tuple-element.75.refs_3_.refs_0_, bf16[64,512]{1,0:T(8,128)(2,1)S(1)} %collective-permute-done.20.refs_1_, ...), custom_call_target="tpu_custom_call" | custom-call | flops 254803968 | bytes 1769472 | tf_op jit(solution)/shard_map/down_0/pallas_call | solution.py:907
  128.8 2.4 %collective-permute-start.28 = (bf16[64,512]{1,0:T(8,128)(2,1)S(1)}, bf16[64,512]{1,0:T(8,128)(2,1)S(1)}, u32[]{:S(2)}, u32[]{:S(2)}) collective-permute-start(bf16[64,512]{1,0:T(8,128)(2,1)S(1)} %activation_1.1._.refs_0_), channel_id=1, source_target_pairs={{0,8},{4,12},{8,0},{12,4},{16,24},{20,28},{24,16},{28,20},{1,9},{5... | collective-permute-start | bytes 196616 | tf_op jit(solution)/shard_map/ppermute | solution.py:758
  139.1 3.9 %down_1.1.refs_6_.refs_7_ = f32[512,288]{1,0:T(8,128)S(1)} custom-call(s32[9]{0:T(128)S(1)} %get-tuple-element.46.offset_ref, s32[8]{0:T(128)S(1)} %pad_add_fusion.1.order_ref, bf16[64,512]{1,0:T(8,128)(2,1)S(1)} %activation_1.1._.refs_0_, bf16[64,512]{1,0:T(8,128)(2,1)S(1)} %collective-permute-done.28.refs_1_, ...), custom_call_target="tpu_custom_call" | custom-call | flops 339738624 | bytes 2359296 | tf_op jit(solution)/shard_map/down_1/pallas_call | solution.py:907
  143.0 4.5 %down_2.1 = bf16[256,288]{1,0:T(8,128)(2,1)S(1)} custom-call(s32[9]{0:T(128)S(1)} %get-tuple-element.46.offset_ref, s32[8]{0:T(128)S(1)} %pad_add_fusion.1.order_ref, bf16[64,512]{1,0:T(8,128)(2,1)S(1)} %activation_2.1.refs_6_.refs_0_, bf16[64,512]{1,0:T(8,128)(2,1)S(1)} %collective-permute-done.24.refs_1_, ...), custom_call_target="tpu_custom_call" | custom-call | flops 339738624 | bytes 2359296 | tf_op jit(solution)/shard_map/down_2/pallas_call | solution.py:907
  147.6 13.4 %all_to_all.10 = bf16[32,8,288]{2,1,0:T(8,128)(2,1)S(1)} all-to-all(bf16[32,8,288]{2,1,0:T(8,128)(2,1)S(1)} %bitcast.33), channel_id=1, replica_groups=mesh['dp'=8,'fsdp'=4] {'dp','fsdp'}, dimensions={0} | all-to-all | bytes 294912 | tf_op jit(solution)/shard_map/all_to_all | solution.py:955
  (114 shorter events, 53.5 us)
Async XLA Ops:
  2.3 20.3 %all-to-all-start = ((bf16[32,8,384]{2,1,0:T(8,128)(2,1)}), bf16[32,8,384]{2,1,0:T(8,128)(2,1)S(1)}, u32[]{:S(2)}, u32[]{:S(2)}) async-start(bf16[32,8,384]{2,1,0:T(8,128)(2,1)} %bitcast.2), calls=%async_computation | async-start | bytes 393216 | tf_op jit(solution)/shard_map/all_to_all | solution.py:764
  25.7 8.7 %collective-permute-start.1 = (bf16[1,32,1536]{2,1,0:T(8,128)(2,1)S(1)}, bf16[1,32,1536]{2,1,0:T(8,128)(2,1)S(1)}, u32[]{:S(2)}, u32[]{:S(2)}) collective-permute-start(bf16[1,32,1536]{2,1,0:T(8,128)(2,1)S(1)} %get-tuple-element.47), channel_id=1, source_target_pairs={{0,8},{4,12},{8,0},{12,4},{16,24},{20,28},{24,16},{28,20},{1,9},{5... | collective-permute-start | bytes 294920 | tf_op jit(solution)/shard_map/ppermute | solution.py:758
  27.6 10.7 %collective-permute-start.2 = (bf16[1,32,1536]{2,1,0:T(8,128)(2,1)S(1)}, bf16[1,32,1536]{2,1,0:T(8,128)(2,1)S(1)}, u32[]{:S(2)}, u32[]{:S(2)}) collective-permute-start(bf16[1,32,1536]{2,1,0:T(8,128)(2,1)S(1)} %get-tuple-element.48), channel_id=1, source_target_pairs={{0,16},{4,20},{8,24},{12,28},{16,0},{20,4},{24,8},{28,12},{1,17},{... | collective-permute-start | bytes 294920 | tf_op jit(solution)/shard_map/ppermute | solution.py:758
  30.0 8.3 %collective-permute-start.3 = (bf16[1,32,1536]{2,1,0:T(8,128)(2,1)S(1)}, bf16[1,32,1536]{2,1,0:T(8,128)(2,1)S(1)}, u32[]{:S(2)}, u32[]{:S(2)}) collective-permute-start(bf16[1,32,1536]{2,1,0:T(8,128)(2,1)S(1)} %get-tuple-element.49), channel_id=1, source_target_pairs={{0,24},{4,28},{8,16},{12,20},{16,8},{20,12},{24,0},{28,4},{1,25},{... | collective-permute-start | bytes 294920 | tf_op jit(solution)/shard_map/ppermute | solution.py:758
  42.2 5.2 %collective-permute-start.5 = (bf16[32,512]{1,0:T(8,128)(2,1)S(1)}, bf16[32,512]{1,0:T(8,128)(2,1)S(1)}, u32[]{:S(2)}, u32[]{:S(2)}) collective-permute-start(bf16[32,512]{1,0:T(8,128)(2,1)S(1)} %attention.1.refs_0_), channel_id=1, source_target_pairs={{0,16},{4,20},{8,24},{12,28},{16,0},{20,4},{24,8},{28,12},{1,17},{... | collective-permute-start | bytes 98312 | tf_op jit(solution)/shard_map/ppermute | solution.py:758
  43.5 5.7 %collective-permute-start.6 = (bf16[32,512]{1,0:T(8,128)(2,1)S(1)}, bf16[32,512]{1,0:T(8,128)(2,1)S(1)}, u32[]{:S(2)}, u32[]{:S(2)}) collective-permute-start(bf16[32,512]{1,0:T(8,128)(2,1)S(1)} %attention.1.refs_0_), channel_id=1, source_target_pairs={{0,24},{4,28},{8,16},{12,20},{16,8},{20,12},{24,0},{28,4},{1,25},{... | collective-permute-start | bytes 98312 | tf_op jit(solution)/shard_map/ppermute | solution.py:758
  51.0 7.7 %collective-permute-start.10 = (bf16[288,256]{1,0:T(8,128)(2,1)S(1)}, bf16[288,256]{1,0:T(8,128)(2,1)S(1)}, u32[]{:S(2)}, u32[]{:S(2)}) collective-permute-start(bf16[288,256]{1,0:T(8,128)(2,1)S(1)} %out_projection.1.refs_0_), channel_id=1, source_target_pairs={{0,3},{1,2},{2,1},{3,0},{4,7},{5,6},{6,5},{7,4},{8,11},{9,10},{10,... | collective-permute-start | bytes 442376 | tf_op jit(solution)/shard_map/ppermute | solution.py:761
  53.4 7.6 %collective-permute-start.8 = (bf16[288,256]{1,0:T(8,128)(2,1)S(1)}, bf16[288,256]{1,0:T(8,128)(2,1)S(1)}, u32[]{:S(2)}, u32[]{:S(2)}) collective-permute-start(bf16[288,256]{1,0:T(8,128)(2,1)S(1)} %out_projection.1.refs_0_), channel_id=1, source_target_pairs={{0,1},{1,0},{2,3},{3,2},{4,5},{5,4},{6,7},{7,6},{8,9},{9,8},{10,11... | collective-permute-start | bytes 442376 | tf_op jit(solution)/shard_map/ppermute | solution.py:761
  54.0 7.1 %collective-permute-start.9 = (bf16[288,256]{1,0:T(8,128)(2,1)S(1)}, bf16[288,256]{1,0:T(8,128)(2,1)S(1)}, u32[]{:S(2)}, u32[]{:S(2)}) collective-permute-start(bf16[288,256]{1,0:T(8,128)(2,1)S(1)} %out_projection.1.refs_0_), channel_id=1, source_target_pairs={{0,2},{1,3},{2,0},{3,1},{4,6},{5,7},{6,4},{7,5},{8,10},{9,11},{10,... | collective-permute-start | bytes 442376 | tf_op jit(solution)/shard_map/ppermute | solution.py:761
  70.9 7.7 %collective-permute-start.12 = (bf16[2,64,896]{2,1,0:T(8,128)(2,1)S(1)}, bf16[2,64,896]{2,1,0:T(8,128)(2,1)S(1)}, u32[]{:S(2)}, u32[]{:S(2)}) collective-permute-start(bf16[2,64,896]{2,1,0:T(8,128)(2,1)S(1)} %get-tuple-element.60), channel_id=1, source_target_pairs={{0,8},{4,12},{8,0},{12,4},{16,24},{20,28},{24,16},{28,20},{1,9},{5... | collective-permute-start | bytes 688136 | tf_op jit(solution)/shard_map/ppermute | solution.py:758
  81.1 8.4 %collective-permute-start.14 = (bf16[2,64,1024]{2,1,0:T(8,128)(2,1)S(1)}, bf16[2,64,1024]{2,1,0:T(8,128)(2,1)S(1)}, u32[]{:S(2)}, u32[]{:S(2)}) collective-permute-start(bf16[2,64,1024]{2,1,0:T(8,128)(2,1)S(1)} %get-tuple-element.66), channel_id=1, source_target_pairs={{0,8},{4,12},{8,0},{12,4},{16,24},{20,28},{24,16},{28,20},{1,9},{5... | collective-permute-start | bytes 786440 | tf_op jit(solution)/shard_map/ppermute | solution.py:758
  89.6 8.6 %collective-permute-start.18 = (bf16[1,64,896]{2,1,0:T(8,128)(2,1)S(1)}, bf16[1,64,896]{2,1,0:T(8,128)(2,1)S(1)}, u32[]{:S(2)}, u32[]{:S(2)}) collective-permute-start(bf16[1,64,896]{2,1,0:T(8,128)(2,1)S(1)} %get-tuple-element.73), channel_id=1, source_target_pairs={{0,16},{4,20},{8,24},{12,28},{16,0},{20,4},{24,8},{28,12},{1,17},{... | collective-permute-start | bytes 344072 | tf_op jit(solution)/shard_map/ppermute | solution.py:758
  98.5 5.3 %collective-permute-start.21 = (bf16[64,512]{1,0:T(8,128)(2,1)S(1)}, bf16[64,512]{1,0:T(8,128)(2,1)S(1)}, u32[]{:S(2)}, u32[]{:S(2)}) collective-permute-start(bf16[64,512]{1,0:T(8,128)(2,1)S(1)} %get-tuple-element.75.refs_3_.refs_0_), channel_id=1, source_target_pairs={{0,16},{4,20},{8,24},{12,28},{16,0},{20,4},{24,8},{28,12},{1,17},{... | collective-permute-start | bytes 196616 | tf_op jit(solution)/shard_map/ppermute | solution.py:758
  98.6 7.3 %collective-permute-start.20 = (bf16[64,512]{1,0:T(8,128)(2,1)S(1)}, bf16[64,512]{1,0:T(8,128)(2,1)S(1)}, u32[]{:S(2)}, u32[]{:S(2)}) collective-permute-start(bf16[64,512]{1,0:T(8,128)(2,1)S(1)} %get-tuple-element.75.refs_3_.refs_0_), channel_id=1, source_target_pairs={{0,8},{4,12},{8,0},{12,4},{16,24},{20,28},{24,16},{28,20},{1,9},{5... | collective-permute-start | bytes 196616 | tf_op jit(solution)/shard_map/ppermute | solution.py:758
  103.9 5.0 %collective-permute-start.22 = (bf16[64,512]{1,0:T(8,128)(2,1)S(1)}, bf16[64,512]{1,0:T(8,128)(2,1)S(1)}, u32[]{:S(2)}, u32[]{:S(2)}) collective-permute-start(bf16[64,512]{1,0:T(8,128)(2,1)S(1)} %collective-permute-done.21.refs_2_), channel_id=1, source_target_pairs={{0,8},{4,12},{8,0},{12,4},{16,24},{20,28},{24,16},{28,20},{1,9},{5... | collective-permute-start | bytes 196616 | tf_op jit(solution)/shard_map/ppermute | solution.py:758
  103.9 14.8 %collective-permute-start.16 = (bf16[2,64,1024]{2,1,0:T(8,128)(2,1)S(1)}, bf16[2,64,1024]{2,1,0:T(8,128)(2,1)S(1)}, u32[]{:S(2)}, u32[]{:S(2)}) collective-permute-start(bf16[2,64,1024]{2,1,0:T(8,128)(2,1)S(1)} %get-tuple-element.71), channel_id=1, source_target_pairs={{0,8},{4,12},{8,0},{12,4},{16,24},{20,28},{24,16},{28,20},{1,9},{5... | collective-permute-start | bytes 786440 | tf_op jit(solution)/shard_map/ppermute | solution.py:758
  109.0 14.0 %collective-permute-start.23 = (bf16[4,64,512]{2,1,0:T(8,128)(2,1)S(1)}, bf16[4,64,512]{2,1,0:T(8,128)(2,1)S(1)}, u32[]{:S(2)}, u32[]{:S(2)}) collective-permute-start(bf16[4,64,512]{2,1,0:T(8,128)(2,1)S(1)} %pad_maximum_fusion), channel_id=1, source_target_pairs={{0,4},{4,0},{8,12},{12,8},{16,20},{20,16},{24,28},{28,24},{1,5},{5... | collective-permute-start | bytes 786440 | tf_op jit(solution)/shard_map/ppermute | solution.py:755
  109.0 9.5 %collective-permute-start.17 = (bf16[1,64,1024]{2,1,0:T(8,128)(2,1)S(1)}, bf16[1,64,1024]{2,1,0:T(8,128)(2,1)S(1)}, u32[]{:S(2)}, u32[]{:S(2)}) collective-permute-start(bf16[1,64,1024]{2,1,0:T(8,128)(2,1)S(1)} %get-tuple-element.72), channel_id=1, source_target_pairs={{0,16},{4,20},{8,24},{12,28},{16,0},{20,4},{24,8},{28,12},{1,17},{... | collective-permute-start | bytes 393224 | tf_op jit(solution)/shard_map/ppermute | solution.py:758
  118.8 9.8 %collective-permute-start.19 = (bf16[1,64,1024]{2,1,0:T(8,128)(2,1)S(1)}, bf16[1,64,1024]{2,1,0:T(8,128)(2,1)S(1)}, u32[]{:S(2)}, u32[]{:S(2)}) collective-permute-start(bf16[1,64,1024]{2,1,0:T(8,128)(2,1)S(1)} %get-tuple-element.77), channel_id=1, source_target_pairs={{0,16},{4,20},{8,24},{12,28},{16,0},{20,4},{24,8},{28,12},{1,17},{... | collective-permute-start | bytes 393224 | tf_op jit(solution)/shard_map/ppermute | solution.py:758
  118.8 12.4 %collective-permute-start.29 = (bf16[64,512]{1,0:T(8,128)(2,1)S(1)}, bf16[64,512]{1,0:T(8,128)(2,1)S(1)}, u32[]{:S(2)}, u32[]{:S(2)}) collective-permute-start(bf16[64,512]{1,0:T(8,128)(2,1)S(1)} %activation_1.1._.refs_0_), channel_id=1, source_target_pairs={{0,16},{4,20},{8,24},{12,28},{16,0},{20,4},{24,8},{28,12},{1,17},{... | collective-permute-start | bytes 196616 | tf_op jit(solution)/shard_map/ppermute | solution.py:758
  128.7 5.7 %collective-permute-start.25 = (bf16[64,512]{1,0:T(8,128)(2,1)S(1)}, bf16[64,512]{1,0:T(8,128)(2,1)S(1)}, u32[]{:S(2)}, u32[]{:S(2)}) collective-permute-start(bf16[64,512]{1,0:T(8,128)(2,1)S(1)} %activation_2.1.refs_6_.refs_0_), channel_id=1, source_target_pairs={{0,16},{4,20},{8,24},{12,28},{16,0},{20,4},{24,8},{28,12},{1,17},{... | collective-permute-start | bytes 196616 | tf_op jit(solution)/shard_map/ppermute | solution.py:758
  128.8 6.3 %collective-permute-start.28 = (bf16[64,512]{1,0:T(8,128)(2,1)S(1)}, bf16[64,512]{1,0:T(8,128)(2,1)S(1)}, u32[]{:S(2)}, u32[]{:S(2)}) collective-permute-start(bf16[64,512]{1,0:T(8,128)(2,1)S(1)} %activation_1.1._.refs_0_), channel_id=1, source_target_pairs={{0,8},{4,12},{8,0},{12,4},{16,24},{20,28},{24,16},{28,20},{1,9},{5... | collective-permute-start | bytes 196616 | tf_op jit(solution)/shard_map/ppermute | solution.py:758
  131.2 5.3 %collective-permute-start.30 = (bf16[64,512]{1,0:T(8,128)(2,1)S(1)}, bf16[64,512]{1,0:T(8,128)(2,1)S(1)}, u32[]{:S(2)}, u32[]{:S(2)}) collective-permute-start(bf16[64,512]{1,0:T(8,128)(2,1)S(1)} %collective-permute-done.29.refs_2_), channel_id=1, source_target_pairs={{0,8},{4,12},{8,0},{12,4},{16,24},{20,28},{24,16},{28,20},{1,9},{5... | collective-permute-start | bytes 196616 | tf_op jit(solution)/shard_map/ppermute | solution.py:758
  131.3 6.7 %collective-permute-start.24 = (bf16[64,512]{1,0:T(8,128)(2,1)S(1)}, bf16[64,512]{1,0:T(8,128)(2,1)S(1)}, u32[]{:S(2)}, u32[]{:S(2)}) collective-permute-start(bf16[64,512]{1,0:T(8,128)(2,1)S(1)} %activation_2.1.refs_6_.refs_0_), channel_id=1, source_target_pairs={{0,8},{4,12},{8,0},{12,4},{16,24},{20,28},{24,16},{28,20},{1,9},{5... | collective-permute-start | bytes 196616 | tf_op jit(solution)/shard_map/ppermute | solution.py:758
  (21 other events, 128.5 us)

commit v3 on v2

--- a/solution.py
+++ b/solution.py
@@ -14,8 +14,8 @@
 BF16 = jnp.bfloat16
 F32 = jnp.float32
 FAR = -3.0e38
-SMALL, ATTENTION, LARGE = 12, 24, 60
-SLOTS = 4
+SMALL, ATTENTION, LARGE = 16, 24, 60
+SLOTS = 8
 
 
 def params(mib=SMALL):
@@ -44,8 +44,15 @@
 
 
 def full_spec(shape):
+    return pl.BlockSpec(memory_space=pltpu.VMEM)
+
+
+def block_spec(shape):
     zeros = (0,) * len(shape)
-    return pl.BlockSpec(tuple(shape), lambda *_: zeros, pipeline_mode=pl.Buffered(1))
+    return pl.BlockSpec(tuple(shape), lambda *_: zeros)
+
+
+SCALARS = pl.BlockSpec(memory_space=pltpu.SMEM)
 
 
 def pack_kernel(hidden_ref, routes_ref, out_ref):
@@ -76,12 +83,11 @@
     out = (slices, copies, req, room)
     return pl.pallas_call(
         pack_kernel,
-        grid=(1,),
         in_specs=[full_spec(hidden_in.shape), full_spec(routes.shape)],
         out_specs=full_spec(out),
         out_shape=jax.ShapeDtypeStruct(out, BF16),
         compiler_params=params(),
-        cost_estimate=pl.CostEstimate(flops=hidden_in.size, bytes_accessed=4 * hidden_in.size, transcendentals=0),
+        cost_estimate=pl.CostEstimate(flops=1, bytes_accessed=1, transcendentals=0),
         name="pack",
     )(hidden_in, routes)
 
@@ -164,22 +170,16 @@
     ]
     return pl.pallas_call(
         functools.partial(places_kernel, experts, width, staying),
-        grid_spec=pltpu.PrefetchScalarGridSpec(
-            num_scalar_prefetch=4,
-            grid=(1,),
-            in_specs=[full_spec(recv.shape), pl.BlockSpec(memory_space=pl.ANY)],
-            out_specs=[
-                pl.BlockSpec(memory_space=pltpu.SMEM),
-                full_spec(outs[1].shape),
-                full_spec(outs[2].shape),
-            ],
-            scratch_shapes=[pltpu.VMEM((total, LANES), F32), pltpu.VMEM((total, LANES), F32)],
-        ),
+        in_specs=[SCALARS] * 4 + [full_spec(recv.shape), pl.BlockSpec(memory_space=pl.ANY)],
+        out_specs=[
+            pl.BlockSpec(memory_space=pltpu.SMEM),
+            full_spec(outs[1].shape),
+            full_spec(outs[2].shape),
+        ],
+        scratch_shapes=[pltpu.VMEM((total, LANES), F32), pltpu.VMEM((total, LANES), F32)],
         out_shape=outs,
         compiler_params=params(room(total)),
-        cost_estimate=pl.CostEstimate(
-            flops=total * total * LANES, bytes_accessed=16 * total * LANES, transcendentals=0
-        ),
+        cost_estimate=pl.CostEstimate(flops=1, bytes_accessed=1, transcendentals=0),
         name="pair_places",
     )(move_target, order, slot_of, column, recv, after)
 
@@ -188,10 +188,15 @@
     pages, page_len, _, cols = pool_ref.shape
     rows = pages * page_len
     both = pool_ref[...].reshape(2 * rows, cols)
-    wide = lax.broadcasted_iota(jnp.int32, (rows, 2 * rows), 1)
-    high = lax.broadcasted_iota(jnp.int32, (rows, 2 * rows), 0)
-    key_ref[...] = dot_nn((wide == 2 * high).astype(BF16), both).astype(BF16)
-    value_ref[...] = dot_nn((wide == 2 * high + 1).astype(BF16), both).astype(BF16)
+    part = min(rows, LANES)
+    wide = lax.broadcasted_iota(jnp.int32, (part, 2 * part), 1)
+    high = lax.broadcasted_iota(jnp.int32, (part, 2 * part), 0)
+    even = (wide == 2 * high).astype(F32).astype(BF16)
+    odd = (wide == 2 * high + 1).astype(F32).astype(BF16)
+    for start in range(0, rows, part):
+        piece = both[2 * start : 2 * (start + part)]
+        key_ref[start : start + part] = dot_nn(even, piece).astype(BF16)
+        value_ref[start : start + part] = dot_nn(odd, piece).astype(BF16)
     requests = bias_ref.shape[0]
     prompts, prompt_len = prompt_ref.shape
     own_len = lists_ref.shape[1] - 2
@@ -221,7 +226,7 @@
             num_scalar_prefetch=1,
             grid=(pages // block,),
             in_specs=[
-                full_spec(lists.shape),
+                block_spec(lists.shape),
                 pl.BlockSpec((block, page_len, 2, cols), lambda b, *_: (b, 0, 0, 0)),
                 pl.BlockSpec(memory_space=pl.ANY),
             ],
@@ -229,11 +234,7 @@
         ),
         out_shape=[out, out, jax.ShapeDtypeStruct((requests, pages * page_len), F32)],
         compiler_params=params(),
-        cost_estimate=pl.CostEstimate(
-            flops=8 * block * page_len * cache_pool.size,
-            bytes_accessed=4 * cache_pool.size,
-            transcendentals=0,
-        ),
+        cost_estimate=pl.CostEstimate(flops=1, bytes_accessed=1, transcendentals=0),
         name="pool_split",
     )(prompt_pages, lists, cache_pool, after)
 
@@ -265,18 +266,12 @@
     raw = jax.ShapeDtypeStruct((total, width), BF16)
     return pl.pallas_call(
         qkv_kernel,
-        grid_spec=pltpu.PrefetchScalarGridSpec(
-            num_scalar_prefetch=1,
-            grid=(1,),
-            in_specs=[full_spec(x.shape) for x in (recv, norm_slice, weights)] + [pl.BlockSpec(memory_space=pl.ANY)],
-            out_specs=[full_spec(out.shape), full_spec(out.shape), full_spec(raw.shape)],
-            scratch_shapes=[pltpu.VMEM((total, width), BF16), pltpu.VMEM((total, width), BF16)],
-        ),
+        in_specs=[SCALARS] * 1 + [full_spec(x.shape) for x in (recv, norm_slice, weights)] + [pl.BlockSpec(memory_space=pl.ANY)],
+        out_specs=[full_spec(out.shape), full_spec(out.shape), full_spec(raw.shape)],
+        scratch_shapes=[pltpu.VMEM((total, width), BF16), pltpu.VMEM((total, width), BF16)],
         out_shape=[out, out, raw],
         compiler_params=params(room(total)),
-        cost_estimate=pl.CostEstimate(
-            flops=6 * total * width * cols, bytes_accessed=6 * total * cols + 6 * width * cols, transcendentals=0
-        ),
+        cost_estimate=pl.CostEstimate(flops=1, bytes_accessed=1, transcendentals=0),
         name="qkv",
     )(order, recv, norm_slice, weights, after)
 
@@ -332,7 +327,6 @@
     operands = [*parts, cosine, sine, bias, keys, values]
     return pl.pallas_call(
         attention_kernel,
-        grid=(1,),
         in_specs=[full_spec(x.shape) for x in operands] + [pl.BlockSpec(memory_space=pl.ANY)],
         out_specs=full_spec((row, cols)),
         out_shape=jax.ShapeDtypeStruct((row, cols), BF16),
@@ -341,11 +335,7 @@
             pltpu.VMEM((heads * row, stretch), BF16),
         ],
         compiler_params=params(ATTENTION),
-        cost_estimate=pl.CostEstimate(
-            flops=4 * heads * row * stretch * cols,
-            bytes_accessed=4 * stretch * cols,
-            transcendentals=heads * row * stretch,
-        ),
+        cost_estimate=pl.CostEstimate(flops=1, bytes_accessed=1, transcendentals=0),
         name="attention",
     )(*operands, after)
 
@@ -364,14 +354,11 @@
     out = (weights.shape[0], 2 * half)
     return pl.pallas_call(
         out_kernel,
-        grid=(1,),
         in_specs=[full_spec(x.shape) for x in operands],
         out_specs=full_spec(out),
         out_shape=jax.ShapeDtypeStruct(out, BF16),
         compiler_params=params(room(2 * half)),
-        cost_estimate=pl.CostEstimate(
-            flops=2 * weights.size * out[1], bytes_accessed=4 * weights.size, transcendentals=0
-        ),
+        cost_estimate=pl.CostEstimate(flops=1, bytes_accessed=1, transcendentals=0),
         name="out_projection",
     )(*operands)
 
@@ -431,14 +418,15 @@
     return pl.ds(start, window), (rows >= first) & (rows < offset_ref[expert + 1])
 
 
-def gate_kernel(count_parts, begin, columns, tail, window, offset_ref, order_ref, *refs):
+def gate_kernel(count_parts, begin, columns, tail, window, waits, offset_ref, order_ref, *refs):
     first = count_parts > 0
+    refs = refs[waits:]
     if first:
         parts, refs = refs[:count_parts], refs[count_parts:]
-        hid_ref, norm_ref, router_ref, line_ref, tail_ref, w_ref, _ = refs[:7]
-        keep_ref, send_ref, resid_ref, spread_ref, held, aux, w_held, w_sems, tail_held, tail_sem = refs[7:]
+        hid_ref, norm_ref, router_ref, line_ref, tail_ref, w_ref = refs[:6]
+        keep_ref, send_ref, resid_ref, spread_ref, held, aux, w_held, w_sems, tail_held, tail_sem = refs[6:]
     else:
-        spread_ref, w_ref, _, keep_ref, send_ref, held, w_held, w_sems = refs
+        spread_ref, w_ref, keep_ref, send_ref, held, w_held, w_sems = refs
     experts = w_ref.shape[0]
     pairs = spread_ref.shape[1]
     width = spread_ref.shape[2] // 2
@@ -510,10 +498,10 @@
             pl.BlockSpec((*lead, LANES), lambda *_: (0,) * len(lead) + (number,)),
             pl.BlockSpec(memory_space=pl.ANY),
         ],
-        out_specs=full_spec(out),
+        out_specs=block_spec(out),
         out_shape=jax.ShapeDtypeStruct(out, BF16),
         compiler_params=params(),
-        cost_estimate=pl.CostEstimate(flops=0, bytes_accessed=4 * out[0] * rows * LANES, transcendentals=0),
+        cost_estimate=pl.CostEstimate(flops=1, bytes_accessed=1, transcendentals=0),
         name=name,
     )(weights, after)
 
@@ -525,7 +513,7 @@
     return 3 * LANES, LANES, 2 * LANES, size
 
 
-def sum_kernel(aux_at, groups, keep_ref, recv_ref, _, *outs):
+def sum_kernel(aux_at, groups, keep_ref, recv_ref, *outs):
     outs = outs[-len(groups) :]
     width = keep_ref.shape[2]
 
@@ -555,28 +543,27 @@
                 out[k, :, span] = value.astype(BF16)
 
 
-def sum_parts(keep, recv, groups, aux_at, name, after=None, hold=None):
+def sum_parts(keep, recv, groups, aux_at, name, after=(), hold=None):
     _, block, width = keep.shape
     outs = [jax.ShapeDtypeStruct((len(group), block, width), BF16) for group in groups]
-    in_specs = [full_spec(keep.shape)] * 2 + [pl.BlockSpec(memory_space=pl.ANY)]
+    in_specs = [full_spec(keep.shape)] * 2 + [pl.BlockSpec(memory_space=pl.ANY)] * len(after)
     out_specs = [full_spec(out.shape) for out in outs]
-    operands = [keep, recv, keep if after is None else after]
+    operands = [keep, recv, *after]
     aliases = {}
     if hold is not None:
         operands.append(hold)
         in_specs.append(pl.BlockSpec(memory_space=pl.ANY))
         outs.insert(0, jax.ShapeDtypeStruct(hold.shape, hold.dtype))
         out_specs.insert(0, pl.BlockSpec(memory_space=pl.ANY))
-        aliases = {3: 0}
+        aliases = {len(operands) - 1: 0}
     return pl.pallas_call(
         functools.partial(sum_kernel, aux_at, groups),
-        grid=(1,),
         in_specs=in_specs,
         out_specs=out_specs,
         out_shape=outs,
         input_output_aliases=aliases,
         compiler_params=params(),
-        cost_estimate=pl.CostEstimate(flops=keep.size, bytes_accessed=6 * keep.size, transcendentals=0),
+        cost_estimate=pl.CostEstimate(flops=1, bytes_accessed=1, transcendentals=0),
         name=name,
     )(*operands)
 
@@ -591,10 +578,10 @@
     for part in parts[1:]:
         total = total + part[0].astype(F32)
     if tail is None:
-        stat_ref, _, act_ref = refs
+        stat_ref, act_ref = refs[0], refs[-1]
         inverse, weight = stat_ref[:, 0:1], stat_ref[:, 1:2]
     else:
-        _, act_ref, stat_ref = refs
+        act_ref, stat_ref = refs[-2:]
         tail_width, up_at, aux_at, size = tail
         base = 2 * columns + aux_at
         squares = total[:, base : base + 1]
@@ -628,65 +615,79 @@
     stat = jax.ShapeDtypeStruct((rows, LANES), F32)
     operands = [*parts] + ([] if tail else [stats])
     outs = [out, stat] if tail else [out]
-    in_specs = [full_spec(x.shape) for x in operands] + [pl.BlockSpec(memory_space=pl.ANY)]
+    in_specs = [full_spec(x.shape) for x in operands] + [pl.BlockSpec(memory_space=pl.ANY)] * len(after)
     result = pl.pallas_call(
         functools.partial(act_kernel, len(parts), columns, tail, features),
-        grid=(1,),
         in_specs=in_specs,
         out_specs=[full_spec(x.shape) for x in outs],
         out_shape=outs,
         compiler_params=params(),
-        cost_estimate=pl.CostEstimate(
-            flops=16 * rows * columns, bytes_accessed=20 * rows * columns, transcendentals=rows * columns
-        ),
+        cost_estimate=pl.CostEstimate(flops=1, bytes_accessed=1, transcendentals=0),
         name=name,
-    )(*operands, after)
+    )(*operands, *after)
     return (result[0], result[1]) if tail else (result[0], stats)
 
 
-def down_kernel(count_parts, begin, columns, tail, window, begins, ends, offset_ref, order_ref, *refs):
-    parts, refs = refs[:count_parts], refs[count_parts:]
-    other_ref, w_ref, _, refs = refs[0], refs[1], refs[2], refs[3:]
+def lane_window(offset_ref, expert, pairs, window):
+    first = offset_ref[expert]
+    start = pl.multiple_of(jnp.minimum(first // LANES * LANES, pairs - window), LANES)
+    lanes = lax.broadcasted_iota(jnp.int32, (1, window), 1) + start
+    return pl.ds(start, window), (lanes >= first) & (lanes < offset_ref[expert + 1])
+
+
+def down_kernel(half, chunks, tail, window, begins, ends, waits, offset_ref, order_ref, *refs):
+    refs = refs[waits:]
+    gathered = []
+    for _ in chunks:
+        gathered.append((refs[:half], refs[half]))
+        refs = refs[half + 1 :]
+    w_ref, refs = refs[0], refs[1:]
     if tail:
         tail_ref, refs = refs[0], refs[1:]
     if not begins:
         before_ref, refs = refs[0], refs[1:]
     if ends:
-        place_ref, resid_ref, out_ref, total_ref, held, w_held, w_sems = refs
+        place_ref, resid_ref, out_ref, total_ref, *held, w_held, w_sems = refs
     else:
-        total_ref, held, w_held, w_sems = refs
-    block = parts[0].shape[0]
-    half = len(parts)
-    pairs = held.shape[0]
+        total_ref, *held, w_held, w_sems = refs
     experts = w_ref.shape[0]
-    copies = [
-        pltpu.make_async_copy(w_ref.at[e, :, pl.ds(begin, columns)], w_held.at[e % SLOTS], w_sems.at[e % SLOTS])
-        for e in range(experts)
-    ]
+    pairs = held[0].shape[0]
+    copies = []
+    for begin, columns in chunks:
+        for e in range(experts):
+            slot = len(copies) % SLOTS
+            copies.append(
+                pltpu.make_async_copy(
+                    w_ref.at[e, :, pl.ds(begin, columns)], w_held.at[slot, :, pl.ds(0, columns)], w_sems.at[slot]
+                )
+            )
     for copy in copies[:SLOTS]:
         copy.start()
-    for slot in range(half):
-        mine = pl.ds(pl.multiple_of(order_ref[slot] * block, block), block)
-        other = pl.ds(pl.multiple_of(order_ref[half + slot] * block, block), block)
-        held[mine] = parts[slot][...]
-        held[other] = other_ref[slot]
+    for (parts, other_ref), into in zip(gathered, held):
+        block = parts[0].shape[0]
+        for slot in range(half):
+            mine = pl.ds(pl.multiple_of(order_ref[slot] * block, block), block)
+            other = pl.ds(pl.multiple_of(order_ref[half + slot] * block, block), block)
+            into[mine] = parts[slot][...]
+            into[other] = other_ref[slot]
     total_ref[...] = jnp.zeros_like(total_ref) if begins else before_ref[...]
-    for expert in range(experts):
-        rows, valid = window_of(offset_ref, expert, pairs, window)
-        copies[expert].wait()
-        result = dot_nt(held[rows, :columns], w_held[expert % SLOTS])
-        if expert + SLOTS < experts:
-            copies[expert + SLOTS].start()
-        if tail:
-            result = result + dot_nt(held[rows, columns:], tail_ref[expert])
-        total_ref[rows] = total_ref[rows] + jnp.where(valid, result, 0.0)
+    for index, (begin, columns) in enumerate(chunks):
+        for expert in range(experts):
+            number = index * experts + expert
+            lanes, valid = lane_window(offset_ref, expert, pairs, window)
+            copies[number].wait()
+            result = dot_nt(w_held[number % SLOTS, :, :columns], held[index][lanes, :columns])
+            if number + SLOTS < len(copies):
+                copies[number + SLOTS].start()
+            if tail and index == 0:
+                result = result + dot_nt(tail_ref[expert], held[index][lanes, columns:])
+            total_ref[:, lanes] = total_ref[:, lanes] + jnp.where(valid, result, 0.0)
 
     if ends:
         total = out_ref.shape[0]
         pieces = [x.astype(BF16) for x in split_bf16(total_ref[...], 2)]
         resid = [x.astype(BF16) for x in split_bf16(resid_ref[...], 2)]
-        step = pair_block(total) if total > 256 else total
-        step = min(step, 256)
+        step = pair_block(total)
         for start in range(0, total, step):
             here = slice(start, start + step)
             pair = lax.broadcasted_iota(jnp.int32, (step, pairs), 1)
@@ -695,9 +696,31 @@
             pick = pick.astype(F32).astype(BF16)
             token = lax.broadcasted_iota(jnp.int32, (step, total), 1)
             move = (token == place[:, 2:3]).astype(F32).astype(BF16)
-            result = dot_nn(pick, pieces[0]) + dot_nn(pick, pieces[1])
+            result = dot_nt(pick, pieces[0]) + dot_nt(pick, pieces[1])
             result = result + dot_nt(move, resid[0]) + dot_nt(move, resid[1])
             out_ref[here] = result.astype(BF16)
+
+
+def stack_kernel(counts, *refs):
+    outs = refs[-len(counts) :]
+    for count, out in zip(counts, outs):
+        parts, refs = refs[:count], refs[count:]
+        for k, part in enumerate(parts):
+            out[k] = part[...]
+
+
+def stack_parts(lists, after):
+    operands = [x for parts in lists for x in parts]
+    outs = [jax.ShapeDtypeStruct((len(parts), *parts[0].shape), BF16) for parts in lists]
+    return pl.pallas_call(
+        functools.partial(stack_kernel, [len(parts) for parts in lists]),
+        in_specs=[full_spec(x.shape) for x in operands] + [pl.BlockSpec(memory_space=pl.ANY)] * len(after),
+        out_specs=[full_spec(x.shape) for x in outs],
+        out_shape=outs,
+        compiler_params=params(),
+        cost_estimate=pl.CostEstimate(flops=1, bytes_accessed=1, transcendentals=0),
+        name="stack_parts",
+    )(*operands, *after)
 
 
 def chunk_columns(units):
@@ -744,6 +767,7 @@
     units = gate_up.shape[3]
     window = windows(pairs, CAP * dp * fs)
 
+    hidden_in = pltpu.with_memory_space_constraint(hidden_in, pltpu.HBM)
     gate_up = pltpu.with_memory_space_constraint(gate_up, pltpu.HBM)
     expert_down = pltpu.with_memory_space_constraint(expert_down, pltpu.HBM)
 
@@ -777,7 +801,7 @@
     def slice_of(vector):
         return lax.dynamic_slice_in_dim(vector, my_row * width, width)
 
-    keys, values, bias = split_pool(prompt_pages, lists, cache_pool, payload)
+    gate_tail = last_units(gate_up, payload, gate_tail_kernel, 2 * width, "gate_tail")
     keep, send, raw = project_qkv(
         order,
         recv,
@@ -785,7 +809,7 @@
         project_in.transpose(1, 0, 2),
         half,
         row,
-        bias,
+        gate_tail,
     )
     sums = sum_parts(keep, swap(send), [[s] for s in range(half)], None, "core_sum_qkv")
     slot_of = (row_ids % 2 ^ my_core) * half + (row_ids // 2 ^ my_chip)
@@ -793,9 +817,9 @@
     offsets, place_table, line_table = pair_places(
         move_target, order, slot_of, column, recv, sums[0], experts, width
     )
-    gate_tail = last_units(gate_up, place_table, gate_tail_kernel, 2 * width, "gate_tail")
+    keys, values, bias = split_pool(prompt_pages, lists, cache_pool, place_table)
     parts = [sums[0]] + [over_chips(sums[s], s) for s in range(1, half)]
-    heads_out = attend(parts, cosine, sine, bias, keys, values, gate_tail)
+    heads_out = attend(parts, cosine, sine, bias, keys, values, place_table)
 
     parts = [heads_out] + [over_chips(heads_out, s) for s in range(1, half)]
     other = swap(jnp.concatenate(parts, axis=0))
@@ -811,9 +835,15 @@
     resid_shape = jax.ShapeDtypeStruct((width, total), F32)
     norm_column = slice_of(norm_second).astype(F32)[:, None]
     router_slice = lax.dynamic_slice_in_dim(router, my_row * width, width).T
-    state = {"after": line_table}
+    state = {"after": [line_table]}
+    flight = []
+
+    def waits():
+        after, flight[:] = state["after"] + flight, []
+        return after
 
     def gate(index):
+        after = state["after"]
         begin, columns = chunks[index]
         first = index == 0
         out_width = 2 * columns + (tail[0] if first else 0)
@@ -833,36 +863,30 @@
             outs = [half_out, half_out]
             scratch += weights
         result = pl.pallas_call(
-            functools.partial(gate_kernel, len(parts) if first else 0, begin, columns, tail, window),
-            grid_spec=pltpu.PrefetchScalarGridSpec(
-                num_scalar_prefetch=2,
-                grid=(1,),
-                in_specs=[*in_specs, anywhere, anywhere],
-                out_specs=[full_spec(x.shape) for x in outs],
-                scratch_shapes=scratch,
-            ),
+            functools.partial(gate_kernel, len(parts) if first else 0, begin, columns, tail, window, len(after)),
+            in_specs=[SCALARS] * 2 + [anywhere] * len(after) + [*in_specs, anywhere],
+            out_specs=[full_spec(x.shape) for x in outs],
+            scratch_shapes=scratch,
             out_shape=outs,
             compiler_params=params(room(total)),
-            cost_estimate=pl.CostEstimate(
-                flops=8 * experts * window * width * columns,
-                bytes_accessed=4 * experts * width * columns,
-                transcendentals=0,
-            ),
+            cost_estimate=pl.CostEstimate(flops=1, bytes_accessed=1, transcendentals=0),
             name=f"gate_up_{index}",
-        )(offsets, order, *operands, gate_up, state["after"])
+        )(offsets, order, *after, *operands, gate_up)
         if first:
             state["resid"], state["spread"] = result[2:]
-        state["after"] = result[0]
+        state["after"] = [result[0]]
         return result[:2]
 
     def combine(index, bit, held, hold=None):
         aux_at = 2 * chunks[index][1] + tail[2] if index == 0 else None
         sums = sum_parts(
-            *held, halves(held[0].shape[0]), aux_at, f"sum_{index}_{bit}", state["after"], hold
+            *held, halves(held[0].shape[0]), aux_at, f"sum_{index}_{bit}", waits() if bit else state["after"], hold
         )
         kept, sent = sums[-2:]
-        state["after"] = kept
-        return [kept, over_chips(sent, 1 << bit)], sums[0]
+        state["after"] = [kept]
+        received = over_chips(sent, 1 << bit)
+        flying.append(received)
+        return [kept, received], sums[0]
 
     def activate(index, held):
         act, state["stats"] = activation(
@@ -872,32 +896,38 @@
             tail if index == 0 else None,
             float(features),
             f"activation_{index}",
-            state["after"],
+            waits(),
         )
-        state["after"] = act
-        parts = {0: act}
-        for bit in reversed(range(stages)):
-            parts.update({s | 1 << bit: over_chips(x, 1 << bit) for s, x in list(parts.items())})
-        return [parts[s] for s in range(half)]
-
-    def down(index, parts):
-        begin, columns = chunks[index]
-        first, last = index == 0, index == len(chunks) - 1
-        operands = [*parts, swap(jnp.stack(parts))]
-        in_specs = [full_spec(x.shape) for x in operands] + [anywhere, anywhere]
-        operands += [expert_down, state["after"]]
+        state["after"] = [act]
+        return act
+
+    def spread_out(parts, fresh):
+        more = {}
+        for s in fresh:
+            low = (s & -s).bit_length() - 1 if s else stages
+            for bit in range(low):
+                more[s | 1 << bit] = over_chips(parts[s], 1 << bit)
+        flying.extend(more.values())
+        parts.update(more)
+        return list(more)
+
+    def down(numbers, lists, after):
+        first, last = numbers[0] == 0, numbers[-1] == len(chunks) - 1
+        stacked = stack_parts(lists, after)
+        others = [swap(x) for x in stacked]
+        operands = [x for parts, other in zip(lists, others) for x in (*parts, other)]
+        in_specs = [full_spec(x.shape) for x in operands] + [anywhere]
+        operands.append(expert_down)
         if first:
             operands.append(state["tail"])
             in_specs.append(full_spec(state["tail"].shape))
         else:
             operands.append(state["sum"])
             in_specs.append(full_spec(state["sum"].shape))
-        sum_shape = jax.ShapeDtypeStruct((pairs, width), F32)
-        scratch = [
-            pltpu.VMEM((pairs, parts[0].shape[1]), BF16),
-            pltpu.VMEM((SLOTS, width, columns), BF16),
-            pltpu.SemaphoreType.DMA((SLOTS,)),
-        ]
+        sum_shape = jax.ShapeDtypeStruct((width, pairs), F32)
+        widest = max(chunks[k][1] for k in numbers)
+        scratch = [pltpu.VMEM((pairs, parts[0].shape[1]), BF16) for parts in lists]
+        scratch += [pltpu.VMEM((SLOTS, width, widest), BF16), pltpu.SemaphoreType.DMA((SLOTS,))]
         outs = [sum_shape]
         if last:
             operands += [place_table, state["resid"]]
@@ -906,51 +936,63 @@
             scratch = [pltpu.VMEM(sum_shape.shape, F32)] + scratch
         result = pl.pallas_call(
             functools.partial(
-                down_kernel, len(parts), begin, columns, tail if first else None, window, first, last
+                down_kernel,
+                half,
+                [chunks[k] for k in numbers],
+                tail if first else None,
+                min(-(-CAP * dp * fs // LANES) * LANES + LANES, pairs),
+                first,
+                last,
+                0,
             ),
-            grid_spec=pltpu.PrefetchScalarGridSpec(
-                num_scalar_prefetch=2,
-                grid=(1,),
-                in_specs=in_specs,
-                out_specs=[full_spec(x.shape) for x in outs],
-                scratch_shapes=scratch,
-            ),
+                    in_specs=[SCALARS] * 2 + in_specs,
+            out_specs=[full_spec(x.shape) for x in outs],
+            scratch_shapes=scratch,
             out_shape=outs,
             compiler_params=params(room(total)),
-            cost_estimate=pl.CostEstimate(
-                flops=2 * experts * window * width * columns,
-                bytes_accessed=2 * experts * width * columns,
-                transcendentals=0,
-            ),
-            name=f"down_{index}",
+            cost_estimate=pl.CostEstimate(flops=1, bytes_accessed=1, transcendentals=0),
+            name=f"down_{numbers[0]}",
         )(offsets, order, *operands)[0]
-        state["sum"] = state["after"] = result
+        state["sum"] = result
         return result
 
     stages = half.bit_length() - 1
     count = len(chunks)
-    held, gathered = {}, {}
-    for step in range(count + stages + 3):
+    early = max(0, count - stages)
+    held, gathered, fresh = {}, {}, {}
+    flying = []
+    for step in range(count + stages):
         sent = None
         if step < count:
             kept, sent = gate(step)
         if step == count - 1:
-            state["tail"] = last_units(expert_down, state["after"], down_tail_kernel, width, "down_tail")
+            state["tail"] = last_units(expert_down, state["after"][0], down_tail_kernel, width, "down_tail")
         for k in range(count):
-            if step - k == stages + 2:
-                result = down(k, gathered[k])
-        for k in range(count):
-            if step >= count and step - k == stages:
-                gathered[k] = activate(k, held[k])
-        for k in range(count):
-            if 1 <= step - k < stages:
+            if step - k == stages:
+                if step == count - 1 + stages:
+                    flight.append(state["tail"])
+                gathered[k] = {0: activate(k, held[k])}
+                if k < count - 1:
+                    fresh[k] = spread_out(gathered[k], [0])
+                else:
+                    gathered[k].update({s: over_chips(gathered[k][0], s) for s in range(1, half)})
+            elif 1 <= step - k < stages:
                 held[k], through = combine(k, step - k, held[k], sent)
                 sent = None if sent is None else through
         if step < count:
             held[step], _ = combine(step, 0, [kept, swap(sent)])
-        for k in range(count):
-            if step < count and step - k == stages:
-                gathered[k] = activate(k, held[k])
+        for k in range(count - 1):
+            if stages < step - k:
+                fresh[k] = spread_out(gathered[k], fresh[k])
+        flight.extend(flying)
+        flying.clear()
+    while any(fresh.values()):
+        fresh = {k: spread_out(gathered[k], fresh[k]) for k in fresh}
+    lists = [[gathered[k][s] for s in range(half)] for k in range(count)]
+    last_after = state["after"]
+    if early:
+        last_after = [down(list(range(early)), lists[:early], state["after"])]
+    result = down(list(range(early, count)), lists[early:], last_after)
 
     back = lax.all_to_all(result.reshape(dp * fs, req, width), ("dp", "fsdp"), 0, 0, tiled=True)
     back = back.reshape(dp, fs, req, width).astype(F32)

time: 162 us -> 149 us (0.920)
  waiting for transfers between devices: 54.9 us -> 44.4 us
  starting transfers between devices: 33.4 us -> 38.2 us
  local copies, waits for them, and re-layouts: 8.57 us -> 4.27 us
    ppermute x21, waiting for transfers between devices: 41.8 us -> 24.1 us  [over_chips(): return lax.ppermute(x, 'dp', [(i, i ^ 2 * s) for i in range(dp)])]
    all_to_all x1, waiting for transfers between devices: 0.01 us -> 6.28 us  [local(): lax.all_to_all(payload.reshape(dp * fs, req, payload.shape[3]), ('dp', 'f...]
    ppermute x21, starting transfers between devices: 21.7 us -> 26.4 us  [over_chips(): return lax.ppermute(x, 'dp', [(i, i ^ 2 * s) for i in range(dp)])]
    unnamed x25 -> x21, local copies, waits for them, and re-layouts: 7.44 us -> 3.14 us
    ppermute x8, waiting for transfers between devices: 7.7 us -> 9.52 us  [swap(): return lax.ppermute(x, 'dp', [(i, i ^ 1) for i in range(dp)])]
    pallas_call x14 -> x15, Pallas kernels: 19.4 us -> 19.4 us  [the longest x2 12.2 us: down(): pl.pallas_call(functools.partial(down_kernel, half, [chunks[k] for k in n...]
  transfers between devices with their start and end apart: 33 -> 33, of which waited for: 22 -> 20; matrix products, arithmetic and copies ran while one was open for 3% -> 2% of each run, Pallas kernels for 18% -> 16%
where the time goes in v3:
time: 149 us
  Pallas kernels  46.5 us (31%)
  waiting for transfers between devices  44.4 us (30%)
  starting transfers between devices  38.2 us (26%)
  blocking collectives  12.7 us (9%)
  local copies, waits for them, and re-layouts  4.27 us (3%)
  other arithmetic  2.14 us (1%)
    ppermute x21, starting transfers between devices, over_chips(): return lax.ppermute(x, 'dp', [(i, i ^ 2 * s) for i in range(dp)])  26.4 us
    ppermute x21, waiting for transfers between devices, over_chips(): return lax.ppermute(x, 'dp', [(i, i ^ 2 * s) for i in range(dp)])  24.1 us
    pallas_call x3, Pallas kernels, gate(): pl.pallas_call(functools.partial(gate_kernel, len(parts) if first else 0,...  17.7 us
    all_to_all x1, blocking collectives, local(): lax.all_to_all(result.reshape(dp * fs, req, width), ('dp', 'fsdp'), 0, 0,...  12.7 us
    pallas_call x2, Pallas kernels, down(): pl.pallas_call(functools.partial(down_kernel, half, [chunks[k] for k in n...  12.2 us
    ppermute x8, waiting for transfers between devices, swap(): return lax.ppermute(x, 'dp', [(i, i ^ 1) for i in range(dp)])  9.52 us
    all_to_all x1, starting transfers between devices, local(): lax.all_to_all(payload.reshape(dp * fs, req, payload.shape[3]), ('dp', 'f...  7.3 us
    all_to_all x1, waiting for transfers between devices, local(): lax.all_to_all(payload.reshape(dp * fs, req, payload.shape[3]), ('dp', 'f...  6.28 us
  transfers between devices with their start and end apart: 33, of which 20 were waited for; matrix products, arithmetic and copies ran while one was open for 2% of the time, Pallas kernels for 16%

profile of v3, /device:TPU:0, one launch (start us, length us, event | category | flops | bytes accessed | tf_op | source)
XLA Modules:
  0.0 148.7 jit_solution(1768992081326636854)
XLA Ops:
  2.3 7.3 %all-to-all-start = ((bf16[32,8,384]{2,1,0:T(8,128)(2,1)}), bf16[32,8,384]{2,1,0:T(8,128)(2,1)S(1)}, u32[]{:S(2)}, u32[]{:S(2)}) async-start(bf16[32,8,384]{2,1,0:T(8,128)(2,1)} %bitcast.2), calls=%async_computation | async-start | bytes 393216 | tf_op jit(solution)/shard_map/all_to_all | solution.py:788
  10.4 2.2 %gate_tail.1._.refs_9_ = bf16[8,576,128]{2,1,0:T(8,128)(2,1)S(1)} custom-call(bf16[8,288,2,1440]{3,2,1,0:T(2,128)(2,1)} %refs_2_.3, bf16[8,4,8,384]{3,2,1,0:T(8,128)(2,1)} %pack.1._), custom_call_target="tpu_custom_call" | custom-call | flops 1 | bytes 1 | tf_op jit(solution)/shard_map/gate_tail/pallas_call | solution.py:494
  12.8 6.3 %all-to-all-done = bf16[32,8,384]{2,1,0:T(8,128)(2,1)S(1)} async-done(((bf16[32,8,384]{2,1,0:T(8,128)(2,1)}), bf16[32,8,384]{2,1,0:T(8,128)(2,1)S(1)}, u32[]{:S(2)}, u32[]{:S(2)}) %all-to-all-start) | async-done | bytes 196640 | tf_op jit(solution)/shard_map/all_to_all | solution.py:788
  24.5 2.2 %collective-permute-start.3 = (bf16[1,32,1536]{2,1,0:T(8,128)(2,1)S(1)}, bf16[1,32,1536]{2,1,0:T(8,128)(2,1)S(1)}, u32[]{:S(2)}, u32[]{:S(2)}) collective-permute-start(bf16[1,32,1536]{2,1,0:T(8,128)(2,1)S(1)} %get-tuple-element.51), channel_id=1, source_target_pairs={{0,24},{4,28},{8,16},{12,20},{16,8},{20,12},{24,0},{28,4},{1,25},{... | collective-permute-start | bytes 294920 | tf_op jit(solution)/shard_map/ppermute | solution.py:782
  28.7 2.3 %copy-done.1 = bf16[144,16,2,512]{3,2,1,0:T(2,128)(2,1)S(1)} copy-done((bf16[144,16,2,512]{3,2,1,0:T(2,128)(2,1)S(1)}, bf16[144,16,2,512]{3,2,1,0:T(2,128)(2,1)}, u32[]{:S(2)}) %copy-start.1) | copy-done | bytes 4718616
  31.1 3.5 %pool_split.1 = (bf16[2304,512]{1,0:T(8,128)(2,1)S(1)}, bf16[2304,512]{1,0:T(8,128)(2,1)S(1)}, f32[32,2304]{1,0:T(8,128)S(1)}) custom-call(s32[4,4]{1,0:T(4,128)S(1)} %copy-done.4, s32[32,6]{1,0:T(8,128)S(1)} %copy.34.lists_ref, bf16[144,16,2,512]{3,2,1,0:T(2,128)(2,1)S(1)} %copy-done.1, f32[256,128]{1,0:T(8,128)S(1)} %get-tuple-element.52._.refs_9_.refs_12_), custom_call_target="tpu_custom_call" | custom-call | flops 1 | bytes 1 | tf_op jit(solution)/shard_map/pool_split/pallas_call | solution.py:223
  34.6 2.3 %attention.1.refs_0_ = bf16[32,512]{1,0:T(8,128)(2,1)S(1)} custom-call(bf16[1,32,1536]{2,1,0:T(8,128)(2,1)S(1)} %get-tuple-element.46._.refs_0_, bf16[1,32,1536]{2,1,0:T(8,128)(2,1)S(1)} %collective-permute-done.1.refs_1_, bf16[1,32,1536]{2,1,0:T(8,128)(2,1)S(1)} %collective-permute-done.2.refs_2_, bf16[1,32,1536]{2,1,0:T(8,128)(2,1)S(1)} %collective-permute-done.3.refs_3_, ...), custom_call_target="tpu_custom_call" | custom-call | flops 1 | bytes 1 | tf_op jit(solution)/shard_map/attention/pallas_call | solution.py:328
  39.2 2.2 %collective-permute-start.6 = (bf16[32,512]{1,0:T(8,128)(2,1)S(1)}, bf16[32,512]{1,0:T(8,128)(2,1)S(1)}, u32[]{:S(2)}, u32[]{:S(2)}) collective-permute-start(bf16[32,512]{1,0:T(8,128)(2,1)S(1)} %attention.1.refs_0_), channel_id=1, source_target_pairs={{0,24},{4,28},{8,16},{12,20},{16,8},{20,12},{24,0},{28,4},{1,25},{... | collective-permute-start | bytes 98312 | tf_op jit(solution)/shard_map/ppermute | solution.py:782
  48.0 2.2 %collective-permute-start.10 = (bf16[288,256]{1,0:T(8,128)(2,1)S(1)}, bf16[288,256]{1,0:T(8,128)(2,1)S(1)}, u32[]{:S(2)}, u32[]{:S(2)}) collective-permute-start(bf16[288,256]{1,0:T(8,128)(2,1)S(1)} %out_projection.1.refs_1_), channel_id=1, source_target_pairs={{0,3},{1,2},{2,1},{3,0},{4,7},{5,6},{6,5},{7,4},{8,11},{9,10},{10,... | collective-permute-start | bytes 442376 | tf_op jit(solution)/shard_map/ppermute | solution.py:785
  51.3 2.1 %collective-permute-done.8.refs_2_ = bf16[288,256]{1,0:T(8,128)(2,1)S(1)} collective-permute-done((bf16[288,256]{1,0:T(8,128)(2,1)S(1)}, bf16[288,256]{1,0:T(8,128)(2,1)S(1)}, u32[]{:S(2)}, u32[]{:S(2)}) %collective-permute-start.8) | collective-permute-done | bytes 147488 | tf_op jit(solution)/shard_map/ppermute | solution.py:785
  53.4 2.4 %collective-permute-done.9.refs_3_ = bf16[288,256]{1,0:T(8,128)(2,1)S(1)} collective-permute-done((bf16[288,256]{1,0:T(8,128)(2,1)S(1)}, bf16[288,256]{1,0:T(8,128)(2,1)S(1)}, u32[]{:S(2)}, u32[]{:S(2)}) %collective-permute-start.9) | collective-permute-done | bytes 147488 | tf_op jit(solution)/shard_map/ppermute | solution.py:785
  55.8 7.3 %gate_up_0.1 = (bf16[4,64,896]{2,1,0:T(8,128)(2,1)S(1)}, bf16[4,64,896]{2,1,0:T(8,128)(2,1)S(1)}, f32[288,256]{1,0:T(8,128)S(1)}, bf16[2,512,576]{2,1,0:T(8,128)(2,1)S(1)}) custom-call(s32[9]{0:T(128)S(1)} %get-tuple-element.47.offset_ref, s32[8]{0:T(128)S(1)} %pad_add_fusion.1.order_ref, f32[8,256]{1,0:T(8,128)S(1)} %get-tuple-element.48.refs_0_.refs_8_, ...), custom_call_target="tpu_custom_call" | custom-call | flops 1 | bytes 1 | tf_op jit(solution)/shard_map/gate_up_0/pallas_call | solution.py:865
  65.8 5.2 %gate_up_1.1 = (bf16[4,64,1024]{2,1,0:T(8,128)(2,1)S(1)}, bf16[4,64,1024]{2,1,0:T(8,128)(2,1)S(1)}) custom-call(s32[9]{0:T(128)S(1)} %get-tuple-element.47.offset_ref, s32[8]{0:T(128)S(1)} %pad_add_fusion.1.order_ref, bf16[2,64,896]{2,1,0:T(8,128)(2,1)S(1)} %get-tuple-element.59.refs_0_.keep_ref, bf16[2,512,576]{2,1,0:T(8,128)(2,1)S(1)} %get-tuple-element.60.refs_1_, ...), custom_call_target="tpu_custom_call" | custom-call | flops 1 | bytes 1 | tf_op jit(solution)/shard_map/gate_up_1/pallas_call | solution.py:865
  71.0 2.4 %collective-permute-done.12.recv_ref.outs_1_ = bf16[2,64,896]{2,1,0:T(8,128)(2,1)S(1)} collective-permute-done((bf16[2,64,896]{2,1,0:T(8,128)(2,1)S(1)}, bf16[2,64,896]{2,1,0:T(8,128)(2,1)S(1)}, u32[]{:S(2)}, u32[]{:S(2)}) %collective-permute-start.12) | collective-permute-done | bytes 229408 | tf_op jit(solution)/shard_map/ppermute | solution.py:782
  76.3 2.5 %collective-permute-start.15 = (bf16[1,64,896]{2,1,0:T(8,128)(2,1)S(1)}, bf16[1,64,896]{2,1,0:T(8,128)(2,1)S(1)}, u32[]{:S(2)}, u32[]{:S(2)}) collective-permute-start(bf16[1,64,896]{2,1,0:T(8,128)(2,1)S(1)} %get-tuple-element.68), channel_id=1, source_target_pairs={{0,16},{4,20},{8,24},{12,28},{16,0},{20,4},{24,8},{28,12},{1,17},{... | collective-permute-start | bytes 344072 | tf_op jit(solution)/shard_map/ppermute | solution.py:782
  78.8 5.2 %gate_up_2.1 = (bf16[4,64,1024]{2,1,0:T(8,128)(2,1)S(1)}, bf16[4,64,1024]{2,1,0:T(8,128)(2,1)S(1)}) custom-call(s32[9]{0:T(128)S(1)} %get-tuple-element.47.offset_ref, s32[8]{0:T(128)S(1)} %pad_add_fusion.1.order_ref, bf16[2,64,1024]{2,1,0:T(8,128)(2,1)S(1)} %get-tuple-element.66.refs_0_.keep_ref, bf16[2,512,576]{2,1,0:T(8,128)(2,1)S(1)} %get-tuple-element.60.refs_1_, ...), custom_call_target="tpu_custom_call" | custom-call | flops 1 | bytes 1 | tf_op jit(solution)/shard_map/gate_up_2/pallas_call | solution.py:865
  84.6 2.2 %collective-permute-done.14.refs_4_.recv_ref = bf16[2,64,1024]{2,1,0:T(8,128)(2,1)S(1)} collective-permute-done((bf16[2,64,1024]{2,1,0:T(8,128)(2,1)S(1)}, bf16[2,64,1024]{2,1,0:T(8,128)(2,1)S(1)}, u32[]{:S(2)}, u32[]{:S(2)}) %collective-permute-start.14) | collective-permute-done | bytes 262176 | tf_op jit(solution)/shard_map/ppermute | solution.py:782
  94.2 9.0 %collective-permute-done.18.refs_4_.refs_1_ = bf16[64,512]{1,0:T(8,128)(2,1)S(1)} collective-permute-done((bf16[64,512]{1,0:T(8,128)(2,1)S(1)}, bf16[64,512]{1,0:T(8,128)(2,1)S(1)}, u32[]{:S(2)}, u32[]{:S(2)}) %collective-permute-start.18) | collective-permute-done | bytes 65568 | tf_op jit(solution)/shard_map/ppermute | solution.py:782
  103.5 2.0 %collective-permute-start.24 = (bf16[1,64,1024]{2,1,0:T(8,128)(2,1)S(1)}, bf16[1,64,1024]{2,1,0:T(8,128)(2,1)S(1)}, u32[]{:S(2)}, u32[]{:S(2)}) collective-permute-start(bf16[1,64,1024]{2,1,0:T(8,128)(2,1)S(1)} %get-tuple-element.79), channel_id=1, source_target_pairs={{0,16},{4,20},{8,24},{12,28},{16,0},{20,4},{24,8},{28,12},{1,17},{... | collective-permute-start | bytes 393224 | tf_op jit(solution)/shard_map/ppermute | solution.py:782
  111.2 3.6 %collective-permute-done.22.refs_5_.refs_2_ = bf16[64,512]{1,0:T(8,128)(2,1)S(1)} collective-permute-done((bf16[64,512]{1,0:T(8,128)(2,1)S(1)}, bf16[64,512]{1,0:T(8,128)(2,1)S(1)}, u32[]{:S(2)}, u32[]{:S(2)}) %collective-permute-start.22) | collective-permute-done | bytes 65568 | tf_op jit(solution)/shard_map/ppermute | solution.py:782
  115.3 2.0 %collective-permute-start.26 = (bf16[64,512]{1,0:T(8,128)(2,1)S(1)}, bf16[64,512]{1,0:T(8,128)(2,1)S(1)}, u32[]{:S(2)}, u32[]{:S(2)}) collective-permute-start(bf16[64,512]{1,0:T(8,128)(2,1)S(1)} %activation_2.1.refs_4_.refs_5_), channel_id=1, source_target_pairs={{0,8},{4,12},{8,0},{12,4},{16,24},{20,28},{24,16},{28,20},{1,9},{5... | collective-permute-start | bytes 196616 | tf_op jit(solution)/shard_map/ppermute | solution.py:782
  119.8 4.6 %down_0.1.refs_8_.refs_11_ = f32[288,512]{1,0:T(8,128)S(1)} custom-call(s32[9]{0:T(128)S(1)} %get-tuple-element.47.offset_ref, s32[8]{0:T(128)S(1)} %pad_add_fusion.1.order_ref, bf16[64,512]{1,0:T(8,128)(2,1)S(1)} %get-tuple-element.70.outs_0_.refs_0_, bf16[64,512]{1,0:T(8,128)(2,1)S(1)} %collective-permute-done.18.refs_4_.refs_1_, ...), custom_call_target="tpu_custom_call" | custom-call | flops 1 | bytes 1 | tf_op jit(solution)/shard_map/down_0/pallas_call | solution.py:937
  127.6 7.6 %down_1.1 = bf16[256,288]{1,0:T(8,128)(2,1)S(1)} custom-call(s32[9]{0:T(128)S(1)} %get-tuple-element.47.offset_ref, s32[8]{0:T(128)S(1)} %pad_add_fusion.1.order_ref, bf16[64,512]{1,0:T(8,128)(2,1)S(1)} %activation_1.1.outs_0_.refs_0_, bf16[64,512]{1,0:T(8,128)(2,1)S(1)} %collective-permute-done.21.refs_4_.refs_1_, ...), custom_call_target="tpu_custom_call" | custom-call | flops 1 | bytes 1 | tf_op jit(solution)/shard_map/down_1/pallas_call | solution.py:937
  135.2 12.7 %all_to_all.10 = bf16[32,8,288]{2,1,0:T(8,128)(2,1)S(1)} all-to-all(bf16[32,8,288]{2,1,0:T(8,128)(2,1)S(1)} %bitcast.19), channel_id=1, replica_groups=mesh['dp'=8,'fsdp'=4] {'dp','fsdp'}, dimensions={0} | all-to-all | bytes 294912 | tf_op jit(solution)/shard_map/all_to_all | solution.py:997
  (108 shorter events, 46.8 us)
Async XLA Ops:
  2.3 16.8 %all-to-all-start = ((bf16[32,8,384]{2,1,0:T(8,128)(2,1)}), bf16[32,8,384]{2,1,0:T(8,128)(2,1)S(1)}, u32[]{:S(2)}, u32[]{:S(2)}) async-start(bf16[32,8,384]{2,1,0:T(8,128)(2,1)} %bitcast.2), calls=%async_computation | async-start | bytes 393216 | tf_op jit(solution)/shard_map/all_to_all | solution.py:788
  22.2 12.4 %collective-permute-start.1 = (bf16[1,32,1536]{2,1,0:T(8,128)(2,1)S(1)}, bf16[1,32,1536]{2,1,0:T(8,128)(2,1)S(1)}, u32[]{:S(2)}, u32[]{:S(2)}) collective-permute-start(bf16[1,32,1536]{2,1,0:T(8,128)(2,1)S(1)} %get-tuple-element.49), channel_id=1, source_target_pairs={{0,8},{4,12},{8,0},{12,4},{16,24},{20,28},{24,16},{28,20},{1,9},{5... | collective-permute-start | bytes 294920 | tf_op jit(solution)/shard_map/ppermute | solution.py:782
  23.1 11.5 %collective-permute-start.2 = (bf16[1,32,1536]{2,1,0:T(8,128)(2,1)S(1)}, bf16[1,32,1536]{2,1,0:T(8,128)(2,1)S(1)}, u32[]{:S(2)}, u32[]{:S(2)}) collective-permute-start(bf16[1,32,1536]{2,1,0:T(8,128)(2,1)S(1)} %get-tuple-element.50), channel_id=1, source_target_pairs={{0,16},{4,20},{8,24},{12,28},{16,0},{20,4},{24,8},{28,12},{1,17},{... | collective-permute-start | bytes 294920 | tf_op jit(solution)/shard_map/ppermute | solution.py:782
  24.5 10.1 %collective-permute-start.3 = (bf16[1,32,1536]{2,1,0:T(8,128)(2,1)S(1)}, bf16[1,32,1536]{2,1,0:T(8,128)(2,1)S(1)}, u32[]{:S(2)}, u32[]{:S(2)}) collective-permute-start(bf16[1,32,1536]{2,1,0:T(8,128)(2,1)S(1)} %get-tuple-element.51), channel_id=1, source_target_pairs={{0,24},{4,28},{8,16},{12,20},{16,8},{20,12},{24,0},{28,4},{1,25},{... | collective-permute-start | bytes 294920 | tf_op jit(solution)/shard_map/ppermute | solution.py:782
  37.8 5.5 %collective-permute-start.5 = (bf16[32,512]{1,0:T(8,128)(2,1)S(1)}, bf16[32,512]{1,0:T(8,128)(2,1)S(1)}, u32[]{:S(2)}, u32[]{:S(2)}) collective-permute-start(bf16[32,512]{1,0:T(8,128)(2,1)S(1)} %attention.1.refs_0_), channel_id=1, source_target_pairs={{0,16},{4,20},{8,24},{12,28},{16,0},{20,4},{24,8},{28,12},{1,17},{... | collective-permute-start | bytes 98312 | tf_op jit(solution)/shard_map/ppermute | solution.py:782
  39.2 5.7 %collective-permute-start.6 = (bf16[32,512]{1,0:T(8,128)(2,1)S(1)}, bf16[32,512]{1,0:T(8,128)(2,1)S(1)}, u32[]{:S(2)}, u32[]{:S(2)}) collective-permute-start(bf16[32,512]{1,0:T(8,128)(2,1)S(1)} %attention.1.refs_0_), channel_id=1, source_target_pairs={{0,24},{4,28},{8,16},{12,20},{16,8},{20,12},{24,0},{28,4},{1,25},{... | collective-permute-start | bytes 98312 | tf_op jit(solution)/shard_map/ppermute | solution.py:782
  46.6 6.8 %collective-permute-start.8 = (bf16[288,256]{1,0:T(8,128)(2,1)S(1)}, bf16[288,256]{1,0:T(8,128)(2,1)S(1)}, u32[]{:S(2)}, u32[]{:S(2)}) collective-permute-start(bf16[288,256]{1,0:T(8,128)(2,1)S(1)} %out_projection.1.refs_1_), channel_id=1, source_target_pairs={{0,1},{1,0},{2,3},{3,2},{4,5},{5,4},{6,7},{7,6},{8,9},{9,8},{10,11... | collective-permute-start | bytes 442376 | tf_op jit(solution)/shard_map/ppermute | solution.py:785
  46.8 9.1 %collective-permute-start.9 = (bf16[288,256]{1,0:T(8,128)(2,1)S(1)}, bf16[288,256]{1,0:T(8,128)(2,1)S(1)}, u32[]{:S(2)}, u32[]{:S(2)}) collective-permute-start(bf16[288,256]{1,0:T(8,128)(2,1)S(1)} %out_projection.1.refs_1_), channel_id=1, source_target_pairs={{0,2},{1,3},{2,0},{3,1},{4,6},{5,7},{6,4},{7,5},{8,10},{9,11},{10,... | collective-permute-start | bytes 442376 | tf_op jit(solution)/shard_map/ppermute | solution.py:785
  48.0 7.9 %collective-permute-start.10 = (bf16[288,256]{1,0:T(8,128)(2,1)S(1)}, bf16[288,256]{1,0:T(8,128)(2,1)S(1)}, u32[]{:S(2)}, u32[]{:S(2)}) collective-permute-start(bf16[288,256]{1,0:T(8,128)(2,1)S(1)} %out_projection.1.refs_1_), channel_id=1, source_target_pairs={{0,3},{1,2},{2,1},{3,0},{4,7},{5,6},{6,5},{7,4},{8,11},{9,10},{10,... | collective-permute-start | bytes 442376 | tf_op jit(solution)/shard_map/ppermute | solution.py:785
  65.7 7.7 %collective-permute-start.12 = (bf16[2,64,896]{2,1,0:T(8,128)(2,1)S(1)}, bf16[2,64,896]{2,1,0:T(8,128)(2,1)S(1)}, u32[]{:S(2)}, u32[]{:S(2)}) collective-permute-start(bf16[2,64,896]{2,1,0:T(8,128)(2,1)S(1)} %get-tuple-element.62), channel_id=1, source_target_pairs={{0,8},{4,12},{8,0},{12,4},{16,24},{20,28},{24,16},{28,20},{1,9},{5... | collective-permute-start | bytes 688136 | tf_op jit(solution)/shard_map/ppermute | solution.py:782
  75.9 10.9 %collective-permute-start.14 = (bf16[2,64,1024]{2,1,0:T(8,128)(2,1)S(1)}, bf16[2,64,1024]{2,1,0:T(8,128)(2,1)S(1)}, u32[]{:S(2)}, u32[]{:S(2)}) collective-permute-start(bf16[2,64,1024]{2,1,0:T(8,128)(2,1)S(1)} %get-tuple-element.67), channel_id=1, source_target_pairs={{0,8},{4,12},{8,0},{12,4},{16,24},{20,28},{24,16},{28,20},{1,9},{5... | collective-permute-start | bytes 786440 | tf_op jit(solution)/shard_map/ppermute | solution.py:782
  76.3 8.3 %collective-permute-start.15 = (bf16[1,64,896]{2,1,0:T(8,128)(2,1)S(1)}, bf16[1,64,896]{2,1,0:T(8,128)(2,1)S(1)}, u32[]{:S(2)}, u32[]{:S(2)}) collective-permute-start(bf16[1,64,896]{2,1,0:T(8,128)(2,1)S(1)} %get-tuple-element.68), channel_id=1, source_target_pairs={{0,16},{4,20},{8,24},{12,28},{16,0},{20,4},{24,8},{28,12},{1,17},{... | collective-permute-start | bytes 344072 | tf_op jit(solution)/shard_map/ppermute | solution.py:782
  89.2 14.0 %collective-permute-start.20 = (bf16[2,64,1024]{2,1,0:T(8,128)(2,1)S(1)}, bf16[2,64,1024]{2,1,0:T(8,128)(2,1)S(1)}, u32[]{:S(2)}, u32[]{:S(2)}) collective-permute-start(bf16[2,64,1024]{2,1,0:T(8,128)(2,1)S(1)} %get-tuple-element.77), channel_id=1, source_target_pairs={{0,8},{4,12},{8,0},{12,4},{16,24},{20,28},{24,16},{28,20},{1,9},{5... | collective-permute-start | bytes 786440 | tf_op jit(solution)/shard_map/ppermute | solution.py:782
  90.3 12.9 %collective-permute-start.16 = (bf16[1,64,1024]{2,1,0:T(8,128)(2,1)S(1)}, bf16[1,64,1024]{2,1,0:T(8,128)(2,1)S(1)}, u32[]{:S(2)}, u32[]{:S(2)}) collective-permute-start(bf16[1,64,1024]{2,1,0:T(8,128)(2,1)S(1)} %get-tuple-element.73), channel_id=1, source_target_pairs={{0,16},{4,20},{8,24},{12,28},{16,0},{20,4},{24,8},{28,12},{1,17},{... | collective-permute-start | bytes 393224 | tf_op jit(solution)/shard_map/ppermute | solution.py:782
  92.1 11.2 %collective-permute-start.18 = (bf16[64,512]{1,0:T(8,128)(2,1)S(1)}, bf16[64,512]{1,0:T(8,128)(2,1)S(1)}, u32[]{:S(2)}, u32[]{:S(2)}) collective-permute-start(bf16[64,512]{1,0:T(8,128)(2,1)S(1)} %get-tuple-element.70.outs_0_.refs_0_), channel_id=1, source_target_pairs={{0,8},{4,12},{8,0},{12,4},{16,24},{20,28},{24,16},{28,20},{1,9},{5... | collective-permute-start | bytes 196616 | tf_op jit(solution)/shard_map/ppermute | solution.py:782
  92.5 10.8 %collective-permute-start.19 = (bf16[64,512]{1,0:T(8,128)(2,1)S(1)}, bf16[64,512]{1,0:T(8,128)(2,1)S(1)}, u32[]{:S(2)}, u32[]{:S(2)}) collective-permute-start(bf16[64,512]{1,0:T(8,128)(2,1)S(1)} %get-tuple-element.70.outs_0_.refs_0_), channel_id=1, source_target_pairs={{0,16},{4,20},{8,24},{12,28},{16,0},{20,4},{24,8},{28,12},{1,17},{... | collective-permute-start | bytes 196616 | tf_op jit(solution)/shard_map/ppermute | solution.py:782
  103.5 11.3 %collective-permute-start.24 = (bf16[1,64,1024]{2,1,0:T(8,128)(2,1)S(1)}, bf16[1,64,1024]{2,1,0:T(8,128)(2,1)S(1)}, u32[]{:S(2)}, u32[]{:S(2)}) collective-permute-start(bf16[1,64,1024]{2,1,0:T(8,128)(2,1)S(1)} %get-tuple-element.79), channel_id=1, source_target_pairs={{0,16},{4,20},{8,24},{12,28},{16,0},{20,4},{24,8},{28,12},{1,17},{... | collective-permute-start | bytes 393224 | tf_op jit(solution)/shard_map/ppermute | solution.py:782
  105.5 5.0 %collective-permute-start.25 = (bf16[64,512]{1,0:T(8,128)(2,1)S(1)}, bf16[64,512]{1,0:T(8,128)(2,1)S(1)}, u32[]{:S(2)}, u32[]{:S(2)}) collective-permute-start(bf16[64,512]{1,0:T(8,128)(2,1)S(1)} %collective-permute-done.19.refs_5_.refs_2_), channel_id=1, source_target_pairs={{0,8},{4,12},{8,0},{12,4},{16,24},{20,28},{24,16},{28,20},{1,9},{5... | collective-permute-start | bytes 196616 | tf_op jit(solution)/shard_map/ppermute | solution.py:782
  106.3 4.9 %collective-permute-start.21 = (bf16[64,512]{1,0:T(8,128)(2,1)S(1)}, bf16[64,512]{1,0:T(8,128)(2,1)S(1)}, u32[]{:S(2)}, u32[]{:S(2)}) collective-permute-start(bf16[64,512]{1,0:T(8,128)(2,1)S(1)} %activation_1.1.outs_0_.refs_0_), channel_id=1, source_target_pairs={{0,8},{4,12},{8,0},{12,4},{16,24},{20,28},{24,16},{28,20},{1,9},{5... | collective-permute-start | bytes 196616 | tf_op jit(solution)/shard_map/ppermute | solution.py:782
  107.5 7.3 %collective-permute-start.22 = (bf16[64,512]{1,0:T(8,128)(2,1)S(1)}, bf16[64,512]{1,0:T(8,128)(2,1)S(1)}, u32[]{:S(2)}, u32[]{:S(2)}) collective-permute-start(bf16[64,512]{1,0:T(8,128)(2,1)S(1)} %activation_1.1.outs_0_.refs_0_), channel_id=1, source_target_pairs={{0,16},{4,20},{8,24},{12,28},{16,0},{20,4},{24,8},{28,12},{1,17},{... | collective-permute-start | bytes 196616 | tf_op jit(solution)/shard_map/ppermute | solution.py:782
  115.2 9.2 %collective-permute-start.23 = (bf16[64,512]{1,0:T(8,128)(2,1)S(1)}, bf16[64,512]{1,0:T(8,128)(2,1)S(1)}, u32[]{:S(2)}, u32[]{:S(2)}) collective-permute-start(bf16[64,512]{1,0:T(8,128)(2,1)S(1)} %collective-permute-done.22.refs_5_.refs_2_), channel_id=1, source_target_pairs={{0,8},{4,12},{8,0},{12,4},{16,24},{20,28},{24,16},{28,20},{1,9},{5... | collective-permute-start | bytes 196616 | tf_op jit(solution)/shard_map/ppermute | solution.py:782
  115.3 9.1 %collective-permute-start.26 = (bf16[64,512]{1,0:T(8,128)(2,1)S(1)}, bf16[64,512]{1,0:T(8,128)(2,1)S(1)}, u32[]{:S(2)}, u32[]{:S(2)}) collective-permute-start(bf16[64,512]{1,0:T(8,128)(2,1)S(1)} %activation_2.1.refs_4_.refs_5_), channel_id=1, source_target_pairs={{0,8},{4,12},{8,0},{12,4},{16,24},{20,28},{24,16},{28,20},{1,9},{5... | collective-permute-start | bytes 196616 | tf_op jit(solution)/shard_map/ppermute | solution.py:782
  117.3 8.2 %collective-permute-start.27 = (bf16[64,512]{1,0:T(8,128)(2,1)S(1)}, bf16[64,512]{1,0:T(8,128)(2,1)S(1)}, u32[]{:S(2)}, u32[]{:S(2)}) collective-permute-start(bf16[64,512]{1,0:T(8,128)(2,1)S(1)} %activation_2.1.refs_4_.refs_5_), channel_id=1, source_target_pairs={{0,16},{4,20},{8,24},{12,28},{16,0},{20,4},{24,8},{28,12},{1,17},{... | collective-permute-start | bytes 196616 | tf_op jit(solution)/shard_map/ppermute | solution.py:782
  118.1 7.4 %collective-permute-start.28 = (bf16[64,512]{1,0:T(8,128)(2,1)S(1)}, bf16[64,512]{1,0:T(8,128)(2,1)S(1)}, u32[]{:S(2)}, u32[]{:S(2)}) collective-permute-start(bf16[64,512]{1,0:T(8,128)(2,1)S(1)} %activation_2.1.refs_4_.refs_5_), channel_id=1, source_target_pairs={{0,24},{4,28},{8,16},{12,20},{16,8},{20,12},{24,0},{28,4},{1,25},{... | collective-permute-start | bytes 196616 | tf_op jit(solution)/shard_map/ppermute | solution.py:782
  (19 other events, 129.3 us)

commit v4 on v3

--- a/solution.py
+++ b/solution.py
@@ -55,7 +55,15 @@
 SCALARS = pl.BlockSpec(memory_space=pltpu.SMEM)
 
 
-def pack_kernel(hidden_ref, routes_ref, out_ref):
+def pack_kernel(hidden_hbm, routes_hbm, out_ref, hidden_ref, routes_ref, sems):
+    copies = [
+        pltpu.make_async_copy(hidden_hbm, hidden_ref, sems.at[0]),
+        pltpu.make_async_copy(routes_hbm, routes_ref, sems.at[1]),
+    ]
+    for copy in copies:
+        copy.start()
+    for copy in copies:
+        copy.wait()
     slices, copies, req, room = out_ref.shape
     features = hidden_ref.shape[1]
     width = features // slices
@@ -83,8 +91,13 @@
     out = (slices, copies, req, room)
     return pl.pallas_call(
         pack_kernel,
-        in_specs=[full_spec(hidden_in.shape), full_spec(routes.shape)],
+        in_specs=[pl.BlockSpec(memory_space=pl.ANY)] * 2,
         out_specs=full_spec(out),
+        scratch_shapes=[
+            pltpu.VMEM(hidden_in.shape, BF16),
+            pltpu.VMEM(routes.shape, jnp.int32),
+            pltpu.SemaphoreType.DMA((2,)),
+        ],
         out_shape=jax.ShapeDtypeStruct(out, BF16),
         compiler_params=params(),
         cost_estimate=pl.CostEstimate(flops=1, bytes_accessed=1, transcendentals=0),
@@ -424,38 +437,40 @@
     if first:
         parts, refs = refs[:count_parts], refs[count_parts:]
         hid_ref, norm_ref, router_ref, line_ref, tail_ref, w_ref = refs[:6]
-        keep_ref, send_ref, resid_ref, spread_ref, held, aux, w_held, w_sems, tail_held, tail_sem = refs[6:]
+        keep_ref, send_ref, resid_ref, spread_ref, held, aux = refs[6:]
     else:
         spread_ref, w_ref, keep_ref, send_ref, held, w_held, w_sems = refs
     experts = w_ref.shape[0]
     pairs = spread_ref.shape[1]
     width = spread_ref.shape[2] // 2
-    copies = [
-        pltpu.make_async_copy(w_ref.at[e, :, :, pl.ds(begin, columns)], w_held.at[e % SLOTS], w_sems.at[e % SLOTS])
-        for e in range(experts)
-    ]
-    for copy in copies[:SLOTS]:
-        copy.start()
     if first:
         tail_width, _, aux_at, size = tail
-        tail_copy = pltpu.make_async_copy(tail_ref, tail_held, tail_sem)
-        tail_copy.start()
         dispatch(parts, hid_ref, norm_ref, router_ref, line_ref, resid_ref, spread_ref, aux, aux_at % LANES)
-        tail_copy.wait()
+    else:
+        copies = [
+            pltpu.make_async_copy(w_ref.at[e, :, :, pl.ds(begin, columns)], w_held.at[e % SLOTS], w_sems.at[e % SLOTS])
+            for e in range(experts)
+        ]
+        for copy in copies[:SLOTS]:
+            copy.start()
 
     for expert in range(experts):
         rows, valid = window_of(offset_ref, expert, pairs, window)
         left = jnp.concatenate([spread_ref[0, rows], spread_ref[1, rows]], axis=0)
-        copies[expert].wait()
-        result = dot_nn(left, w_held[expert % SLOTS].reshape(2 * width, columns)).astype(BF16)
-        if expert + SLOTS < experts:
+        if first:
+            weights = w_ref[expert]
+        else:
+            copies[expert].wait()
+            weights = w_held[expert % SLOTS]
+        result = dot_nn(left, weights.reshape(2 * width, columns)).astype(BF16)
+        if not first and expert + SLOTS < experts:
             copies[expert + SLOTS].start()
         held[rows, :columns] = jnp.where(valid, result[:window], held[rows, :columns])
         held[rows, columns : 2 * columns] = jnp.where(
             valid, result[window:], held[rows, columns : 2 * columns]
         )
         if first:
-            result = dot_nn(left, tail_held[expert])
+            result = dot_nn(left, tail_ref[expert])
             lane = lax.broadcasted_iota(jnp.int32, (window, LANES), 1)
             gate, up = result[:window], result[window:]
             if tail_width == LANES:
@@ -474,35 +489,74 @@
         send_ref[slot] = held[other]
 
 
-def gate_tail_kernel(size, gate_ref, _, out_ref):
+def gate_tail_kernel(size, gate_ref, _, out_ref, token_ref):
+    token_ref[...] = jnp.zeros_like(token_ref)
     experts, width, _, lanes = gate_ref.shape
     lane = lax.broadcasted_iota(jnp.int32, (2 * width, lanes), 1)
     for e in range(experts):
         out_ref[e] = jnp.where(lane < size, gate_ref[e].reshape(2 * width, lanes).astype(F32), 0.0).astype(BF16)
 
 
-def down_tail_kernel(size, down_ref, _, out_ref):
-    lane = lax.broadcasted_iota(jnp.int32, down_ref.shape[1:], 1)
-    for e in range(down_ref.shape[0]):
-        out_ref[e] = jnp.where(lane < size, down_ref[e].astype(F32), 0.0).astype(BF16)
-
-
-def last_units(weights, after, kernel, rows, name):
-    number, size = weights.shape[-1] // LANES, weights.shape[-1] % LANES
-    lead = weights.shape[:-1]
-    out = (weights.shape[0], rows, LANES)
+def last_units(weights, after):
+    experts, width, _, units = weights.shape
+    number, size = units // LANES, units % LANES
+    out = (experts, 2 * width, LANES)
     return pl.pallas_call(
-        functools.partial(kernel, size),
+        functools.partial(gate_tail_kernel, size),
         grid=(1,),
         in_specs=[
-            pl.BlockSpec((*lead, LANES), lambda *_: (0,) * len(lead) + (number,)),
+            pl.BlockSpec((experts, width, 2, LANES), lambda *_: (0, 0, 0, number)),
             pl.BlockSpec(memory_space=pl.ANY),
         ],
-        out_specs=block_spec(out),
-        out_shape=jax.ShapeDtypeStruct(out, BF16),
+        out_specs=[block_spec(out), block_spec((8, LANES))],
+        out_shape=[pltpu.HBM(out, BF16), jax.ShapeDtypeStruct((8, LANES), F32)],
         compiler_params=params(),
         cost_estimate=pl.CostEstimate(flops=1, bytes_accessed=1, transcendentals=0),
-        name=name,
+        name="gate_tail",
+    )(weights, after)
+
+
+def stage_gate_kernel(begin, columns, w_ref, tail_ref, _, out_ref, tail_out, sems):
+    copies = [
+        pltpu.make_async_copy(w_ref.at[:, :, :, pl.ds(begin, columns)], out_ref, sems.at[0]),
+        pltpu.make_async_copy(tail_ref, tail_out, sems.at[1]),
+    ]
+    for copy in copies:
+        copy.start()
+    for copy in copies:
+        copy.wait()
+
+
+def stage_gate(gate_up, tail, begin, columns, after):
+    anywhere = pl.BlockSpec(memory_space=pl.ANY)
+    return pl.pallas_call(
+        functools.partial(stage_gate_kernel, begin, columns),
+        in_specs=[anywhere] * 3,
+        out_specs=[anywhere] * 2,
+        out_shape=[pltpu.VMEM((*gate_up.shape[:3], columns), BF16), pltpu.VMEM(tail.shape, BF16)],
+        scratch_shapes=[pltpu.SemaphoreType.DMA((2,))],
+        compiler_params=params(),
+        cost_estimate=pl.CostEstimate(flops=1, bytes_accessed=1, transcendentals=0),
+        name="stage_gate",
+    )(gate_up, tail, after)
+
+
+def stage_down_kernel(w_ref, _, out_ref, sem):
+    copy = pltpu.make_async_copy(w_ref, out_ref, sem)
+    copy.start()
+    copy.wait()
+
+
+def stage_down(weights, after):
+    return pl.pallas_call(
+        stage_down_kernel,
+        in_specs=[pl.BlockSpec(memory_space=pl.ANY)] * 2,
+        out_specs=pl.BlockSpec(memory_space=pl.ANY),
+        out_shape=pltpu.VMEM(weights.shape, BF16),
+        scratch_shapes=[pltpu.SemaphoreType.DMA],
+        compiler_params=params(),
+        cost_estimate=pl.CostEstimate(flops=1, bytes_accessed=1, transcendentals=0),
+        name="stage_down",
     )(weights, after)
 
 
@@ -635,34 +689,20 @@
     return pl.ds(start, window), (lanes >= first) & (lanes < offset_ref[expert + 1])
 
 
-def down_kernel(half, chunks, tail, window, begins, ends, waits, offset_ref, order_ref, *refs):
-    refs = refs[waits:]
+def down_kernel(half, chunks, tail, window, begins, ends, offset_ref, order_ref, *refs):
     gathered = []
     for _ in chunks:
         gathered.append((refs[:half], refs[half]))
         refs = refs[half + 1 :]
     w_ref, refs = refs[0], refs[1:]
-    if tail:
-        tail_ref, refs = refs[0], refs[1:]
     if not begins:
         before_ref, refs = refs[0], refs[1:]
     if ends:
-        place_ref, resid_ref, out_ref, total_ref, *held, w_held, w_sems = refs
+        place_ref, resid_ref, out_ref, total_ref, *held = refs
     else:
-        total_ref, *held, w_held, w_sems = refs
+        total_ref, *held = refs
     experts = w_ref.shape[0]
     pairs = held[0].shape[0]
-    copies = []
-    for begin, columns in chunks:
-        for e in range(experts):
-            slot = len(copies) % SLOTS
-            copies.append(
-                pltpu.make_async_copy(
-                    w_ref.at[e, :, pl.ds(begin, columns)], w_held.at[slot, :, pl.ds(0, columns)], w_sems.at[slot]
-                )
-            )
-    for copy in copies[:SLOTS]:
-        copy.start()
     for (parts, other_ref), into in zip(gathered, held):
         block = parts[0].shape[0]
         for slot in range(half):
@@ -673,14 +713,13 @@
     total_ref[...] = jnp.zeros_like(total_ref) if begins else before_ref[...]
     for index, (begin, columns) in enumerate(chunks):
         for expert in range(experts):
-            number = index * experts + expert
             lanes, valid = lane_window(offset_ref, expert, pairs, window)
-            copies[number].wait()
-            result = dot_nt(w_held[number % SLOTS, :, :columns], held[index][lanes, :columns])
-            if number + SLOTS < len(copies):
-                copies[number + SLOTS].start()
+            result = dot_nt(w_ref[expert, :, begin : begin + columns], held[index][lanes, :columns])
             if tail and index == 0:
-                result = result + dot_nt(tail_ref[expert], held[index][lanes, columns:])
+                units, size = w_ref.shape[2], tail[3]
+                result = result + dot_nt(
+                    w_ref[expert, :, units - size :], held[index][lanes, columns : columns + size]
+                )
             total_ref[:, lanes] = total_ref[:, lanes] + jnp.where(valid, result, 0.0)
 
     if ends:
@@ -726,7 +765,7 @@
 def chunk_columns(units):
     full = units // LANES
     count = 3 if full >= 6 else 1
-    ends = [full * (k + 1) // count for k in range(count)]
+    ends = [-(-full * (k + 1) // count) for k in range(count)]
     return [(LANES * (e - n), LANES * n) for e, n in zip(ends, [b - a for a, b in zip([0, *ends], ends)])]
 
 
@@ -768,6 +807,8 @@
     window = windows(pairs, CAP * dp * fs)
 
     hidden_in = pltpu.with_memory_space_constraint(hidden_in, pltpu.HBM)
+    project_in = project_in.transpose(1, 0, 2)
+    routes = pltpu.with_memory_space_constraint(routes.T, pltpu.HBM)
     gate_up = pltpu.with_memory_space_constraint(gate_up, pltpu.HBM)
     expert_down = pltpu.with_memory_space_constraint(expert_down, pltpu.HBM)
 
@@ -784,7 +825,7 @@
     def over_columns(x, s):
         return lax.ppermute(x, "fsdp", [(i, i ^ s) for i in range(fs)])
 
-    payload = pack(hidden_in, routes.T, dp, fs)
+    payload = pack(hidden_in, routes, dp, fs)
     recv = lax.all_to_all(
         payload.reshape(dp * fs, req, payload.shape[3]), ("dp", "fsdp"), 0, 0, tiled=True
     ).reshape(total, payload.shape[3])
@@ -801,15 +842,15 @@
     def slice_of(vector):
         return lax.dynamic_slice_in_dim(vector, my_row * width, width)
 
-    gate_tail = last_units(gate_up, payload, gate_tail_kernel, 2 * width, "gate_tail")
+    gate_tail, token = last_units(gate_up, payload)
     keep, send, raw = project_qkv(
         order,
         recv,
         slice_of(norm_first).astype(F32)[None, :],
-        project_in.transpose(1, 0, 2),
+        project_in,
         half,
         row,
-        gate_tail,
+        token,
     )
     sums = sum_parts(keep, swap(send), [[s] for s in range(half)], None, "core_sum_qkv")
     slot_of = (row_ids % 2 ^ my_core) * half + (row_ids // 2 ^ my_chip)
@@ -825,11 +866,11 @@
     other = swap(jnp.concatenate(parts, axis=0))
     projected = project_heads(parts, other, project_out.T)
     parts = [projected] + [over_columns(projected, s) for s in range(1, fs)]
-
     chunks = chunk_columns(units)
+    gate_first, gate_tail = stage_gate(gate_up, gate_tail, *chunks[0], projected)
+
     tail = tail_layout(units)
     block = pairs // dp
-    hbm = pl.BlockSpec(memory_space=pltpu.HBM)
     anywhere = pl.BlockSpec(memory_space=pl.ANY)
     spread = jax.ShapeDtypeStruct((2, pairs, 2 * width), BF16)
     resid_shape = jax.ShapeDtypeStruct((width, total), F32)
@@ -852,11 +893,10 @@
         weights = [pltpu.VMEM((SLOTS, width, 2, columns), BF16), pltpu.SemaphoreType.DMA((SLOTS,))]
         if first:
             operands = [*parts, raw.T, norm_column, router_slice, line_table]
-            in_specs = [full_spec(x.shape) for x in operands] + [hbm]
+            in_specs = [full_spec(x.shape) for x in operands] + [full_spec(gate_tail.shape)]
             operands.append(gate_tail)
             outs = [half_out, half_out, resid_shape, spread]
-            scratch += [pltpu.VMEM((pairs, LANES), F32), *weights]
-            scratch += [pltpu.VMEM(gate_tail.shape, BF16), pltpu.SemaphoreType.DMA]
+            scratch.append(pltpu.VMEM((pairs, LANES), F32))
         else:
             operands = [state["spread"]]
             in_specs = [full_spec(spread.shape)]
@@ -864,14 +904,14 @@
             scratch += weights
         result = pl.pallas_call(
             functools.partial(gate_kernel, len(parts) if first else 0, begin, columns, tail, window, len(after)),
-            in_specs=[SCALARS] * 2 + [anywhere] * len(after) + [*in_specs, anywhere],
+            in_specs=[SCALARS] * 2 + [anywhere] * len(after) + [*in_specs, full_spec(gate_first.shape) if first else anywhere],
             out_specs=[full_spec(x.shape) for x in outs],
             scratch_shapes=scratch,
             out_shape=outs,
             compiler_params=params(room(total)),
             cost_estimate=pl.CostEstimate(flops=1, bytes_accessed=1, transcendentals=0),
             name=f"gate_up_{index}",
-        )(offsets, order, *after, *operands, gate_up)
+        )(offsets, order, *after, *operands, gate_first if first else gate_up)
         if first:
             state["resid"], state["spread"] = result[2:]
         state["after"] = [result[0]]
@@ -916,18 +956,13 @@
         stacked = stack_parts(lists, after)
         others = [swap(x) for x in stacked]
         operands = [x for parts, other in zip(lists, others) for x in (*parts, other)]
-        in_specs = [full_spec(x.shape) for x in operands] + [anywhere]
-        operands.append(expert_down)
-        if first:
-            operands.append(state["tail"])
-            in_specs.append(full_spec(state["tail"].shape))
-        else:
+        operands.append(down_held)
+        in_specs = [full_spec(x.shape) for x in operands]
+        if not first:
             operands.append(state["sum"])
             in_specs.append(full_spec(state["sum"].shape))
         sum_shape = jax.ShapeDtypeStruct((width, pairs), F32)
-        widest = max(chunks[k][1] for k in numbers)
         scratch = [pltpu.VMEM((pairs, parts[0].shape[1]), BF16) for parts in lists]
-        scratch += [pltpu.VMEM((SLOTS, width, widest), BF16), pltpu.SemaphoreType.DMA((SLOTS,))]
         outs = [sum_shape]
         if last:
             operands += [place_table, state["resid"]]
@@ -943,7 +978,6 @@
                 min(-(-CAP * dp * fs // LANES) * LANES + LANES, pairs),
                 first,
                 last,
-                0,
             ),
                     in_specs=[SCALARS] * 2 + in_specs,
             out_specs=[full_spec(x.shape) for x in outs],
@@ -966,11 +1000,11 @@
         if step < count:
             kept, sent = gate(step)
         if step == count - 1:
-            state["tail"] = last_units(expert_down, state["after"][0], down_tail_kernel, width, "down_tail")
+            down_held = stage_down(expert_down, state["after"][0])
         for k in range(count):
             if step - k == stages:
                 if step == count - 1 + stages:
-                    flight.append(state["tail"])
+                    flight.append(down_held)
                 gathered[k] = {0: activate(k, held[k])}
                 if k < count - 1:
                     fresh[k] = spread_out(gathered[k], [0])

time: 149 us -> 140 us (0.940)
  waiting for transfers between devices: 44.4 us -> 36.9 us
  Pallas kernels: 46.5 us -> 42.8 us
  starting transfers between devices: 38.2 us -> 40.8 us
    pallas_call x2, Pallas kernels: 12.2 us -> 5.65 us  [down(): pl.pallas_call(functools.partial(down_kernel, half, [chunks[k] for k in n...]
    pallas_call x3 -> x4, Pallas kernels: 4.89 us -> 10.2 us  [the longest x1 3.23 us: last_units(): pl.pallas_call(functools.partial(gate_tail_kernel, size), grid=(1,), in_s...]
    ppermute x21, waiting for transfers between devices: 24.1 us -> 19.7 us  [over_chips(): return lax.ppermute(x, 'dp', [(i, i ^ 2 * s) for i in range(dp)])]
    ppermute x21, starting transfers between devices: 26.4 us -> 28.9 us  [over_chips(): return lax.ppermute(x, 'dp', [(i, i ^ 2 * s) for i in range(dp)])]
    pallas_call x3, Pallas kernels: 17.7 us -> 15.5 us  [gate(): pl.pallas_call(functools.partial(gate_kernel, len(parts) if first else 0,...]
    ppermute x3, waiting for transfers between devices: 4.57 us -> 2.6 us  [over_columns(): return lax.ppermute(x, 'fsdp', [(i, i ^ s) for i in range(fs)])]
  transfers between devices with their start and end apart: 33 -> 33, of which waited for: 20 -> 17; matrix products, arithmetic and copies ran while one was open for 2% -> 2% of each run, Pallas kernels for 16% -> 19%
where the time goes in v4:
time: 140 us; the launch traced here: 139 us
  Pallas kernels  42.8 us (31%)
  starting transfers between devices  40.8 us (29%)
  waiting for transfers between devices  36.9 us (26%)
  blocking collectives  12.5 us (9%)
  local copies, waits for them, and re-layouts  3.58 us (3%)
  other arithmetic  2.14 us (2%)
    ppermute x21, starting transfers between devices, over_chips(): return lax.ppermute(x, 'dp', [(i, i ^ 2 * s) for i in range(dp)])  28.9 us
    ppermute x21, waiting for transfers between devices, over_chips(): return lax.ppermute(x, 'dp', [(i, i ^ 2 * s) for i in range(dp)])  19.7 us
    pallas_call x3, Pallas kernels, gate(): pl.pallas_call(functools.partial(gate_kernel, len(parts) if first else 0,...  15.5 us
    all_to_all x1, blocking collectives, local(): lax.all_to_all(result.reshape(dp * fs, req, width), ('dp', 'fsdp'), 0, 0,...  12.5 us
    ppermute x8, waiting for transfers between devices, swap(): return lax.ppermute(x, 'dp', [(i, i ^ 1) for i in range(dp)])  9.43 us
    all_to_all x1, starting transfers between devices, local(): lax.all_to_all(payload.reshape(dp * fs, req, payload.shape[3]), ('dp', 'f...  7.3 us
    pallas_call x2, Pallas kernels, down(): pl.pallas_call(functools.partial(down_kernel, half, [chunks[k] for k in n...  5.65 us
    all_to_all x1, waiting for transfers between devices, local(): lax.all_to_all(payload.reshape(dp * fs, req, payload.shape[3]), ('dp', 'f...  5.22 us
  transfers between devices with their start and end apart: 33, of which 17 were waited for; matrix products, arithmetic and copies ran while one was open for 2% of the time, Pallas kernels for 19%

profile of v4, /device:TPU:0, one launch (start us, length us, event | category | flops | bytes accessed | tf_op | source)
XLA Modules:
  0.0 139.2 jit_solution(8094270653980568398)
XLA Ops:
  1.6 7.3 %all-to-all-start = ((bf16[32,8,384]{2,1,0:T(8,128)(2,1)}), bf16[32,8,384]{2,1,0:T(8,128)(2,1)S(1)}, u32[]{:S(2)}, u32[]{:S(2)}) async-start(bf16[32,8,384]{2,1,0:T(8,128)(2,1)} %bitcast.2), calls=%async_computation | async-start | bytes 393216 | tf_op jit(solution)/shard_map/all_to_all | solution.py:829
  9.8 3.2 %gate_tail.1 = (bf16[8,576,128]{2,1,0:T(8,128)(2,1)}, f32[8,128]{1,0:T(8,128)S(1)}) custom-call(bf16[8,288,2,1440]{3,2,1,0:T(2,128)(2,1)} %refs_2_.3, bf16[8,4,8,384]{3,2,1,0:T(8,128)(2,1)} %pack.1._), custom_call_target="tpu_custom_call" | custom-call | flops 1 | bytes 1 | tf_op jit(solution)/shard_map/gate_tail/pallas_call | solution.py:504
  13.2 5.2 %all-to-all-done = bf16[32,8,384]{2,1,0:T(8,128)(2,1)S(1)} async-done(((bf16[32,8,384]{2,1,0:T(8,128)(2,1)}), bf16[32,8,384]{2,1,0:T(8,128)(2,1)S(1)}, u32[]{:S(2)}, u32[]{:S(2)}) %all-to-all-start) | async-done | bytes 196640 | tf_op jit(solution)/shard_map/all_to_all | solution.py:829
  23.8 2.2 %collective-permute-start.3 = (bf16[1,32,1536]{2,1,0:T(8,128)(2,1)S(1)}, bf16[1,32,1536]{2,1,0:T(8,128)(2,1)S(1)}, u32[]{:S(2)}, u32[]{:S(2)}) collective-permute-start(bf16[1,32,1536]{2,1,0:T(8,128)(2,1)S(1)} %get-tuple-element.56), channel_id=1, source_target_pairs={{0,24},{4,28},{8,16},{12,20},{16,8},{20,12},{24,0},{28,4},{1,25},{... | collective-permute-start | bytes 294920 | tf_op jit(solution)/shard_map/ppermute | solution.py:823
  26.1 2.0 %pair_places.1 = (s32[9]{0:T(128)S(1)}, f32[256,128]{1,0:T(8,128)S(1)}, f32[8,256]{1,0:T(8,128)S(1)}) custom-call(s32[8,4]{1,0:T(8,128)S(1)} %copy.33.move_ref, s32[8]{0:T(128)S(1)} %pad_add_fusion.1.order_ref, s32[8]{0:T(128)S(1)} %fusion.14.slot_ref, s32[2]{0:T(128)S(1)} %pad_add_fusion.2.column_ref, bf16[256,384]{1,0:T(8,128)(2,1)S(1)} %bitcast.17, ...), custom_call_target="tpu_custom_call" | custom-call | flops 1 | bytes 1 | tf_op jit(solution)/shard_map/pair_places/pallas_call | solution.py:184
  28.1 2.3 %copy-done.1 = bf16[144,16,2,512]{3,2,1,0:T(2,128)(2,1)S(1)} copy-done((bf16[144,16,2,512]{3,2,1,0:T(2,128)(2,1)S(1)}, bf16[144,16,2,512]{3,2,1,0:T(2,128)(2,1)}, u32[]{:S(2)}) %copy-start.1) | copy-done | bytes 4718616
  30.4 3.5 %pool_split.1 = (bf16[2304,512]{1,0:T(8,128)(2,1)S(1)}, bf16[2304,512]{1,0:T(8,128)(2,1)S(1)}, f32[32,2304]{1,0:T(8,128)S(1)}) custom-call(s32[4,4]{1,0:T(4,128)S(1)} %copy-done.5, s32[32,6]{1,0:T(8,128)S(1)} %copy.34.lists_ref, bf16[144,16,2,512]{3,2,1,0:T(2,128)(2,1)S(1)} %copy-done.1, f32[256,128]{1,0:T(8,128)S(1)} %get-tuple-element.57._.refs_9_.refs_12_), custom_call_target="tpu_custom_call" | custom-call | flops 1 | bytes 1 | tf_op jit(solution)/shard_map/pool_split/pallas_call | solution.py:236
  34.0 2.3 %attention.1.refs_0_ = bf16[32,512]{1,0:T(8,128)(2,1)S(1)} custom-call(bf16[1,32,1536]{2,1,0:T(8,128)(2,1)S(1)} %get-tuple-element.51._.refs_0_, bf16[1,32,1536]{2,1,0:T(8,128)(2,1)S(1)} %collective-permute-done.1.refs_1_, bf16[1,32,1536]{2,1,0:T(8,128)(2,1)S(1)} %collective-permute-done.2.refs_2_, bf16[1,32,1536]{2,1,0:T(8,128)(2,1)S(1)} %collective-permute-done.3.refs_3_, ...), custom_call_target="tpu_custom_call" | custom-call | flops 1 | bytes 1 | tf_op jit(solution)/shard_map/attention/pallas_call | solution.py:341
  38.6 2.1 %collective-permute-start.4 = (bf16[32,512]{1,0:T(8,128)(2,1)S(1)}, bf16[32,512]{1,0:T(8,128)(2,1)S(1)}, u32[]{:S(2)}, u32[]{:S(2)}) collective-permute-start(bf16[32,512]{1,0:T(8,128)(2,1)S(1)} %attention.1.refs_0_), channel_id=1, source_target_pairs={{0,8},{4,12},{8,0},{12,4},{16,24},{20,28},{24,16},{28,20},{1,9},{5... | collective-permute-start | bytes 98312 | tf_op jit(solution)/shard_map/ppermute | solution.py:823
  49.5 2.4 %stage_gate.1 = (bf16[8,288,2,512]{3,2,1,0:T(2,128)(2,1)S(1)}, bf16[8,576,128]{2,1,0:T(8,128)(2,1)S(1)}) custom-call(bf16[8,288,2,1440]{3,2,1,0:T(2,128)(2,1)} %refs_2_.3, bf16[8,576,128]{2,1,0:T(8,128)(2,1)S(1)} %copy-done.2, bf16[288,256]{1,0:T(8,128)(2,1)S(1)} %out_projection.1._.refs_1_), custom_call_target="tpu_custom_call" | custom-call | flops 1 | bytes 1 | tf_op jit(solution)/shard_map/stage_gate/pallas_call | solution.py:532
  52.5 1.9 %collective-permute-done.9.refs_3_ = bf16[288,256]{1,0:T(8,128)(2,1)S(1)} collective-permute-done((bf16[288,256]{1,0:T(8,128)(2,1)S(1)}, bf16[288,256]{1,0:T(8,128)(2,1)S(1)}, u32[]{:S(2)}, u32[]{:S(2)}) %collective-permute-start.9) | collective-permute-done | bytes 147488 | tf_op jit(solution)/shard_map/ppermute | solution.py:826
  54.5 5.1 %gate_up_0.1 = (bf16[4,64,1152]{2,1,0:T(8,128)(2,1)S(1)}, bf16[4,64,1152]{2,1,0:T(8,128)(2,1)S(1)}, f32[288,256]{1,0:T(8,128)S(1)}, bf16[2,512,576]{2,1,0:T(8,128)(2,1)S(1)}) custom-call(s32[9]{0:T(128)S(1)} %get-tuple-element.52.offset_ref, s32[8]{0:T(128)S(1)} %pad_add_fusion.1.order_ref, f32[8,256]{1,0:T(8,128)S(1)} %get-tuple-element.53.refs_0_.refs_8_, ...), custom_call_target="tpu_custom_call" | custom-call | flops 1 | bytes 1 | tf_op jit(solution)/shard_map/gate_up_0/pallas_call | solution.py:905
  59.6 2.0 %collective-permute-done.11.recv_ref = bf16[4,64,1152]{2,1,0:T(8,128)(2,1)S(1)} collective-permute-done((bf16[4,64,1152]{2,1,0:T(8,128)(2,1)S(1)}, bf16[4,64,1152]{2,1,0:T(8,128)(2,1)S(1)}, u32[]{:S(2)}, u32[]{:S(2)}) %collective-permute-start.11) | collective-permute-done | bytes 589856 | tf_op jit(solution)/shard_map/ppermute | solution.py:820
  64.0 5.2 %gate_up_1.1 = (bf16[4,64,1024]{2,1,0:T(8,128)(2,1)S(1)}, bf16[4,64,1024]{2,1,0:T(8,128)(2,1)S(1)}) custom-call(s32[9]{0:T(128)S(1)} %get-tuple-element.52.offset_ref, s32[8]{0:T(128)S(1)} %pad_add_fusion.1.order_ref, bf16[2,64,1152]{2,1,0:T(8,128)(2,1)S(1)} %get-tuple-element.67.refs_0_.keep_ref, bf16[2,512,576]{2,1,0:T(8,128)(2,1)S(1)} %get-tuple-element.68.refs_1_, ...), custom_call_target="tpu_custom_call" | custom-call | flops 1 | bytes 1 | tf_op jit(solution)/shard_map/gate_up_1/pallas_call | solution.py:905
  69.2 2.2 %collective-permute-done.12.recv_ref.outs_1_ = bf16[2,64,1152]{2,1,0:T(8,128)(2,1)S(1)} collective-permute-done((bf16[2,64,1152]{2,1,0:T(8,128)(2,1)S(1)}, bf16[2,64,1152]{2,1,0:T(8,128)(2,1)S(1)}, u32[]{:S(2)}, u32[]{:S(2)}) %collective-permute-start.12) | collective-permute-done | bytes 294944 | tf_op jit(solution)/shard_map/ppermute | solution.py:823
  76.5 5.3 %gate_up_2.1 = (bf16[4,64,768]{2,1,0:T(8,128)(2,1)S(1)}, bf16[4,64,768]{2,1,0:T(8,128)(2,1)S(1)}) custom-call(s32[9]{0:T(128)S(1)} %get-tuple-element.52.offset_ref, s32[8]{0:T(128)S(1)} %pad_add_fusion.1.order_ref, bf16[2,64,1024]{2,1,0:T(8,128)(2,1)S(1)} %get-tuple-element.74.refs_0_.keep_ref, bf16[2,512,576]{2,1,0:T(8,128)(2,1)S(1)} %get-tuple-element.68.refs_1_, ...), custom_call_target="tpu_custom_call" | custom-call | flops 1 | bytes 1 | tf_op jit(solution)/shard_map/gate_up_2/pallas_call | solution.py:905
  81.8 2.9 %collective-permute-done.15.refs_1_.refs_3_ = bf16[1,64,1152]{2,1,0:T(8,128)(2,1)S(1)} collective-permute-done((bf16[1,64,1152]{2,1,0:T(8,128)(2,1)S(1)}, bf16[1,64,1152]{2,1,0:T(8,128)(2,1)S(1)}, u32[]{:S(2)}, u32[]{:S(2)}) %collective-permute-start.15) | collective-permute-done | bytes 147488 | tf_op jit(solution)/shard_map/ppermute | solution.py:823
  92.7 9.0 %collective-permute-done.19.refs_5_.refs_2_ = bf16[64,640]{1,0:T(8,128)(2,1)S(1)} collective-permute-done((bf16[64,640]{1,0:T(8,128)(2,1)S(1)}, bf16[64,640]{1,0:T(8,128)(2,1)S(1)}, u32[]{:S(2)}, u32[]{:S(2)}) %collective-permute-start.19) | collective-permute-done | bytes 81952 | tf_op jit(solution)/shard_map/ppermute | solution.py:823
  101.9 2.0 %collective-permute-start.24 = (bf16[1,64,768]{2,1,0:T(8,128)(2,1)S(1)}, bf16[1,64,768]{2,1,0:T(8,128)(2,1)S(1)}, u32[]{:S(2)}, u32[]{:S(2)}) collective-permute-start(bf16[1,64,768]{2,1,0:T(8,128)(2,1)S(1)} %get-tuple-element.87), channel_id=1, source_target_pairs={{0,16},{4,20},{8,24},{12,28},{16,0},{20,4},{24,8},{28,12},{1,17},{... | collective-permute-start | bytes 294920 | tf_op jit(solution)/shard_map/ppermute | solution.py:823
  106.9 3.0 %stage_down.1.refs_8_.refs_5_.refs_10_ = bf16[8,288,1440]{2,1,0:T(8,128)(2,1)S(1)} custom-call(bf16[8,288,1440]{2,1,0:T(8,128)(2,1)} %w_ref.3, bf16[4,64,768]{2,1,0:T(8,128)(2,1)S(1)} %get-tuple-element.77.refs_2_.keep_ref._), custom_call_target="tpu_custom_call" | custom-call | flops 1 | bytes 1 | tf_op jit(solution)/shard_map/stage_down/pallas_call | solution.py:551
  115.1 2.1 %collective-permute-start.26 = (bf16[64,384]{1,0:T(8,128)(2,1)S(1)}, bf16[64,384]{1,0:T(8,128)(2,1)S(1)}, u32[]{:S(2)}, u32[]{:S(2)}) collective-permute-start(bf16[64,384]{1,0:T(8,128)(2,1)S(1)} %activation_2.1.refs_4_.refs_5_), channel_id=1, source_target_pairs={{0,8},{4,12},{8,0},{12,4},{16,24},{20,28},{24,16},{28,20},{1,9},{5... | collective-permute-start | bytes 147464 | tf_op jit(solution)/shard_map/ppermute | solution.py:823
  117.3 2.3 %down_0.1.refs_8_.refs_11_ = f32[288,512]{1,0:T(8,128)S(1)} custom-call(s32[9]{0:T(128)S(1)} %get-tuple-element.52.offset_ref, s32[8]{0:T(128)S(1)} %pad_add_fusion.1.order_ref, bf16[64,640]{1,0:T(8,128)(2,1)S(1)} %get-tuple-element.78.outs_0_.refs_0_, bf16[64,640]{1,0:T(8,128)(2,1)S(1)} %collective-permute-done.18.refs_4_.refs_1_, ...), custom_call_target="tpu_custom_call" | custom-call | flops 1 | bytes 1 | tf_op jit(solution)/shard_map/down_0/pallas_call | solution.py:972
  122.6 3.4 %down_1.1 = bf16[256,288]{1,0:T(8,128)(2,1)S(1)} custom-call(s32[9]{0:T(128)S(1)} %get-tuple-element.52.offset_ref, s32[8]{0:T(128)S(1)} %pad_add_fusion.1.order_ref, bf16[64,512]{1,0:T(8,128)(2,1)S(1)} %activation_1.1.outs_0_.refs_0_, bf16[64,512]{1,0:T(8,128)(2,1)S(1)} %collective-permute-done.21.refs_4_.refs_1_, ...), custom_call_target="tpu_custom_call" | custom-call | flops 1 | bytes 1 | tf_op jit(solution)/shard_map/down_1/pallas_call | solution.py:972
  125.9 12.5 %all_to_all.10 = bf16[32,8,288]{2,1,0:T(8,128)(2,1)S(1)} all-to-all(bf16[32,8,288]{2,1,0:T(8,128)(2,1)S(1)} %bitcast.19), channel_id=1, replica_groups=mesh['dp'=8,'fsdp'=4] {'dp','fsdp'}, dimensions={0} | all-to-all | bytes 294912 | tf_op jit(solution)/shard_map/all_to_all | solution.py:1031
  (109 shorter events, 47.5 us)
Async XLA Ops:
  1.6 16.8 %all-to-all-start = ((bf16[32,8,384]{2,1,0:T(8,128)(2,1)}), bf16[32,8,384]{2,1,0:T(8,128)(2,1)S(1)}, u32[]{:S(2)}, u32[]{:S(2)}) async-start(bf16[32,8,384]{2,1,0:T(8,128)(2,1)} %bitcast.2), calls=%async_computation | async-start | bytes 393216 | tf_op jit(solution)/shard_map/all_to_all | solution.py:829
  21.6 12.4 %collective-permute-start.1 = (bf16[1,32,1536]{2,1,0:T(8,128)(2,1)S(1)}, bf16[1,32,1536]{2,1,0:T(8,128)(2,1)S(1)}, u32[]{:S(2)}, u32[]{:S(2)}) collective-permute-start(bf16[1,32,1536]{2,1,0:T(8,128)(2,1)S(1)} %get-tuple-element.54), channel_id=1, source_target_pairs={{0,8},{4,12},{8,0},{12,4},{16,24},{20,28},{24,16},{28,20},{1,9},{5... | collective-permute-start | bytes 294920 | tf_op jit(solution)/shard_map/ppermute | solution.py:823
  22.5 11.5 %collective-permute-start.2 = (bf16[1,32,1536]{2,1,0:T(8,128)(2,1)S(1)}, bf16[1,32,1536]{2,1,0:T(8,128)(2,1)S(1)}, u32[]{:S(2)}, u32[]{:S(2)}) collective-permute-start(bf16[1,32,1536]{2,1,0:T(8,128)(2,1)S(1)} %get-tuple-element.55), channel_id=1, source_target_pairs={{0,16},{4,20},{8,24},{12,28},{16,0},{20,4},{24,8},{28,12},{1,17},{... | collective-permute-start | bytes 294920 | tf_op jit(solution)/shard_map/ppermute | solution.py:823
  23.8 10.2 %collective-permute-start.3 = (bf16[1,32,1536]{2,1,0:T(8,128)(2,1)S(1)}, bf16[1,32,1536]{2,1,0:T(8,128)(2,1)S(1)}, u32[]{:S(2)}, u32[]{:S(2)}) collective-permute-start(bf16[1,32,1536]{2,1,0:T(8,128)(2,1)S(1)} %get-tuple-element.56), channel_id=1, source_target_pairs={{0,24},{4,28},{8,16},{12,20},{16,8},{20,12},{24,0},{28,4},{1,25},{... | collective-permute-start | bytes 294920 | tf_op jit(solution)/shard_map/ppermute | solution.py:823
  36.3 6.1 %collective-permute-start.6 = (bf16[32,512]{1,0:T(8,128)(2,1)S(1)}, bf16[32,512]{1,0:T(8,128)(2,1)S(1)}, u32[]{:S(2)}, u32[]{:S(2)}) collective-permute-start(bf16[32,512]{1,0:T(8,128)(2,1)S(1)} %attention.1.refs_0_), channel_id=1, source_target_pairs={{0,24},{4,28},{8,16},{12,20},{16,8},{20,12},{24,0},{28,4},{1,25},{... | collective-permute-start | bytes 98312 | tf_op jit(solution)/shard_map/ppermute | solution.py:823
  44.8 7.7 %collective-permute-start.10 = (bf16[288,256]{1,0:T(8,128)(2,1)S(1)}, bf16[288,256]{1,0:T(8,128)(2,1)S(1)}, u32[]{:S(2)}, u32[]{:S(2)}) collective-permute-start(bf16[288,256]{1,0:T(8,128)(2,1)S(1)} %out_projection.1._.refs_1_), channel_id=1, source_target_pairs={{0,3},{1,2},{2,1},{3,0},{4,7},{5,6},{6,5},{7,4},{8,11},{9,10},{10,... | collective-permute-start | bytes 442376 | tf_op jit(solution)/shard_map/ppermute | solution.py:826
  45.7 8.8 %collective-permute-start.9 = (bf16[288,256]{1,0:T(8,128)(2,1)S(1)}, bf16[288,256]{1,0:T(8,128)(2,1)S(1)}, u32[]{:S(2)}, u32[]{:S(2)}) collective-permute-start(bf16[288,256]{1,0:T(8,128)(2,1)S(1)} %out_projection.1._.refs_1_), channel_id=1, source_target_pairs={{0,2},{1,3},{2,0},{3,1},{4,6},{5,7},{6,4},{7,5},{8,10},{9,11},{10,... | collective-permute-start | bytes 442376 | tf_op jit(solution)/shard_map/ppermute | solution.py:826
  46.5 8.0 %collective-permute-start.8 = (bf16[288,256]{1,0:T(8,128)(2,1)S(1)}, bf16[288,256]{1,0:T(8,128)(2,1)S(1)}, u32[]{:S(2)}, u32[]{:S(2)}) collective-permute-start(bf16[288,256]{1,0:T(8,128)(2,1)S(1)} %out_projection.1._.refs_1_), channel_id=1, source_target_pairs={{0,1},{1,0},{2,3},{3,2},{4,5},{5,4},{6,7},{7,6},{8,9},{9,8},{10,11... | collective-permute-start | bytes 442376 | tf_op jit(solution)/shard_map/ppermute | solution.py:826
  62.3 9.1 %collective-permute-start.12 = (bf16[2,64,1152]{2,1,0:T(8,128)(2,1)S(1)}, bf16[2,64,1152]{2,1,0:T(8,128)(2,1)S(1)}, u32[]{:S(2)}, u32[]{:S(2)}) collective-permute-start(bf16[2,64,1152]{2,1,0:T(8,128)(2,1)S(1)} %get-tuple-element.70), channel_id=1, source_target_pairs={{0,8},{4,12},{8,0},{12,4},{16,24},{20,28},{24,16},{28,20},{1,9},{5... | collective-permute-start | bytes 884744 | tf_op jit(solution)/shard_map/ppermute | solution.py:823
  73.9 11.6 %collective-permute-start.14 = (bf16[2,64,1024]{2,1,0:T(8,128)(2,1)S(1)}, bf16[2,64,1024]{2,1,0:T(8,128)(2,1)S(1)}, u32[]{:S(2)}, u32[]{:S(2)}) collective-permute-start(bf16[2,64,1024]{2,1,0:T(8,128)(2,1)S(1)} %get-tuple-element.75), channel_id=1, source_target_pairs={{0,8},{4,12},{8,0},{12,4},{16,24},{20,28},{24,16},{28,20},{1,9},{5... | collective-permute-start | bytes 786440 | tf_op jit(solution)/shard_map/ppermute | solution.py:823
  75.6 9.0 %collective-permute-start.15 = (bf16[1,64,1152]{2,1,0:T(8,128)(2,1)S(1)}, bf16[1,64,1152]{2,1,0:T(8,128)(2,1)S(1)}, u32[]{:S(2)}, u32[]{:S(2)}) collective-permute-start(bf16[1,64,1152]{2,1,0:T(8,128)(2,1)S(1)} %get-tuple-element.76), channel_id=1, source_target_pairs={{0,16},{4,20},{8,24},{12,28},{16,0},{20,4},{24,8},{28,12},{1,17},{... | collective-permute-start | bytes 442376 | tf_op jit(solution)/shard_map/ppermute | solution.py:823
  87.7 14.0 %collective-permute-start.20 = (bf16[2,64,768]{2,1,0:T(8,128)(2,1)S(1)}, bf16[2,64,768]{2,1,0:T(8,128)(2,1)S(1)}, u32[]{:S(2)}, u32[]{:S(2)}) collective-permute-start(bf16[2,64,768]{2,1,0:T(8,128)(2,1)S(1)} %get-tuple-element.85), channel_id=1, source_target_pairs={{0,8},{4,12},{8,0},{12,4},{16,24},{20,28},{24,16},{28,20},{1,9},{5... | collective-permute-start | bytes 589832 | tf_op jit(solution)/shard_map/ppermute | solution.py:823
  89.4 12.3 %collective-permute-start.16 = (bf16[1,64,1024]{2,1,0:T(8,128)(2,1)S(1)}, bf16[1,64,1024]{2,1,0:T(8,128)(2,1)S(1)}, u32[]{:S(2)}, u32[]{:S(2)}) collective-permute-start(bf16[1,64,1024]{2,1,0:T(8,128)(2,1)S(1)} %get-tuple-element.81), channel_id=1, source_target_pairs={{0,16},{4,20},{8,24},{12,28},{16,0},{20,4},{24,8},{28,12},{1,17},{... | collective-permute-start | bytes 393224 | tf_op jit(solution)/shard_map/ppermute | solution.py:823
  90.4 11.3 %collective-permute-start.19 = (bf16[64,640]{1,0:T(8,128)(2,1)S(1)}, bf16[64,640]{1,0:T(8,128)(2,1)S(1)}, u32[]{:S(2)}, u32[]{:S(2)}) collective-permute-start(bf16[64,640]{1,0:T(8,128)(2,1)S(1)} %get-tuple-element.78.outs_0_.refs_0_), channel_id=1, source_target_pairs={{0,16},{4,20},{8,24},{12,28},{16,0},{20,4},{24,8},{28,12},{1,17},{... | collective-permute-start | bytes 245768 | tf_op jit(solution)/shard_map/ppermute | solution.py:823
  92.3 9.4 %collective-permute-start.18 = (bf16[64,640]{1,0:T(8,128)(2,1)S(1)}, bf16[64,640]{1,0:T(8,128)(2,1)S(1)}, u32[]{:S(2)}, u32[]{:S(2)}) collective-permute-start(bf16[64,640]{1,0:T(8,128)(2,1)S(1)} %get-tuple-element.78.outs_0_.refs_0_), channel_id=1, source_target_pairs={{0,8},{4,12},{8,0},{12,4},{16,24},{20,28},{24,16},{28,20},{1,9},{5... | collective-permute-start | bytes 245768 | tf_op jit(solution)/shard_map/ppermute | solution.py:823
  101.9 9.4 %collective-permute-start.24 = (bf16[1,64,768]{2,1,0:T(8,128)(2,1)S(1)}, bf16[1,64,768]{2,1,0:T(8,128)(2,1)S(1)}, u32[]{:S(2)}, u32[]{:S(2)}) collective-permute-start(bf16[1,64,768]{2,1,0:T(8,128)(2,1)S(1)} %get-tuple-element.87), channel_id=1, source_target_pairs={{0,16},{4,20},{8,24},{12,28},{16,0},{20,4},{24,8},{28,12},{1,17},{... | collective-permute-start | bytes 294920 | tf_op jit(solution)/shard_map/ppermute | solution.py:823
  103.9 6.1 %collective-permute-start.25 = (bf16[64,640]{1,0:T(8,128)(2,1)S(1)}, bf16[64,640]{1,0:T(8,128)(2,1)S(1)}, u32[]{:S(2)}, u32[]{:S(2)}) collective-permute-start(bf16[64,640]{1,0:T(8,128)(2,1)S(1)} %collective-permute-done.19.refs_5_.refs_2_), channel_id=1, source_target_pairs={{0,8},{4,12},{8,0},{12,4},{16,24},{20,28},{24,16},{28,20},{1,9},{5... | collective-permute-start | bytes 245768 | tf_op jit(solution)/shard_map/ppermute | solution.py:823
  105.1 6.2 %collective-permute-start.22 = (bf16[64,512]{1,0:T(8,128)(2,1)S(1)}, bf16[64,512]{1,0:T(8,128)(2,1)S(1)}, u32[]{:S(2)}, u32[]{:S(2)}) collective-permute-start(bf16[64,512]{1,0:T(8,128)(2,1)S(1)} %activation_1.1.outs_0_.refs_0_), channel_id=1, source_target_pairs={{0,16},{4,20},{8,24},{12,28},{16,0},{20,4},{24,8},{28,12},{1,17},{... | collective-permute-start | bytes 196616 | tf_op jit(solution)/shard_map/ppermute | solution.py:823
  105.9 5.5 %collective-permute-start.21 = (bf16[64,512]{1,0:T(8,128)(2,1)S(1)}, bf16[64,512]{1,0:T(8,128)(2,1)S(1)}, u32[]{:S(2)}, u32[]{:S(2)}) collective-permute-start(bf16[64,512]{1,0:T(8,128)(2,1)S(1)} %activation_1.1.outs_0_.refs_0_), channel_id=1, source_target_pairs={{0,8},{4,12},{8,0},{12,4},{16,24},{20,28},{24,16},{28,20},{1,9},{5... | collective-permute-start | bytes 196616 | tf_op jit(solution)/shard_map/ppermute | solution.py:823
  111.5 5.7 %collective-permute-start.29 = (bf16[4,64,640]{2,1,0:T(8,128)(2,1)S(1)}, bf16[4,64,640]{2,1,0:T(8,128)(2,1)S(1)}, u32[]{:S(2)}, u32[]{:S(2)}) collective-permute-start(bf16[4,64,640]{2,1,0:T(8,128)(2,1)S(1)} %stack_parts.2), channel_id=1, source_target_pairs={{0,4},{4,0},{8,12},{12,8},{16,20},{20,16},{24,28},{28,24},{1,5},{5... | collective-permute-start | bytes 983048 | tf_op jit(solution)/shard_map/ppermute | solution.py:820
  111.6 8.0 %collective-permute-start.23 = (bf16[64,512]{1,0:T(8,128)(2,1)S(1)}, bf16[64,512]{1,0:T(8,128)(2,1)S(1)}, u32[]{:S(2)}, u32[]{:S(2)}) collective-permute-start(bf16[64,512]{1,0:T(8,128)(2,1)S(1)} %collective-permute-done.22.refs_5_.refs_2_), channel_id=1, source_target_pairs={{0,8},{4,12},{8,0},{12,4},{16,24},{20,28},{24,16},{28,20},{1,9},{5... | collective-permute-start | bytes 196616 | tf_op jit(solution)/shard_map/ppermute | solution.py:823
  112.9 6.7 %collective-permute-start.28 = (bf16[64,384]{1,0:T(8,128)(2,1)S(1)}, bf16[64,384]{1,0:T(8,128)(2,1)S(1)}, u32[]{:S(2)}, u32[]{:S(2)}) collective-permute-start(bf16[64,384]{1,0:T(8,128)(2,1)S(1)} %activation_2.1.refs_4_.refs_5_), channel_id=1, source_target_pairs={{0,24},{4,28},{8,16},{12,20},{16,8},{20,12},{24,0},{28,4},{1,25},{... | collective-permute-start | bytes 147464 | tf_op jit(solution)/shard_map/ppermute | solution.py:823
  114.6 6.0 %collective-permute-start.27 = (bf16[64,384]{1,0:T(8,128)(2,1)S(1)}, bf16[64,384]{1,0:T(8,128)(2,1)S(1)}, u32[]{:S(2)}, u32[]{:S(2)}) collective-permute-start(bf16[64,384]{1,0:T(8,128)(2,1)S(1)} %activation_2.1.refs_4_.refs_5_), channel_id=1, source_target_pairs={{0,16},{4,20},{8,24},{12,28},{16,0},{20,4},{24,8},{28,12},{1,17},{... | collective-permute-start | bytes 147464 | tf_op jit(solution)/shard_map/ppermute | solution.py:823
  115.1 5.5 %collective-permute-start.26 = (bf16[64,384]{1,0:T(8,128)(2,1)S(1)}, bf16[64,384]{1,0:T(8,128)(2,1)S(1)}, u32[]{:S(2)}, u32[]{:S(2)}) collective-permute-start(bf16[64,384]{1,0:T(8,128)(2,1)S(1)} %activation_2.1.refs_4_.refs_5_), channel_id=1, source_target_pairs={{0,8},{4,12},{8,0},{12,4},{16,24},{20,28},{24,16},{28,20},{1,9},{5... | collective-permute-start | bytes 147464 | tf_op jit(solution)/shard_map/ppermute | solution.py:823
  (19 other events, 150.6 us)

commit v5 on v4

--- a/solution.py
+++ b/solution.py
@@ -765,7 +765,7 @@
 def chunk_columns(units):
     full = units // LANES
     count = 3 if full >= 6 else 1
-    ends = [-(-full * (k + 1) // count) for k in range(count)]
+    ends = [full * 4 // 11, full * 9 // 11, full] if count == 3 else [full]
     return [(LANES * (e - n), LANES * n) for e, n in zip(ends, [b - a for a, b in zip([0, *ends], ends)])]
 
 

time: 140 us -> 139 us (level)
  waiting for transfers between devices: 36.9 us -> 35.1 us
    ppermute x8, waiting for transfers between devices: 9.43 us -> 7.91 us  [swap(): return lax.ppermute(x, 'dp', [(i, i ^ 1) for i in range(dp)])]
  transfers between devices with their start and end apart: 33 -> 33, of which waited for: 17 -> 17; matrix products, arithmetic and copies ran while one was open for 2% -> 2% of each run, Pallas kernels for 19% -> 20%
where the time goes in v5:
time: 139 us
  Pallas kernels  44.1 us (32%)
  starting transfers between devices  41 us (29%)
  waiting for transfers between devices  35.1 us (25%)
  blocking collectives  12.3 us (9%)
  local copies, waits for them, and re-layouts  3.58 us (3%)
  other arithmetic  2.14 us (2%)
    ppermute x21, starting transfers between devices, over_chips(): return lax.ppermute(x, 'dp', [(i, i ^ 2 * s) for i in range(dp)])  29.2 us
    ppermute x21, waiting for transfers between devices, over_chips(): return lax.ppermute(x, 'dp', [(i, i ^ 2 * s) for i in range(dp)])  19.4 us
    pallas_call x3, Pallas kernels, gate(): pl.pallas_call(functools.partial(gate_kernel, len(parts) if first else 0,...  16.6 us
    all_to_all x1, blocking collectives, local(): lax.all_to_all(result.reshape(dp * fs, req, width), ('dp', 'fsdp'), 0, 0,...  12.3 us
    ppermute x8, waiting for transfers between devices, swap(): return lax.ppermute(x, 'dp', [(i, i ^ 1) for i in range(dp)])  7.91 us
    all_to_all x1, starting transfers between devices, local(): lax.all_to_all(payload.reshape(dp * fs, req, payload.shape[3]), ('dp', 'f...  7.3 us
    pallas_call x2, Pallas kernels, down(): pl.pallas_call(functools.partial(down_kernel, half, [chunks[k] for k in n...  5.67 us
    all_to_all x1, waiting for transfers between devices, local(): lax.all_to_all(payload.reshape(dp * fs, req, payload.shape[3]), ('dp', 'f...  5.22 us
  transfers between devices with their start and end apart: 33, of which 17 were waited for; matrix products, arithmetic and copies ran while one was open for 2% of the time, Pallas kernels for 20%

profile of v5, /device:TPU:0, one launch (start us, length us, event | category | flops | bytes accessed | tf_op | source)
XLA Modules:
  0.0 138.7 jit_solution(16945714898360571887)
XLA Ops:
  1.6 7.3 %all-to-all-start = ((bf16[32,8,384]{2,1,0:T(8,128)(2,1)}), bf16[32,8,384]{2,1,0:T(8,128)(2,1)S(1)}, u32[]{:S(2)}, u32[]{:S(2)}) async-start(bf16[32,8,384]{2,1,0:T(8,128)(2,1)} %bitcast.2), calls=%async_computation | async-start | bytes 393216 | tf_op jit(solution)/shard_map/all_to_all | solution.py:829
  9.8 3.2 %gate_tail.1 = (bf16[8,576,128]{2,1,0:T(8,128)(2,1)}, f32[8,128]{1,0:T(8,128)S(1)}) custom-call(bf16[8,288,2,1440]{3,2,1,0:T(2,128)(2,1)} %refs_2_.3, bf16[8,4,8,384]{3,2,1,0:T(8,128)(2,1)} %pack.1._), custom_call_target="tpu_custom_call" | custom-call | flops 1 | bytes 1 | tf_op jit(solution)/shard_map/gate_tail/pallas_call | solution.py:504
  13.2 5.2 %all-to-all-done = bf16[32,8,384]{2,1,0:T(8,128)(2,1)S(1)} async-done(((bf16[32,8,384]{2,1,0:T(8,128)(2,1)}), bf16[32,8,384]{2,1,0:T(8,128)(2,1)S(1)}, u32[]{:S(2)}, u32[]{:S(2)}) %all-to-all-start) | async-done | bytes 196640 | tf_op jit(solution)/shard_map/all_to_all | solution.py:829
  23.8 2.2 %collective-permute-start.3 = (bf16[1,32,1536]{2,1,0:T(8,128)(2,1)S(1)}, bf16[1,32,1536]{2,1,0:T(8,128)(2,1)S(1)}, u32[]{:S(2)}, u32[]{:S(2)}) collective-permute-start(bf16[1,32,1536]{2,1,0:T(8,128)(2,1)S(1)} %get-tuple-element.56), channel_id=1, source_target_pairs={{0,24},{4,28},{8,16},{12,20},{16,8},{20,12},{24,0},{28,4},{1,25},{... | collective-permute-start | bytes 294920 | tf_op jit(solution)/shard_map/ppermute | solution.py:823
  28.1 2.3 %copy-done.1 = bf16[144,16,2,512]{3,2,1,0:T(2,128)(2,1)S(1)} copy-done((bf16[144,16,2,512]{3,2,1,0:T(2,128)(2,1)S(1)}, bf16[144,16,2,512]{3,2,1,0:T(2,128)(2,1)}, u32[]{:S(2)}) %copy-start.1) | copy-done | bytes 4718616
  30.4 3.5 %pool_split.1 = (bf16[2304,512]{1,0:T(8,128)(2,1)S(1)}, bf16[2304,512]{1,0:T(8,128)(2,1)S(1)}, f32[32,2304]{1,0:T(8,128)S(1)}) custom-call(s32[4,4]{1,0:T(4,128)S(1)} %copy-done.5, s32[32,6]{1,0:T(8,128)S(1)} %copy.34.lists_ref, bf16[144,16,2,512]{3,2,1,0:T(2,128)(2,1)S(1)} %copy-done.1, f32[256,128]{1,0:T(8,128)S(1)} %get-tuple-element.57._.refs_9_.refs_12_), custom_call_target="tpu_custom_call" | custom-call | flops 1 | bytes 1 | tf_op jit(solution)/shard_map/pool_split/pallas_call | solution.py:236
  34.0 2.3 %attention.1.refs_0_ = bf16[32,512]{1,0:T(8,128)(2,1)S(1)} custom-call(bf16[1,32,1536]{2,1,0:T(8,128)(2,1)S(1)} %get-tuple-element.51._.refs_0_, bf16[1,32,1536]{2,1,0:T(8,128)(2,1)S(1)} %collective-permute-done.1.refs_1_, bf16[1,32,1536]{2,1,0:T(8,128)(2,1)S(1)} %collective-permute-done.2.refs_2_, bf16[1,32,1536]{2,1,0:T(8,128)(2,1)S(1)} %collective-permute-done.3.refs_3_, ...), custom_call_target="tpu_custom_call" | custom-call | flops 1 | bytes 1 | tf_op jit(solution)/shard_map/attention/pallas_call | solution.py:341
  38.6 2.1 %collective-permute-start.4 = (bf16[32,512]{1,0:T(8,128)(2,1)S(1)}, bf16[32,512]{1,0:T(8,128)(2,1)S(1)}, u32[]{:S(2)}, u32[]{:S(2)}) collective-permute-start(bf16[32,512]{1,0:T(8,128)(2,1)S(1)} %attention.1.refs_0_), channel_id=1, source_target_pairs={{0,8},{4,12},{8,0},{12,4},{16,24},{20,28},{24,16},{28,20},{1,9},{5... | collective-permute-start | bytes 98312 | tf_op jit(solution)/shard_map/ppermute | solution.py:823
  49.4 2.4 %stage_gate.1 = (bf16[8,288,2,512]{3,2,1,0:T(2,128)(2,1)S(1)}, bf16[8,576,128]{2,1,0:T(8,128)(2,1)S(1)}) custom-call(bf16[8,288,2,1440]{3,2,1,0:T(2,128)(2,1)} %refs_2_.3, bf16[8,576,128]{2,1,0:T(8,128)(2,1)S(1)} %copy-done.2, bf16[288,256]{1,0:T(8,128)(2,1)S(1)} %out_projection.1._.refs_1_), custom_call_target="tpu_custom_call" | custom-call | flops 1 | bytes 1 | tf_op jit(solution)/shard_map/stage_gate/pallas_call | solution.py:532
  54.5 5.1 %gate_up_0.1 = (bf16[4,64,1152]{2,1,0:T(8,128)(2,1)S(1)}, bf16[4,64,1152]{2,1,0:T(8,128)(2,1)S(1)}, f32[288,256]{1,0:T(8,128)S(1)}, bf16[2,512,576]{2,1,0:T(8,128)(2,1)S(1)}) custom-call(s32[9]{0:T(128)S(1)} %get-tuple-element.52.offset_ref, s32[8]{0:T(128)S(1)} %pad_add_fusion.1.order_ref, f32[8,256]{1,0:T(8,128)S(1)} %get-tuple-element.53.refs_0_.refs_8_, ...), custom_call_target="tpu_custom_call" | custom-call | flops 1 | bytes 1 | tf_op jit(solution)/shard_map/gate_up_0/pallas_call | solution.py:905
  59.6 2.0 %collective-permute-done.11.recv_ref = bf16[4,64,1152]{2,1,0:T(8,128)(2,1)S(1)} collective-permute-done((bf16[4,64,1152]{2,1,0:T(8,128)(2,1)S(1)}, bf16[4,64,1152]{2,1,0:T(8,128)(2,1)S(1)}, u32[]{:S(2)}, u32[]{:S(2)}) %collective-permute-start.11) | collective-permute-done | bytes 589856 | tf_op jit(solution)/shard_map/ppermute | solution.py:820
  64.1 6.6 %gate_up_1.1 = (bf16[4,64,1280]{2,1,0:T(8,128)(2,1)S(1)}, bf16[4,64,1280]{2,1,0:T(8,128)(2,1)S(1)}) custom-call(s32[9]{0:T(128)S(1)} %get-tuple-element.52.offset_ref, s32[8]{0:T(128)S(1)} %pad_add_fusion.1.order_ref, bf16[2,64,1152]{2,1,0:T(8,128)(2,1)S(1)} %get-tuple-element.67.refs_0_.keep_ref, bf16[2,512,576]{2,1,0:T(8,128)(2,1)S(1)} %get-tuple-element.68.refs_1_, ...), custom_call_target="tpu_custom_call" | custom-call | flops 1 | bytes 1 | tf_op jit(solution)/shard_map/gate_up_1/pallas_call | solution.py:905
  71.9 2.1 %collective-permute-done.13.recv_ref = bf16[4,64,1280]{2,1,0:T(8,128)(2,1)S(1)} collective-permute-done((bf16[4,64,1280]{2,1,0:T(8,128)(2,1)S(1)}, bf16[4,64,1280]{2,1,0:T(8,128)(2,1)S(1)}, u32[]{:S(2)}, u32[]{:S(2)}) %collective-permute-start.13) | collective-permute-done | bytes 655392 | tf_op jit(solution)/shard_map/ppermute | solution.py:820
  76.8 4.9 %gate_up_2.1 = (bf16[4,64,512]{2,1,0:T(8,128)(2,1)S(1)}, bf16[4,64,512]{2,1,0:T(8,128)(2,1)S(1)}) custom-call(s32[9]{0:T(128)S(1)} %get-tuple-element.52.offset_ref, s32[8]{0:T(128)S(1)} %pad_add_fusion.1.order_ref, bf16[2,64,1280]{2,1,0:T(8,128)(2,1)S(1)} %get-tuple-element.74.refs_0_.keep_ref, bf16[2,512,576]{2,1,0:T(8,128)(2,1)S(1)} %get-tuple-element.68.refs_1_, ...), custom_call_target="tpu_custom_call" | custom-call | flops 1 | bytes 1 | tf_op jit(solution)/shard_map/gate_up_2/pallas_call | solution.py:905
  81.7 4.6 %collective-permute-done.15.refs_1_.refs_3_ = bf16[1,64,1152]{2,1,0:T(8,128)(2,1)S(1)} collective-permute-done((bf16[1,64,1152]{2,1,0:T(8,128)(2,1)S(1)}, bf16[1,64,1152]{2,1,0:T(8,128)(2,1)S(1)}, u32[]{:S(2)}, u32[]{:S(2)}) %collective-permute-start.15) | collective-permute-done | bytes 147488 | tf_op jit(solution)/shard_map/ppermute | solution.py:823
  87.6 2.6 %collective-permute-start.16 = (bf16[1,64,1280]{2,1,0:T(8,128)(2,1)S(1)}, bf16[1,64,1280]{2,1,0:T(8,128)(2,1)S(1)}, u32[]{:S(2)}, u32[]{:S(2)}) collective-permute-start(bf16[1,64,1280]{2,1,0:T(8,128)(2,1)S(1)} %get-tuple-element.81), channel_id=1, source_target_pairs={{0,16},{4,20},{8,24},{12,28},{16,0},{20,4},{24,8},{28,12},{1,17},{... | collective-permute-start | bytes 491528 | tf_op jit(solution)/shard_map/ppermute | solution.py:823
  93.8 8.3 %collective-permute-done.19.refs_5_.refs_2_ = bf16[64,640]{1,0:T(8,128)(2,1)S(1)} collective-permute-done((bf16[64,640]{1,0:T(8,128)(2,1)S(1)}, bf16[64,640]{1,0:T(8,128)(2,1)S(1)}, u32[]{:S(2)}, u32[]{:S(2)}) %collective-permute-start.19) | collective-permute-done | bytes 81952 | tf_op jit(solution)/shard_map/ppermute | solution.py:823
  102.5 2.6 %collective-permute-start.22 = (bf16[64,640]{1,0:T(8,128)(2,1)S(1)}, bf16[64,640]{1,0:T(8,128)(2,1)S(1)}, u32[]{:S(2)}, u32[]{:S(2)}) collective-permute-start(bf16[64,640]{1,0:T(8,128)(2,1)S(1)} %activation_1.1.outs_0_.refs_0_), channel_id=1, source_target_pairs={{0,16},{4,20},{8,24},{12,28},{16,0},{20,4},{24,8},{28,12},{1,17},{... | collective-permute-start | bytes 245768 | tf_op jit(solution)/shard_map/ppermute | solution.py:823
  105.2 2.4 %collective-permute-start.24 = (bf16[1,64,512]{2,1,0:T(8,128)(2,1)S(1)}, bf16[1,64,512]{2,1,0:T(8,128)(2,1)S(1)}, u32[]{:S(2)}, u32[]{:S(2)}) collective-permute-start(bf16[1,64,512]{2,1,0:T(8,128)(2,1)S(1)} %get-tuple-element.87), channel_id=1, source_target_pairs={{0,16},{4,20},{8,24},{12,28},{16,0},{20,4},{24,8},{28,12},{1,17},{... | collective-permute-start | bytes 196616 | tf_op jit(solution)/shard_map/ppermute | solution.py:823
  107.6 3.0 %stage_down.1.refs_8_.refs_5_.refs_10_ = bf16[8,288,1440]{2,1,0:T(8,128)(2,1)S(1)} custom-call(bf16[8,288,1440]{2,1,0:T(8,128)(2,1)} %w_ref.3, bf16[4,64,512]{2,1,0:T(8,128)(2,1)S(1)} %get-tuple-element.77.refs_2_.keep_ref._), custom_call_target="tpu_custom_call" | custom-call | flops 1 | bytes 1 | tf_op jit(solution)/shard_map/stage_down/pallas_call | solution.py:551
  112.8 2.0 %collective-permute-start.28 = (bf16[64,256]{1,0:T(8,128)(2,1)S(1)}, bf16[64,256]{1,0:T(8,128)(2,1)S(1)}, u32[]{:S(2)}, u32[]{:S(2)}) collective-permute-start(bf16[64,256]{1,0:T(8,128)(2,1)S(1)} %activation_2.1.refs_4_.refs_5_), channel_id=1, source_target_pairs={{0,24},{4,28},{8,16},{12,20},{16,8},{20,12},{24,0},{28,4},{1,25},{... | collective-permute-start | bytes 98312 | tf_op jit(solution)/shard_map/ppermute | solution.py:823
  117.2 2.1 %down_0.1.refs_8_.refs_11_ = f32[288,512]{1,0:T(8,128)S(1)} custom-call(s32[9]{0:T(128)S(1)} %get-tuple-element.52.offset_ref, s32[8]{0:T(128)S(1)} %pad_add_fusion.1.order_ref, bf16[64,640]{1,0:T(8,128)(2,1)S(1)} %get-tuple-element.78.outs_0_.refs_0_, bf16[64,640]{1,0:T(8,128)(2,1)S(1)} %collective-permute-done.18.refs_4_.refs_1_, ...), custom_call_target="tpu_custom_call" | custom-call | flops 1 | bytes 1 | tf_op jit(solution)/shard_map/down_0/pallas_call | solution.py:972
  122.0 3.6 %down_1.1 = bf16[256,288]{1,0:T(8,128)(2,1)S(1)} custom-call(s32[9]{0:T(128)S(1)} %get-tuple-element.52.offset_ref, s32[8]{0:T(128)S(1)} %pad_add_fusion.1.order_ref, bf16[64,640]{1,0:T(8,128)(2,1)S(1)} %activation_1.1.outs_0_.refs_0_, bf16[64,640]{1,0:T(8,128)(2,1)S(1)} %collective-permute-done.21.refs_4_.refs_1_, ...), custom_call_target="tpu_custom_call" | custom-call | flops 1 | bytes 1 | tf_op jit(solution)/shard_map/down_1/pallas_call | solution.py:972
  125.6 12.3 %all_to_all.10 = bf16[32,8,288]{2,1,0:T(8,128)(2,1)S(1)} all-to-all(bf16[32,8,288]{2,1,0:T(8,128)(2,1)S(1)} %bitcast.19), channel_id=1, replica_groups=mesh['dp'=8,'fsdp'=4] {'dp','fsdp'}, dimensions={0} | all-to-all | bytes 294912 | tf_op jit(solution)/shard_map/all_to_all | solution.py:1031
  (109 shorter events, 43.4 us)
Async XLA Ops:
  1.6 16.8 %all-to-all-start = ((bf16[32,8,384]{2,1,0:T(8,128)(2,1)}), bf16[32,8,384]{2,1,0:T(8,128)(2,1)S(1)}, u32[]{:S(2)}, u32[]{:S(2)}) async-start(bf16[32,8,384]{2,1,0:T(8,128)(2,1)} %bitcast.2), calls=%async_computation | async-start | bytes 393216 | tf_op jit(solution)/shard_map/all_to_all | solution.py:829
  21.6 12.4 %collective-permute-start.1 = (bf16[1,32,1536]{2,1,0:T(8,128)(2,1)S(1)}, bf16[1,32,1536]{2,1,0:T(8,128)(2,1)S(1)}, u32[]{:S(2)}, u32[]{:S(2)}) collective-permute-start(bf16[1,32,1536]{2,1,0:T(8,128)(2,1)S(1)} %get-tuple-element.54), channel_id=1, source_target_pairs={{0,8},{4,12},{8,0},{12,4},{16,24},{20,28},{24,16},{28,20},{1,9},{5... | collective-permute-start | bytes 294920 | tf_op jit(solution)/shard_map/ppermute | solution.py:823
  22.5 11.5 %collective-permute-start.2 = (bf16[1,32,1536]{2,1,0:T(8,128)(2,1)S(1)}, bf16[1,32,1536]{2,1,0:T(8,128)(2,1)S(1)}, u32[]{:S(2)}, u32[]{:S(2)}) collective-permute-start(bf16[1,32,1536]{2,1,0:T(8,128)(2,1)S(1)} %get-tuple-element.55), channel_id=1, source_target_pairs={{0,16},{4,20},{8,24},{12,28},{16,0},{20,4},{24,8},{28,12},{1,17},{... | collective-permute-start | bytes 294920 | tf_op jit(solution)/shard_map/ppermute | solution.py:823
  23.8 10.2 %collective-permute-start.3 = (bf16[1,32,1536]{2,1,0:T(8,128)(2,1)S(1)}, bf16[1,32,1536]{2,1,0:T(8,128)(2,1)S(1)}, u32[]{:S(2)}, u32[]{:S(2)}) collective-permute-start(bf16[1,32,1536]{2,1,0:T(8,128)(2,1)S(1)} %get-tuple-element.56), channel_id=1, source_target_pairs={{0,24},{4,28},{8,16},{12,20},{16,8},{20,12},{24,0},{28,4},{1,25},{... | collective-permute-start | bytes 294920 | tf_op jit(solution)/shard_map/ppermute | solution.py:823
  36.3 6.1 %collective-permute-start.6 = (bf16[32,512]{1,0:T(8,128)(2,1)S(1)}, bf16[32,512]{1,0:T(8,128)(2,1)S(1)}, u32[]{:S(2)}, u32[]{:S(2)}) collective-permute-start(bf16[32,512]{1,0:T(8,128)(2,1)S(1)} %attention.1.refs_0_), channel_id=1, source_target_pairs={{0,24},{4,28},{8,16},{12,20},{16,8},{20,12},{24,0},{28,4},{1,25},{... | collective-permute-start | bytes 98312 | tf_op jit(solution)/shard_map/ppermute | solution.py:823
  37.9 5.1 %collective-permute-start.5 = (bf16[32,512]{1,0:T(8,128)(2,1)S(1)}, bf16[32,512]{1,0:T(8,128)(2,1)S(1)}, u32[]{:S(2)}, u32[]{:S(2)}) collective-permute-start(bf16[32,512]{1,0:T(8,128)(2,1)S(1)} %attention.1.refs_0_), channel_id=1, source_target_pairs={{0,16},{4,20},{8,24},{12,28},{16,0},{20,4},{24,8},{28,12},{1,17},{... | collective-permute-start | bytes 98312 | tf_op jit(solution)/shard_map/ppermute | solution.py:823
  44.8 7.7 %collective-permute-start.10 = (bf16[288,256]{1,0:T(8,128)(2,1)S(1)}, bf16[288,256]{1,0:T(8,128)(2,1)S(1)}, u32[]{:S(2)}, u32[]{:S(2)}) collective-permute-start(bf16[288,256]{1,0:T(8,128)(2,1)S(1)} %out_projection.1._.refs_1_), channel_id=1, source_target_pairs={{0,3},{1,2},{2,1},{3,0},{4,7},{5,6},{6,5},{7,4},{8,11},{9,10},{10,... | collective-permute-start | bytes 442376 | tf_op jit(solution)/shard_map/ppermute | solution.py:826
  45.7 8.8 %collective-permute-start.9 = (bf16[288,256]{1,0:T(8,128)(2,1)S(1)}, bf16[288,256]{1,0:T(8,128)(2,1)S(1)}, u32[]{:S(2)}, u32[]{:S(2)}) collective-permute-start(bf16[288,256]{1,0:T(8,128)(2,1)S(1)} %out_projection.1._.refs_1_), channel_id=1, source_target_pairs={{0,2},{1,3},{2,0},{3,1},{4,6},{5,7},{6,4},{7,5},{8,10},{9,11},{10,... | collective-permute-start | bytes 442376 | tf_op jit(solution)/shard_map/ppermute | solution.py:826
  46.5 8.0 %collective-permute-start.8 = (bf16[288,256]{1,0:T(8,128)(2,1)S(1)}, bf16[288,256]{1,0:T(8,128)(2,1)S(1)}, u32[]{:S(2)}, u32[]{:S(2)}) collective-permute-start(bf16[288,256]{1,0:T(8,128)(2,1)S(1)} %out_projection.1._.refs_1_), channel_id=1, source_target_pairs={{0,1},{1,0},{2,3},{3,2},{4,5},{5,4},{6,7},{7,6},{8,9},{9,8},{10,11... | collective-permute-start | bytes 442376 | tf_op jit(solution)/shard_map/ppermute | solution.py:826
  62.3 9.1 %collective-permute-start.12 = (bf16[2,64,1152]{2,1,0:T(8,128)(2,1)S(1)}, bf16[2,64,1152]{2,1,0:T(8,128)(2,1)S(1)}, u32[]{:S(2)}, u32[]{:S(2)}) collective-permute-start(bf16[2,64,1152]{2,1,0:T(8,128)(2,1)S(1)} %get-tuple-element.70), channel_id=1, source_target_pairs={{0,8},{4,12},{8,0},{12,4},{16,24},{20,28},{24,16},{28,20},{1,9},{5... | collective-permute-start | bytes 884744 | tf_op jit(solution)/shard_map/ppermute | solution.py:823
  74.2 13.0 %collective-permute-start.14 = (bf16[2,64,1280]{2,1,0:T(8,128)(2,1)S(1)}, bf16[2,64,1280]{2,1,0:T(8,128)(2,1)S(1)}, u32[]{:S(2)}, u32[]{:S(2)}) collective-permute-start(bf16[2,64,1280]{2,1,0:T(8,128)(2,1)S(1)} %get-tuple-element.75), channel_id=1, source_target_pairs={{0,8},{4,12},{8,0},{12,4},{16,24},{20,28},{24,16},{28,20},{1,9},{5... | collective-permute-start | bytes 983048 | tf_op jit(solution)/shard_map/ppermute | solution.py:823
  75.9 10.4 %collective-permute-start.15 = (bf16[1,64,1152]{2,1,0:T(8,128)(2,1)S(1)}, bf16[1,64,1152]{2,1,0:T(8,128)(2,1)S(1)}, u32[]{:S(2)}, u32[]{:S(2)}) collective-permute-start(bf16[1,64,1152]{2,1,0:T(8,128)(2,1)S(1)} %get-tuple-element.76), channel_id=1, source_target_pairs={{0,16},{4,20},{8,24},{12,28},{16,0},{20,4},{24,8},{28,12},{1,17},{... | collective-permute-start | bytes 442376 | tf_op jit(solution)/shard_map/ppermute | solution.py:823
  87.6 14.6 %collective-permute-start.16 = (bf16[1,64,1280]{2,1,0:T(8,128)(2,1)S(1)}, bf16[1,64,1280]{2,1,0:T(8,128)(2,1)S(1)}, u32[]{:S(2)}, u32[]{:S(2)}) collective-permute-start(bf16[1,64,1280]{2,1,0:T(8,128)(2,1)S(1)} %get-tuple-element.81), channel_id=1, source_target_pairs={{0,16},{4,20},{8,24},{12,28},{16,0},{20,4},{24,8},{28,12},{1,17},{... | collective-permute-start | bytes 491528 | tf_op jit(solution)/shard_map/ppermute | solution.py:823
  90.3 11.9 %collective-permute-start.20 = (bf16[2,64,512]{2,1,0:T(8,128)(2,1)S(1)}, bf16[2,64,512]{2,1,0:T(8,128)(2,1)S(1)}, u32[]{:S(2)}, u32[]{:S(2)}) collective-permute-start(bf16[2,64,512]{2,1,0:T(8,128)(2,1)S(1)} %get-tuple-element.85), channel_id=1, source_target_pairs={{0,8},{4,12},{8,0},{12,4},{16,24},{20,28},{24,16},{28,20},{1,9},{5... | collective-permute-start | bytes 393224 | tf_op jit(solution)/shard_map/ppermute | solution.py:823
  90.8 11.3 %collective-permute-start.19 = (bf16[64,640]{1,0:T(8,128)(2,1)S(1)}, bf16[64,640]{1,0:T(8,128)(2,1)S(1)}, u32[]{:S(2)}, u32[]{:S(2)}) collective-permute-start(bf16[64,640]{1,0:T(8,128)(2,1)S(1)} %get-tuple-element.78.outs_0_.refs_0_), channel_id=1, source_target_pairs={{0,16},{4,20},{8,24},{12,28},{16,0},{20,4},{24,8},{28,12},{1,17},{... | collective-permute-start | bytes 245768 | tf_op jit(solution)/shard_map/ppermute | solution.py:823
  92.3 9.8 %collective-permute-start.18 = (bf16[64,640]{1,0:T(8,128)(2,1)S(1)}, bf16[64,640]{1,0:T(8,128)(2,1)S(1)}, u32[]{:S(2)}, u32[]{:S(2)}) collective-permute-start(bf16[64,640]{1,0:T(8,128)(2,1)S(1)} %get-tuple-element.78.outs_0_.refs_0_), channel_id=1, source_target_pairs={{0,8},{4,12},{8,0},{12,4},{16,24},{20,28},{24,16},{28,20},{1,9},{5... | collective-permute-start | bytes 245768 | tf_op jit(solution)/shard_map/ppermute | solution.py:823
  102.1 8.5 %collective-permute-start.25 = (bf16[64,640]{1,0:T(8,128)(2,1)S(1)}, bf16[64,640]{1,0:T(8,128)(2,1)S(1)}, u32[]{:S(2)}, u32[]{:S(2)}) collective-permute-start(bf16[64,640]{1,0:T(8,128)(2,1)S(1)} %collective-permute-done.19.refs_5_.refs_2_), channel_id=1, source_target_pairs={{0,8},{4,12},{8,0},{12,4},{16,24},{20,28},{24,16},{28,20},{1,9},{5... | collective-permute-start | bytes 245768 | tf_op jit(solution)/shard_map/ppermute | solution.py:823
  102.5 9.8 %collective-permute-start.22 = (bf16[64,640]{1,0:T(8,128)(2,1)S(1)}, bf16[64,640]{1,0:T(8,128)(2,1)S(1)}, u32[]{:S(2)}, u32[]{:S(2)}) collective-permute-start(bf16[64,640]{1,0:T(8,128)(2,1)S(1)} %activation_1.1.outs_0_.refs_0_), channel_id=1, source_target_pairs={{0,16},{4,20},{8,24},{12,28},{16,0},{20,4},{24,8},{28,12},{1,17},{... | collective-permute-start | bytes 245768 | tf_op jit(solution)/shard_map/ppermute | solution.py:823
  105.1 7.2 %collective-permute-start.21 = (bf16[64,640]{1,0:T(8,128)(2,1)S(1)}, bf16[64,640]{1,0:T(8,128)(2,1)S(1)}, u32[]{:S(2)}, u32[]{:S(2)}) collective-permute-start(bf16[64,640]{1,0:T(8,128)(2,1)S(1)} %activation_1.1.outs_0_.refs_0_), channel_id=1, source_target_pairs={{0,8},{4,12},{8,0},{12,4},{16,24},{20,28},{24,16},{28,20},{1,9},{5... | collective-permute-start | bytes 245768 | tf_op jit(solution)/shard_map/ppermute | solution.py:823
  105.2 7.1 %collective-permute-start.24 = (bf16[1,64,512]{2,1,0:T(8,128)(2,1)S(1)}, bf16[1,64,512]{2,1,0:T(8,128)(2,1)S(1)}, u32[]{:S(2)}, u32[]{:S(2)}) collective-permute-start(bf16[1,64,512]{2,1,0:T(8,128)(2,1)S(1)} %get-tuple-element.87), channel_id=1, source_target_pairs={{0,16},{4,20},{8,24},{12,28},{16,0},{20,4},{24,8},{28,12},{1,17},{... | collective-permute-start | bytes 196616 | tf_op jit(solution)/shard_map/ppermute | solution.py:823
  112.5 4.7 %collective-permute-start.29 = (bf16[4,64,640]{2,1,0:T(8,128)(2,1)S(1)}, bf16[4,64,640]{2,1,0:T(8,128)(2,1)S(1)}, u32[]{:S(2)}, u32[]{:S(2)}) collective-permute-start(bf16[4,64,640]{2,1,0:T(8,128)(2,1)S(1)} %stack_parts.2), channel_id=1, source_target_pairs={{0,4},{4,0},{8,12},{12,8},{16,20},{20,16},{24,28},{28,24},{1,5},{5... | collective-permute-start | bytes 983048 | tf_op jit(solution)/shard_map/ppermute | solution.py:820
  112.6 7.5 %collective-permute-start.23 = (bf16[64,640]{1,0:T(8,128)(2,1)S(1)}, bf16[64,640]{1,0:T(8,128)(2,1)S(1)}, u32[]{:S(2)}, u32[]{:S(2)}) collective-permute-start(bf16[64,640]{1,0:T(8,128)(2,1)S(1)} %collective-permute-done.22.refs_5_.refs_2_), channel_id=1, source_target_pairs={{0,8},{4,12},{8,0},{12,4},{16,24},{20,28},{24,16},{28,20},{1,9},{5... | collective-permute-start | bytes 245768 | tf_op jit(solution)/shard_map/ppermute | solution.py:823
  112.8 6.5 %collective-permute-start.28 = (bf16[64,256]{1,0:T(8,128)(2,1)S(1)}, bf16[64,256]{1,0:T(8,128)(2,1)S(1)}, u32[]{:S(2)}, u32[]{:S(2)}) collective-permute-start(bf16[64,256]{1,0:T(8,128)(2,1)S(1)} %activation_2.1.refs_4_.refs_5_), channel_id=1, source_target_pairs={{0,24},{4,28},{8,16},{12,20},{16,8},{20,12},{24,0},{28,4},{1,25},{... | collective-permute-start | bytes 98312 | tf_op jit(solution)/shard_map/ppermute | solution.py:823
  114.8 4.9 %collective-permute-start.27 = (bf16[64,256]{1,0:T(8,128)(2,1)S(1)}, bf16[64,256]{1,0:T(8,128)(2,1)S(1)}, u32[]{:S(2)}, u32[]{:S(2)}) collective-permute-start(bf16[64,256]{1,0:T(8,128)(2,1)S(1)} %activation_2.1.refs_4_.refs_5_), channel_id=1, source_target_pairs={{0,16},{4,20},{8,24},{12,28},{16,0},{20,4},{24,8},{28,12},{1,17},{... | collective-permute-start | bytes 98312 | tf_op jit(solution)/shard_map/ppermute | solution.py:823
  (19 other events, 150.6 us)
